TPU v7x, 32 devices: a whole 2x2x4 slice. The times are simulated.
32 devices in a mesh: rep: 2 (over x), blk: 16 (over z, y, core).
Axes of the slice: x: 2, y: 2, z: 4, core: 2. Of those that a mesh axis runs over, the one named last changes fastest.
Arguments:
- features: bfloat16 [4096, 256], P(('rep', 'blk')), may hold values from -6 to 6
- weight: bfloat16 [256, 256], replicated, may hold values from -0.375 to 0.375
- cotangent: bfloat16 [4096, 256], P(('rep', 'blk')), may hold values from -6 to 6
- tile_row: int32 [2, 16, 8, 4], P('rep', 'blk'), may hold values from 0 to 31, as said below
- tile_col: int32 [2, 16, 8, 4], P('rep', 'blk'), may hold values from 0 to 31, as said below
- tile_count: int32 [2, 16, 8], P('rep', 'blk'), may hold values from 1 to 4, as said below
- tile_vals: bfloat16 [2, 16, 8, 4, 128, 128], P('rep', 'blk'), may hold values from 0 to 0.015625
Outputs:
- activations: bfloat16 [4096, 256], P(('rep', 'blk'))
- weight_grad: float32 [256, 256], replicated
- feature_grad: bfloat16 [4096, 256], P(('rep', 'blk'))
Inputs may be any that keep to these rules, and one draw needn't show every extreme that they name: In slot (r, p, t, k) the row block lies in row panel p: p * 2 <= tile_row < (p + 1) * 2. The live slots of one (r, p, t) hold distinct (tile_row, tile_col) pairs. In slot (r, p, t, k) the column block lies in column panel q = (p - 8 * r - t) mod 16: q * 2 <= tile_col < (q + 1) * 2. Slots with k >= tile_count[r, p, t] are unused. `tile_count`: the value 4 occurs in every draw.
All inputs are finite; a program needn't handle non-finite values.
Results may differ from a plain program's by a relative error of at most 0.018.
Values may be sent and summed in bfloat16 or wider, within the bound.
No kernel may reach another device: no remote copies, remote signals or barrier semaphores. Data moves between devices by JAX's collectives and lax.ppermute only.
A program may use at most 64 MiB of HBM per device.

v0:
```python
import math

import jax
import jax.numpy as jnp
from jax import lax
from jax.sharding import PartitionSpec as P


def passed_along(array, axis, by):
    peers = lax.axis_size(axis)
    return lax.ppermute(array, axis, [(i, (i + by) % peers) for i in range(peers)])


def silu_slope(values):
    sigmoid_part = jax.nn.sigmoid(values)
    return sigmoid_part * (1.0 + values * (1.0 - sigmoid_part))


def block_select(block_ids, live_slots, blocks):
    levels = lax.broadcasted_iota(jnp.int32, (block_ids.shape[0], blocks), 1)
    return ((block_ids[:, None] == levels) & live_slots[:, None]).astype(jnp.float32)


def forward_terms(panel, tiles, rows_local, cols_local, live_slots):
    picked = jnp.take(panel, cols_local, axis=0)
    product = jnp.einsum("kij,kjf->kif", tiles, picked, preferred_element_type=jnp.float32)
    select_rows = block_select(rows_local, live_slots, panel.shape[0])
    return jnp.einsum("kc,kif->cif", select_rows, product, precision=lax.Precision.HIGHEST)


def backward_terms(panel, tiles, rows_local, cols_local, live_slots):
    picked = jnp.take(panel, rows_local, axis=0)
    product = jnp.einsum("kji,kjf->kif", tiles, picked, preferred_element_type=jnp.float32)
    select_cols = block_select(cols_local, live_slots, panel.shape[0])
    return jnp.einsum("kc,kif->cif", select_cols, product, precision=lax.Precision.HIGHEST)


def on_device(features, weight, cotangent, tile_row, tile_col, tile_count, tile_vals):
    slab_rows, width = features.shape
    groups = lax.axis_size("rep")
    panels = lax.axis_size("blk")
    steps = panels // groups
    tile_size = tile_vals.shape[-1]
    blocks = groups * slab_rows // tile_size
    slots = tile_vals.shape[3]
    member = lax.axis_index("rep")
    rows_local = tile_row[0, 0] % blocks
    cols_local = tile_col[0, 0] % blocks
    live_slots = lax.broadcasted_iota(jnp.int32, (steps, slots), 1) < tile_count[0, 0][:, None]
    tiles = tile_vals[0, 0]
    total_nodes = slab_rows * groups * panels

    def forward_at(panel, index):
        return forward_terms(
            panel, tiles[index], rows_local[index], cols_local[index], live_slots[index]
        )

    def backward_at(panel, index):
        return backward_terms(
            panel, tiles[index], rows_local[index], cols_local[index], live_slots[index]
        )

    panel = lax.all_gather(features, "rep", axis=0, tiled=True)
    for level in range(groups.bit_length() - 1):
        moved = passed_along(panel, "blk", steps << level)
        panel = jnp.where(member >> level & 1 == 1, moved, panel)
    panel = panel.reshape(blocks, tile_size, width)
    partial_value = forward_at(panel, 0)
    for index in range(1, steps):
        panel = passed_along(panel, "blk", 1)
        partial_value = partial_value + forward_at(panel, index)
    row_part = lax.psum_scatter(
        partial_value.reshape(-1, width), "rep", scatter_dimension=0, tiled=True
    )
    aggregated = row_part.astype(jnp.bfloat16)
    preact = jnp.dot(aggregated, weight, preferred_element_type=jnp.float32)
    activations = jax.nn.silu(preact).astype(jnp.bfloat16)
    slope_grad = (cotangent.astype(jnp.float32) * silu_slope(preact)).astype(jnp.bfloat16)
    local_grad = jnp.dot(aggregated.T, slope_grad, preferred_element_type=jnp.float32)
    weight_grad = lax.psum(local_grad, ("rep", "blk")) * (1.0 / math.sqrt(total_nodes))
    back_rows = jnp.dot(slope_grad, weight.T, preferred_element_type=jnp.float32).astype(
        jnp.bfloat16
    )
    grad_panel = lax.all_gather(back_rows, "rep", axis=0, tiled=True).reshape(
        blocks, tile_size, width
    )
    carried = backward_at(grad_panel, steps - 1)
    for index in range(steps - 2, -1, -1):
        carried = passed_along(carried, "blk", -1) + backward_at(grad_panel, index)
    for level in range(groups.bit_length() - 1):
        moved = passed_along(carried.astype(jnp.bfloat16), "blk", -(steps << level)).astype(
            carried.dtype
        )
        carried = jnp.where(member >> level & 1 == 1, moved, carried)
    column_part = lax.psum_scatter(
        carried.reshape(-1, width).astype(jnp.bfloat16), "rep", scatter_dimension=0, tiled=True
    )
    return (activations, weight_grad, column_part)


def solution(mesh):
    return jax.shard_map(
        on_device,
        mesh=mesh,
        in_specs=(
            P(("rep", "blk"), None),
            P(),
            P(("rep", "blk"), None),
            P("rep", "blk", None, None),
            P("rep", "blk", None, None),
            P("rep", "blk", None),
            P("rep", "blk", None, None, None, None),
        ),
        out_specs=(P(("rep", "blk"), None), P(), P(("rep", "blk"), None)),
        check_vma=False,
    )
```

profile of v0, /device:TPU:0, one launch (start us, length us, event | category | flops | bytes accessed | tf_op | source)
XLA Modules:
  0.0 304.7 jit_solution(6873848316006853587)
XLA Ops:
  7.2 6.2 %all_gather.6 = bf16[256,256]{1,0:T(8,128)(2,1)S(1)} all-gather(bf16[128,256]{1,0:T(8,128)(2,1)} %param.9), channel_id=1, replica_groups=mesh['rep'=2,'blk'=16] {'rep'}, dimensions={0}, use_global_device_ids=true | all-gather | bytes 196608 | tf_op jit(solution)/shard_map/all_gather | solution.py:63
  13.5 3.1 %collective-permute-start = (bf16[256,256]{1,0:T(8,128)(2,1)S(1)}, bf16[256,256]{1,0:T(8,128)(2,1)S(1)}, u32[]{:S(2)}, u32[]{:S(2)}) collective-permute-start(bf16[256,256]{1,0:T(8,128)(2,1)S(1)} %all_gather.6), channel_id=1, source_target_pairs={{0,8},{1,9},{2,10},{3,11},{4,12},{5,13},{6,14},{7,15},{8,0},{9,1},... | collective-permute-start | bytes 393224 | tf_op jit(solution)/shard_map/ppermute | solution.py:11
  17.1 0.7 add_select_fusion.1
  18.1 0.7 iota_compare_fusion
  19.1 2.6 collective-permute-done
  21.8 0.6 gather_fusion
  23.0 0.6 fusion.22
  23.6 5.3 %collective-permute-done.1 = bf16[2,128,256]{2,1,0:T(8,128)(2,1)S(1)} collective-permute-done((bf16[2,128,256]{2,1,0:T(8,128)(2,1)S(1)}, bf16[2,128,256]{2,1,0:T(8,128)(2,1)S(1)}, u32[]{:S(2)}, u32[]{:S(2)}) %collective-permute-start.1) | collective-permute-done | bytes 131104 | tf_op jit(solution)/shard_map/ppermute | solution.py:11
  28.9 0.6 gather_fusion.1
  30.1 0.6 convolution_add_fusion.7
  30.8 6.4 %collective-permute-done.2 = bf16[2,128,256]{2,1,0:T(8,128)(2,1)S(1)} collective-permute-done((bf16[2,128,256]{2,1,0:T(8,128)(2,1)S(1)}, bf16[2,128,256]{2,1,0:T(8,128)(2,1)S(1)}, u32[]{:S(2)}, u32[]{:S(2)}) %collective-permute-start.2) | collective-permute-done | bytes 131104 | tf_op jit(solution)/shard_map/ppermute | solution.py:11
  37.2 0.6 gather_fusion.2
  38.4 0.6 convolution_add_fusion.6
  39.1 6.4 %collective-permute-done.3 = bf16[2,128,256]{2,1,0:T(8,128)(2,1)S(1)} collective-permute-done((bf16[2,128,256]{2,1,0:T(8,128)(2,1)S(1)}, bf16[2,128,256]{2,1,0:T(8,128)(2,1)S(1)}, u32[]{:S(2)}, u32[]{:S(2)}) %collective-permute-start.3) | collective-permute-done | bytes 131104 | tf_op jit(solution)/shard_map/ppermute | solution.py:11
  45.5 0.6 gather_fusion.3
  46.7 0.6 convolution_add_fusion.5
  47.4 6.4 %collective-permute-done.4 = bf16[2,128,256]{2,1,0:T(8,128)(2,1)S(1)} collective-permute-done((bf16[2,128,256]{2,1,0:T(8,128)(2,1)S(1)}, bf16[2,128,256]{2,1,0:T(8,128)(2,1)S(1)}, u32[]{:S(2)}, u32[]{:S(2)}) %collective-permute-start.4) | collective-permute-done | bytes 131104 | tf_op jit(solution)/shard_map/ppermute | solution.py:11
  53.8 0.6 gather_fusion.4
  55.0 0.6 convolution_add_fusion.4
  55.7 6.4 %collective-permute-done.5 = bf16[2,128,256]{2,1,0:T(8,128)(2,1)S(1)} collective-permute-done((bf16[2,128,256]{2,1,0:T(8,128)(2,1)S(1)}, bf16[2,128,256]{2,1,0:T(8,128)(2,1)S(1)}, u32[]{:S(2)}, u32[]{:S(2)}) %collective-permute-start.5) | collective-permute-done | bytes 131104 | tf_op jit(solution)/shard_map/ppermute | solution.py:11
  63.3 0.6 convolution_add_fusion.3
  64.0 6.4 %collective-permute-done.6 = bf16[2,128,256]{2,1,0:T(8,128)(2,1)S(1)} collective-permute-done((bf16[2,128,256]{2,1,0:T(8,128)(2,1)S(1)}, bf16[2,128,256]{2,1,0:T(8,128)(2,1)S(1)}, u32[]{:S(2)}, u32[]{:S(2)}) %collective-permute-start.6) | collective-permute-done | bytes 131104 | tf_op jit(solution)/shard_map/ppermute | solution.py:11
  70.4 0.6 gather_fusion.6
  71.7 0.6 convolution_add_fusion.2
  72.3 6.4 %collective-permute-done.7 = bf16[2,128,256]{2,1,0:T(8,128)(2,1)S(1)} collective-permute-done((bf16[2,128,256]{2,1,0:T(8,128)(2,1)S(1)}, bf16[2,128,256]{2,1,0:T(8,128)(2,1)S(1)}, u32[]{:S(2)}, u32[]{:S(2)}) %collective-permute-start.7) | collective-permute-done | bytes 131104 | tf_op jit(solution)/shard_map/ppermute | solution.py:11
  79.9 0.6 convolution_add_fusion.1
  80.5 0.7 copy.10
  81.4 9.0 %reduce-scatter.3.cloned.1.call-done = f32[128,256]{1,0:T(8,128)} async-done(((f32[256,256]{1,0:T(8,128)}), f32[128,256]{1,0:T(8,128)}) %reduce-scatter.3.cloned.1.call-update) | async-done | bytes 131088 | tf_op jit(solution)/shard_map/reduce_scatter | solution.py:72
  90.4 1.7 multiply_convert_fusion.1
  92.8 4.9 %all_gather.7 = bf16[256,256]{1,0:T(8,128)(2,1)S(1)} all-gather(bf16[128,256]{1,0:T(8,128)(2,1)S(1)} %convolution_convert_fusion), channel_id=1, replica_groups=mesh['rep'=2,'blk'=16] {'rep'}, dimensions={0}, use_global_device_ids=true | all-gather | bytes 196608 | tf_op jit(solution)/shard_map/all_gather | solution.py:84
  98.9 0.6 fusion.13
  99.5 2.7 collective-permute-start.8
  103.4 0.6 gather_fusion.10
  104.0 2.1 collective-permute-done.8
  106.1 0.6 convolution_add_fusion
  106.8 4.7 %collective-permute-start.9 = (f32[2,128,256]{2,0,1:T(2,128)S(1)}, f32[2,128,256]{2,0,1:T(2,128)S(1)}, u32[]{:S(2)}, u32[]{:S(2)}) collective-permute-start(f32[2,128,256]{2,0,1:T(2,128)S(1)} %convolution_add_fusion), channel_id=1, source_target_pairs={{0,15},{1,0},{2,1},{3,2},{4,3},{5,4},{6,5},{7,6},{8,7},{9,8},{10,9... | collective-permute-start | bytes 786440 | tf_op jit(solution)/shard_map/ppermute | solution.py:11
  112.0 0.6 gather_fusion.11
  112.6 0.6 fusion.10
  113.2 2.1 collective-permute-done.9
  115.5 4.7 %collective-permute-start.10 = (f32[2,128,256]{2,0,1:T(2,128)S(1)}, f32[2,128,256]{2,0,1:T(2,128)S(1)}, u32[]{:S(2)}, u32[]{:S(2)}) collective-permute-start(f32[2,128,256]{2,0,1:T(2,128)S(1)} %add.81), channel_id=1, source_target_pairs={{0,15},{1,0},{2,1},{3,2},{4,3},{5,4},{6,5},{7,6},{8,7},{9,8},{10,9... | collective-permute-start | bytes 786440 | tf_op jit(solution)/shard_map/ppermute | solution.py:11
  120.7 0.6 gather_fusion.12
  121.3 0.6 fusion.8
  121.9 2.1 collective-permute-done.10
  124.2 4.7 %collective-permute-start.11 = (f32[2,128,256]{2,0,1:T(2,128)S(1)}, f32[2,128,256]{2,0,1:T(2,128)S(1)}, u32[]{:S(2)}, u32[]{:S(2)}) collective-permute-start(f32[2,128,256]{2,0,1:T(2,128)S(1)} %add.82), channel_id=1, source_target_pairs={{0,15},{1,0},{2,1},{3,2},{4,3},{5,4},{6,5},{7,6},{8,7},{9,8},{10,9... | collective-permute-start | bytes 786440 | tf_op jit(solution)/shard_map/ppermute | solution.py:11
  129.4 0.6 gather_fusion.13
  130.0 0.6 fusion.6
  130.6 2.1 collective-permute-done.11
  132.8 4.7 %collective-permute-start.12 = (f32[2,128,256]{2,0,1:T(2,128)S(1)}, f32[2,128,256]{2,0,1:T(2,128)S(1)}, u32[]{:S(2)}, u32[]{:S(2)}) collective-permute-start(f32[2,128,256]{2,0,1:T(2,128)S(1)} %add.83), channel_id=1, source_target_pairs={{0,15},{1,0},{2,1},{3,2},{4,3},{5,4},{6,5},{7,6},{8,7},{9,8},{10,9... | collective-permute-start | bytes 786440 | tf_op jit(solution)/shard_map/ppermute | solution.py:11
  138.1 0.6 gather_fusion.14
  138.7 0.6 fusion.4
  139.3 2.1 collective-permute-done.12
  141.5 4.7 %collective-permute-start.13 = (f32[2,128,256]{2,0,1:T(2,128)S(1)}, f32[2,128,256]{2,0,1:T(2,128)S(1)}, u32[]{:S(2)}, u32[]{:S(2)}) collective-permute-start(f32[2,128,256]{2,0,1:T(2,128)S(1)} %add.84), channel_id=1, source_target_pairs={{0,15},{1,0},{2,1},{3,2},{4,3},{5,4},{6,5},{7,6},{8,7},{9,8},{10,9... | collective-permute-start | bytes 786440 | tf_op jit(solution)/shard_map/ppermute | solution.py:11
  146.8 0.6 gather_fusion.15
  147.4 0.6 fusion.2
  148.0 2.1 collective-permute-done.13
  150.2 4.8 %collective-permute-start.14 = (f32[2,128,256]{2,0,1:T(2,128)S(1)}, f32[2,128,256]{2,0,1:T(2,128)S(1)}, u32[]{:S(2)}, u32[]{:S(2)}) collective-permute-start(f32[2,128,256]{2,0,1:T(2,128)S(1)} %add.85), channel_id=1, source_target_pairs={{0,15},{1,0},{2,1},{3,2},{4,3},{5,4},{6,5},{7,6},{8,7},{9,8},{10,9... | collective-permute-start | bytes 786440 | tf_op jit(solution)/shard_map/ppermute | solution.py:11
  155.6 0.6 fusion
  156.2 2.7 collective-permute-done.14
  159.1 0.9 fusion.120
  160.1 4.8 %collective-permute-done.15 = bf16[2,128,256]{2,0,1:T(2,128)(2,1)S(1)} collective-permute-done((bf16[2,128,256]{2,0,1:T(2,128)(2,1)S(1)}, bf16[2,128,256]{2,0,1:T(2,128)(2,1)S(1)}, u32[]{:S(2)}, u32[]{:S(2)}) %collective-permute-start.15) | collective-permute-done | bytes 131104 | tf_op jit(solution)/shard_map/ppermute | solution.py:11
  165.1 0.7 copy.11
  165.8 120.2 %all-reduce.2.cloned.1.call-done = f32[256,256]{1,0:T(8,128)} async-done(((f32[256,256]{1,0:T(8,128)}), f32[256,256]{1,0:T(8,128)}) %all-reduce.2.cloned.1.call-update) | async-done | bytes 262160 | tf_op jit(solution)/shard_map/psum | solution.py:80
  286.0 1.7 broadcast_multiply_fusion
  287.7 10.5 %reduce-scatter.5.cloned.1.call-done = bf16[128,256]{1,0:T(8,128)(2,1)} async-done(((bf16[256,256]{1,0:T(8,128)(2,1)}), bf16[128,256]{1,0:T(8,128)(2,1)}) %reduce-scatter.5.cloned.1.call-update) | async-done | bytes 65552 | tf_op jit(solution)/shard_map/reduce_scatter | solution.py:95
  (119 shorter events, 14.7 us)
Async XLA Ops:
  7.2 83.3 %copy-start = (bf16[256,256]{1,0:T(8,128)(2,1)S(1)}, bf16[256,256]{1,0:T(8,128)(2,1)}, u32[]{:S(2)}) copy-start(bf16[256,256]{1,0:T(8,128)(2,1)} %param.10) | copy-start | bytes 393220
  7.2 9.4 %copy-start.2 = (s32[1,1,8,4]{2,3,1,0:T(4,128)S(1)}, s32[1,1,8,4]{2,3,1,0:T(4,128)}, u32[]{:S(2)}) copy-start(s32[1,1,8,4]{2,3,1,0:T(4,128)} %param.13) | copy-start | bytes 388
  7.2 15.2 %copy-start.1 = (bf16[1,1,8,4,128,128]{5,4,3,2,1,0:T(8,128)(2,1)S(1)}, bf16[1,1,8,4,128,128]{5,4,3,2,1,0:T(8,128)(2,1)}, u32[]{:S(2)}) copy-start(bf16[1,1,8,4,128,128]{5,4,3,2,1,0:T(8,128)(2,1)} %param.15) | copy-start | bytes 3145732
  7.2 83.2 %reduce-scatter.3.cloned.1.call-start = ((), (), s32[]{:S(2)}) async-start(), calls=%async_computation.2 | async-start | bytes 393216 | tf_op jit(solution)/shard_map/reduce_scatter | solution.py:72
  13.5 8.2 %collective-permute-start = (bf16[256,256]{1,0:T(8,128)(2,1)S(1)}, bf16[256,256]{1,0:T(8,128)(2,1)S(1)}, u32[]{:S(2)}, u32[]{:S(2)}) collective-permute-start(bf16[256,256]{1,0:T(8,128)(2,1)S(1)} %all_gather.6), channel_id=1, source_target_pairs={{0,8},{1,9},{2,10},{3,11},{4,12},{5,13},{6,14},{7,15},{8,0},{9,1},... | collective-permute-start | bytes 393224 | tf_op jit(solution)/shard_map/ppermute | solution.py:11
  21.7 7.1 %collective-permute-start.1 = (bf16[2,128,256]{2,1,0:T(8,128)(2,1)S(1)}, bf16[2,128,256]{2,1,0:T(8,128)(2,1)S(1)}, u32[]{:S(2)}, u32[]{:S(2)}) collective-permute-start(bf16[2,128,256]{2,1,0:T(8,128)(2,1)S(1)} %bitcast.175), channel_id=1, source_target_pairs={{0,1},{1,2},{2,3},{3,4},{4,5},{5,6},{6,7},{7,8},{8,9},{9,10},{10,1... | collective-permute-start | bytes 393224 | tf_op jit(solution)/shard_map/ppermute | solution.py:11
  30.0 7.1 %collective-permute-start.2 = (bf16[2,128,256]{2,1,0:T(8,128)(2,1)S(1)}, bf16[2,128,256]{2,1,0:T(8,128)(2,1)S(1)}, u32[]{:S(2)}, u32[]{:S(2)}) collective-permute-start(bf16[2,128,256]{2,1,0:T(8,128)(2,1)S(1)} %collective-permute-done.1), channel_id=1, source_target_pairs={{0,1},{1,2},{2,3},{3,4},{4,5},{5,6},{6,7},{7,8},{8,9},{9,10},{10,1... | collective-permute-start | bytes 393224 | tf_op jit(solution)/shard_map/ppermute | solution.py:11
  38.4 7.1 %collective-permute-start.3 = (bf16[2,128,256]{2,1,0:T(8,128)(2,1)S(1)}, bf16[2,128,256]{2,1,0:T(8,128)(2,1)S(1)}, u32[]{:S(2)}, u32[]{:S(2)}) collective-permute-start(bf16[2,128,256]{2,1,0:T(8,128)(2,1)S(1)} %collective-permute-done.2), channel_id=1, source_target_pairs={{0,1},{1,2},{2,3},{3,4},{4,5},{5,6},{6,7},{7,8},{8,9},{9,10},{10,1... | collective-permute-start | bytes 393224 | tf_op jit(solution)/shard_map/ppermute | solution.py:11
  46.7 7.1 %collective-permute-start.4 = (bf16[2,128,256]{2,1,0:T(8,128)(2,1)S(1)}, bf16[2,128,256]{2,1,0:T(8,128)(2,1)S(1)}, u32[]{:S(2)}, u32[]{:S(2)}) collective-permute-start(bf16[2,128,256]{2,1,0:T(8,128)(2,1)S(1)} %collective-permute-done.3), channel_id=1, source_target_pairs={{0,1},{1,2},{2,3},{3,4},{4,5},{5,6},{6,7},{7,8},{8,9},{9,10},{10,1... | collective-permute-start | bytes 393224 | tf_op jit(solution)/shard_map/ppermute | solution.py:11
  55.0 7.1 %collective-permute-start.5 = (bf16[2,128,256]{2,1,0:T(8,128)(2,1)S(1)}, bf16[2,128,256]{2,1,0:T(8,128)(2,1)S(1)}, u32[]{:S(2)}, u32[]{:S(2)}) collective-permute-start(bf16[2,128,256]{2,1,0:T(8,128)(2,1)S(1)} %collective-permute-done.4), channel_id=1, source_target_pairs={{0,1},{1,2},{2,3},{3,4},{4,5},{5,6},{6,7},{7,8},{8,9},{9,10},{10,1... | collective-permute-start | bytes 393224 | tf_op jit(solution)/shard_map/ppermute | solution.py:11
  63.3 7.1 %collective-permute-start.6 = (bf16[2,128,256]{2,1,0:T(8,128)(2,1)S(1)}, bf16[2,128,256]{2,1,0:T(8,128)(2,1)S(1)}, u32[]{:S(2)}, u32[]{:S(2)}) collective-permute-start(bf16[2,128,256]{2,1,0:T(8,128)(2,1)S(1)} %collective-permute-done.5), channel_id=1, source_target_pairs={{0,1},{1,2},{2,3},{3,4},{4,5},{5,6},{6,7},{7,8},{8,9},{9,10},{10,1... | collective-permute-start | bytes 393224 | tf_op jit(solution)/shard_map/ppermute | solution.py:11
  71.6 7.1 %collective-permute-start.7 = (bf16[2,128,256]{2,1,0:T(8,128)(2,1)S(1)}, bf16[2,128,256]{2,1,0:T(8,128)(2,1)S(1)}, u32[]{:S(2)}, u32[]{:S(2)}) collective-permute-start(bf16[2,128,256]{2,1,0:T(8,128)(2,1)S(1)} %collective-permute-done.6), channel_id=1, source_target_pairs={{0,1},{1,2},{2,3},{3,4},{4,5},{5,6},{6,7},{7,8},{8,9},{9,10},{10,1... | collective-permute-start | bytes 393224 | tf_op jit(solution)/shard_map/ppermute | solution.py:11
  81.3 204.7 %all-reduce.2.cloned.1.call-start = ((), (), s32[]{:S(2)}) async-start(), calls=%async_computation.3 | async-start | bytes 524288 | tf_op jit(solution)/shard_map/psum | solution.py:80
  81.4 10.8 %copy-start.4 = (bf16[128,256]{1,0:T(8,128)(2,1)S(1)}, bf16[128,256]{1,0:T(8,128)(2,1)}, u32[]{:S(2)}) copy-start(bf16[128,256]{1,0:T(8,128)(2,1)} %param.11) | copy-start | bytes 196612
  92.2 0.7 copy-start.6
  99.5 6.6 %collective-permute-start.8 = (f32[2,128,256]{2,0,1:T(2,128)S(1)}, f32[2,128,256]{2,0,1:T(2,128)S(1)}, u32[]{:S(2)}, u32[]{:S(2)}) collective-permute-start(f32[2,128,256]{2,0,1:T(2,128)S(1)} %fusion.13), channel_id=1, source_target_pairs={{0,15},{1,0},{2,1},{3,2},{4,3},{5,4},{6,5},{7,6},{8,7},{9,8},{10,9... | collective-permute-start | bytes 786440 | tf_op jit(solution)/shard_map/ppermute | solution.py:11
  106.8 8.5 %collective-permute-start.9 = (f32[2,128,256]{2,0,1:T(2,128)S(1)}, f32[2,128,256]{2,0,1:T(2,128)S(1)}, u32[]{:S(2)}, u32[]{:S(2)}) collective-permute-start(f32[2,128,256]{2,0,1:T(2,128)S(1)} %convolution_add_fusion), channel_id=1, source_target_pairs={{0,15},{1,0},{2,1},{3,2},{4,3},{5,4},{6,5},{7,6},{8,7},{9,8},{10,9... | collective-permute-start | bytes 786440 | tf_op jit(solution)/shard_map/ppermute | solution.py:11
  115.5 8.5 %collective-permute-start.10 = (f32[2,128,256]{2,0,1:T(2,128)S(1)}, f32[2,128,256]{2,0,1:T(2,128)S(1)}, u32[]{:S(2)}, u32[]{:S(2)}) collective-permute-start(f32[2,128,256]{2,0,1:T(2,128)S(1)} %add.81), channel_id=1, source_target_pairs={{0,15},{1,0},{2,1},{3,2},{4,3},{5,4},{6,5},{7,6},{8,7},{9,8},{10,9... | collective-permute-start | bytes 786440 | tf_op jit(solution)/shard_map/ppermute | solution.py:11
  124.2 8.5 %collective-permute-start.11 = (f32[2,128,256]{2,0,1:T(2,128)S(1)}, f32[2,128,256]{2,0,1:T(2,128)S(1)}, u32[]{:S(2)}, u32[]{:S(2)}) collective-permute-start(f32[2,128,256]{2,0,1:T(2,128)S(1)} %add.82), channel_id=1, source_target_pairs={{0,15},{1,0},{2,1},{3,2},{4,3},{5,4},{6,5},{7,6},{8,7},{9,8},{10,9... | collective-permute-start | bytes 786440 | tf_op jit(solution)/shard_map/ppermute | solution.py:11
  132.8 8.5 %collective-permute-start.12 = (f32[2,128,256]{2,0,1:T(2,128)S(1)}, f32[2,128,256]{2,0,1:T(2,128)S(1)}, u32[]{:S(2)}, u32[]{:S(2)}) collective-permute-start(f32[2,128,256]{2,0,1:T(2,128)S(1)} %add.83), channel_id=1, source_target_pairs={{0,15},{1,0},{2,1},{3,2},{4,3},{5,4},{6,5},{7,6},{8,7},{9,8},{10,9... | collective-permute-start | bytes 786440 | tf_op jit(solution)/shard_map/ppermute | solution.py:11
  141.5 8.5 %collective-permute-start.13 = (f32[2,128,256]{2,0,1:T(2,128)S(1)}, f32[2,128,256]{2,0,1:T(2,128)S(1)}, u32[]{:S(2)}, u32[]{:S(2)}) collective-permute-start(f32[2,128,256]{2,0,1:T(2,128)S(1)} %add.84), channel_id=1, source_target_pairs={{0,15},{1,0},{2,1},{3,2},{4,3},{5,4},{6,5},{7,6},{8,7},{9,8},{10,9... | collective-permute-start | bytes 786440 | tf_op jit(solution)/shard_map/ppermute | solution.py:11
  150.2 8.6 %collective-permute-start.14 = (f32[2,128,256]{2,0,1:T(2,128)S(1)}, f32[2,128,256]{2,0,1:T(2,128)S(1)}, u32[]{:S(2)}, u32[]{:S(2)}) collective-permute-start(f32[2,128,256]{2,0,1:T(2,128)S(1)} %add.85), channel_id=1, source_target_pairs={{0,15},{1,0},{2,1},{3,2},{4,3},{5,4},{6,5},{7,6},{8,7},{9,8},{10,9... | collective-permute-start | bytes 786440 | tf_op jit(solution)/shard_map/ppermute | solution.py:11
  156.2 2.9 copy-start.3
  156.2 2.9 copy-start.5
  156.2 2.9 copy-start.7
  159.0 5.9 %collective-permute-start.15 = (bf16[2,128,256]{2,0,1:T(2,128)(2,1)S(1)}, bf16[2,128,256]{2,0,1:T(2,128)(2,1)S(1)}, u32[]{:S(2)}, u32[]{:S(2)}) collective-permute-start(bf16[2,128,256]{2,0,1:T(2,128)(2,1)S(1)} %add.86), channel_id=1, source_target_pairs={{0,8},{1,9},{2,10},{3,11},{4,12},{5,13},{6,14},{7,15},{8,0},{9,1},... | collective-permute-start | bytes 393224 | tf_op jit(solution)/shard_map/ppermute | solution.py:11
  160.1 138.1 %reduce-scatter.5.cloned.1.call-start = ((), (), s32[]{:S(2)}) async-start(), calls=%async_computation.4 | async-start | bytes 196608 | tf_op jit(solution)/shard_map/reduce_scatter | solution.py:95
Sparse Core Ops, SparseCore 0:
  81.4 8.9 reduce-scatter.2
  160.2 125.7 all-reduce.1
  288.9 9.2 reduce-scatter.4
where the time goes:
time: 305 us
  waiting for transfers between devices  206 us (68%)
  starting transfers between devices  34.5 us (11%)
  matrix products  18.3 us (6%)
  local copies, waits for them, and re-layouts  15.2 us (5%)
  between operations  14.7 us (5%)
  blocking collectives  11.2 us (4%)
  other arithmetic  4.32 us (1%)
    psum x1, waiting for transfers between devices, on_device(): lax.psum(local_grad, ('rep', 'blk')) * (1.0 / math.sqrt(total_nodes))  120 us
    ppermute x16, waiting for transfers between devices, passed_along(): lax.ppermute(array, axis, [(i, (i + by) % peers) for i in range(peers)])  66.7 us
    ppermute x16, starting transfers between devices, passed_along(): lax.ppermute(array, axis, [(i, (i + by) % peers) for i in range(peers)])  34.3 us
    reduce_scatter x1, waiting for transfers between devices, on_device(): lax.psum_scatter(carried.reshape(-1, width).astype(jnp.bfloat16), 'rep',...  10.5 us
    reduce_scatter x1, waiting for transfers between devices, on_device(): lax.psum_scatter(partial_value.reshape(-1, width), 'rep', scatter_dimensi...  9.01 us
    all_gather x1, blocking collectives, on_device(): panel = lax.all_gather(features, 'rep', axis=0, tiled=True)  6.24 us
  transfers between devices with their start and end apart: 19, of which 19 were waited for; matrix products, arithmetic and copies ran while one was open for 7% of the time, Pallas kernels for 0%

commit v1 on v0

v1 whole, which is shorter than its diff:
```python
import functools
import math

import jax
import jax.numpy as jnp
from jax import lax
from jax.experimental import pallas as pl
from jax.experimental.pallas import tpu as pltpu
from jax.sharding import PartitionSpec as P

BOTH = ("rep", "blk")


def xor_pairs(count, bit):
    return [(i, i ^ bit) for i in range(count)]


def tree_sum(terms):
    terms = list(terms)
    while len(terms) > 1:
        terms = [terms[i] + terms[i + 1] for i in range(0, len(terms), 2)]
    return terms[0]


def limit_for(*arrays):
    total = sum(math.prod(a.shape) * a.dtype.itemsize for a in arrays)
    return int(2 * total + (8 << 20))


def like(shape, dtype):
    return jax.ShapeDtypeStruct(shape, dtype)


def panel_slots(groups, panels, steps):
    def device(member, panel):
        return member * panels + panel % panels

    def moves(members, shift_of, odd_only=False):
        return [
            (device(m, p), device(m, p + shift_of(m)))
            for m in members
            for p in range(panels)
            if not (odd_only and p % 2 == 0)
        ]

    first = moves(range(1, groups), lambda m: steps * m)
    last = moves(range(groups - 1), lambda m: steps * (m + 1), odd_only=True)
    slots = []
    if groups == 2:
        slots.append((first + last, lambda m: steps, lambda m: m >= 0))
    else:
        slots.append((first, lambda m: steps * m, lambda m: m >= 1))
        slots.append((last, lambda m: steps * (m + 1), lambda m: m <= groups - 2))
    for k in range(1, steps // 2):
        shift = functools.partial(lambda k, m: steps * m + 2 * k, k)
        slots.append((moves(range(groups), shift), shift, lambda m: m >= 0))
    return slots


def place_kernel(step_of, rows, cols, counts, own_tiles, pass_tiles, own_ref, pass_ref):
    slot = pl.program_id(0)
    slots = pl.num_programs(0)
    cap, size = own_tiles.shape[1], own_tiles.shape[2]
    for which, tiles, out in ((0, own_tiles, own_ref), (1, pass_tiles, pass_ref)):
        step = step_of[which * slots + slot]
        there = jnp.maximum(step, 0)
        out[...] = jnp.zeros_like(out)
        for k in range(cap):

            @pl.when((step >= 0) & (k < counts[there]))
            def _():
                row = pl.multiple_of(rows[there * cap + k] * size, size)
                col = pl.multiple_of(cols[there * cap + k] * size, size)
                out[0, pl.ds(row, size), pl.ds(col, size)] = tiles[0, k]


def place_tiles(step_of, rows, cols, counts, tiles, span):
    slots = step_of.shape[0] // 2
    steps, cap, size, _ = tiles.shape
    block = (1, cap, size, size)

    def at(which):
        return pl.BlockSpec(
            block, lambda s, so, *_: (jnp.maximum(so[which * slots + s], 0), 0, 0, 0)
        )

    out = like((slots, span, span), tiles.dtype)
    return pl.pallas_call(
        place_kernel,
        grid_spec=pltpu.PrefetchScalarGridSpec(
            num_scalar_prefetch=4,
            grid=(slots,),
            in_specs=[at(0), at(1)],
            out_specs=[pl.BlockSpec((1, span, span), lambda s, *_: (s, 0, 0))] * 2,
        ),
        out_shape=[out, out],
        cost_estimate=pl.CostEstimate(
            flops=0, bytes_accessed=4 * slots * span * span * 2, transcendentals=0
        ),
        name="place_tiles",
    )(step_of, rows.reshape(-1), cols.reshape(-1), counts, tiles, tiles)


def gather_kernel(slots, groups, own_a, sib_a, *refs):
    slabs, (own_out, sib_out) = refs[:-2], refs[-2:]
    own = sib = None
    for s in range(slots):
        panel = jnp.concatenate([slabs[s * groups + i][...] for i in range(groups)], axis=0)
        a = jnp.dot(own_a[s], panel, preferred_element_type=jnp.float32)
        b = jnp.dot(sib_a[s], panel, preferred_element_type=jnp.float32)
        own = a if own is None else own + a
        sib = b if sib is None else sib + b
    own_out[...] = own
    sib_out[...] = sib.astype(sib_out.dtype)


def forward_product(own_a, sib_a, slabs, groups):
    slots, span, _ = own_a.shape
    width = slabs[0].shape[1]
    return pl.pallas_call(
        functools.partial(gather_kernel, slots, groups),
        out_shape=[like((span, width), jnp.float32), like((span, width), jnp.bfloat16)],
        compiler_params=pltpu.CompilerParams(vmem_limit_bytes=limit_for(own_a, sib_a, *slabs)),
        cost_estimate=pl.CostEstimate(
            flops=4 * slots * span * span * width,
            bytes_accessed=4 * slots * span * span,
            transcendentals=0,
        ),
        name="forward_product",
    )(own_a, sib_a, *slabs)


def layer_kernel(groups, core, first, second, weight, *refs):
    cots, (act_out, keep_out, pass_out, back_out, grad) = refs[:groups], refs[groups:]
    size = cots[0].shape[0]
    half = keep_out.shape[0]
    grads = []
    for i in range(groups):
        here = pl.ds(i * size, size)
        there = pl.ds((i ^ (groups // 2)) * size, size)
        total = first[here, :].astype(jnp.float32) + second[there, :].astype(jnp.float32)
        aggregated = total.astype(jnp.bfloat16)
        preact = jnp.dot(aggregated, weight[...], preferred_element_type=jnp.float32)
        s = 1.0 / (1.0 + jnp.exp(-preact))
        if i == 0:
            act_out[...] = (preact * s).astype(act_out.dtype)
        slope = cots[i][...].astype(jnp.float32) * s * (1.0 + preact * (1.0 - s))
        slope = slope.astype(jnp.bfloat16)
        grads.append(
            lax.dot_general(
                aggregated, slope, (((0,), (0,)), ((), ())), preferred_element_type=jnp.float32
            )
        )
        back = lax.dot_general(
            slope, weight[...], (((1,), (1,)), ((), ())), preferred_element_type=jnp.float32
        )
        back_out[here, :] = back.astype(back_out.dtype)
    grad[...] = tree_sum(grads)
    keep = pl.multiple_of(core[0] * half, half)
    away = pl.multiple_of((1 - core[0]) * half, half)
    keep_out[...] = grad[pl.ds(keep, half), :].astype(keep_out.dtype)
    pass_out[...] = grad[pl.ds(away, half), :].astype(pass_out.dtype)


def layer(core, first, second, weight, cots, groups):
    span, width = first.shape
    size = cots[0].shape[0]
    whole = pl.BlockSpec(memory_space=pltpu.VMEM)
    return pl.pallas_call(
        functools.partial(layer_kernel, groups),
        in_specs=[pl.BlockSpec(memory_space=pltpu.SMEM)] + [whole] * (3 + groups),
        out_shape=[
            like((size, width), jnp.bfloat16),
            like((width // 2, width), jnp.bfloat16),
            like((width // 2, width), jnp.bfloat16),
            like((span, width), jnp.bfloat16),
        ],
        scratch_shapes=[pltpu.VMEM((width, width), jnp.float32)],
        compiler_params=pltpu.CompilerParams(vmem_limit_bytes=limit_for(first, second, *cots)),
        cost_estimate=pl.CostEstimate(
            flops=6 * span * width * width,
            bytes_accessed=8 * span * width,
            transcendentals=span * width,
        ),
        name="layer",
    )(core, first, second, weight, *cots)


def scatter_kernel(slots, own_a, sib_a, own_rows, sib_rows, *outs):
    for s in range(slots):
        turned = (((0,), (0,)), ((), ()))
        total = lax.dot_general(
            own_a[s], own_rows[...], turned, preferred_element_type=jnp.float32
        ) + lax.dot_general(sib_a[s], sib_rows[...], turned, preferred_element_type=jnp.float32)
        outs[s][...] = total.astype(outs[s].dtype)


def backward_product(own_a, sib_a, own_rows, sib_rows):
    slots, span, _ = own_a.shape
    width = own_rows.shape[1]
    return pl.pallas_call(
        functools.partial(scatter_kernel, slots),
        out_shape=[
            like((span, width), jnp.float32 if s == 0 else jnp.bfloat16) for s in range(slots)
        ],
        compiler_params=pltpu.CompilerParams(
            vmem_limit_bytes=limit_for(own_a, sib_a) + slots * span * width * 8
        ),
        cost_estimate=pl.CostEstimate(
            flops=4 * slots * span * span * width,
            bytes_accessed=4 * slots * span * span,
            transcendentals=0,
        ),
        name="backward_product",
    )(own_a, sib_a, own_rows, sib_rows)


def on_device(features, weight, cotangent, tile_row, tile_col, tile_count, tile_vals):
    size, width = features.shape
    groups = lax.axis_size("rep")
    panels = lax.axis_size("blk")
    steps = panels // groups
    span = groups * size
    member = lax.axis_index("rep")
    panel = lax.axis_index("blk")
    core = panel % 2
    slots = panel_slots(groups, panels, steps)

    def across(array, bit):
        return lax.ppermute(array, "rep", xor_pairs(groups, bit))

    def along(array, bit):
        return lax.ppermute(array, "blk", xor_pairs(panels, bit))

    slabs = [features] + [across(features, i) for i in range(1, groups)]
    cots = [cotangent] + [across(cotangent, i) for i in range(1, groups)]

    shifts = [(jnp.int32(0), True)] + [(shift(member), had(member)) for _, shift, had in slots]
    own_steps, pass_steps = [], []
    for shift, had in shifts:
        for offset, into in ((0, own_steps), (2 * core - 1, pass_steps)):
            step = (shift - steps * member + offset) % panels
            into.append(jnp.where((step < steps) & had, step, -1))
    step_of = jnp.stack(own_steps + pass_steps).astype(jnp.int32)
    own_a, pass_a = place_tiles(
        step_of,
        (tile_row[0, 0] % groups) ^ member,
        (tile_col[0, 0] % groups) ^ member,
        tile_count[0, 0],
        tile_vals[0, 0],
        span,
    )
    sib_a = along(pass_a, 1)

    held = list(slabs)
    for pairs, _, _ in slots:
        held += [lax.ppermute(slab, BOTH, pairs) for slab in slabs]
    own_part, sib_part = forward_product(own_a, sib_a, held, groups)
    total = (own_part + along(sib_part, 1).astype(jnp.float32)).astype(jnp.bfloat16)
    bit = 1
    while 2 * bit < groups:
        moved = across(total, bit).reshape(groups, size, width)
        moved = moved[jnp.arange(groups) ^ bit].reshape(span, width)
        total = (total.astype(jnp.float32) + moved.astype(jnp.float32)).astype(jnp.bfloat16)
        bit *= 2
    other = across(total, bit)

    activations, grad_keep, grad_pass, back_rows = layer(
        core.reshape(1).astype(jnp.int32), total, other, weight, cots, groups
    )
    parts = backward_product(own_a, sib_a, back_rows, along(back_rows, 1))

    grad = (grad_keep.astype(jnp.float32) + along(grad_pass, 1).astype(jnp.float32)).astype(
        jnp.bfloat16
    )
    bit = 2
    while bit < panels:
        grad = (grad.astype(jnp.float32) + along(grad, bit).astype(jnp.float32)).astype(
            jnp.bfloat16
        )
        bit *= 2
    mate = along(grad, 1)
    weight_grad = jnp.where(
        core == 0, jnp.concatenate([grad, mate]), jnp.concatenate([mate, grad])
    ).astype(jnp.float32) * (1.0 / math.sqrt(size * groups * panels))

    column = parts[0]
    for (pairs, _, _), part in zip(slots, parts[1:]):
        column = column + lax.ppermute(part, BOTH, [(b, a) for a, b in pairs]).astype(jnp.float32)
    column = column.reshape(groups, size, width)
    feature_grad = column[0]
    for i in range(1, groups):
        feature_grad = feature_grad + across(column[i].astype(jnp.bfloat16), i).astype(jnp.float32)
    return activations, weight_grad, feature_grad.astype(jnp.bfloat16)


def solution(mesh):
    return jax.shard_map(
        on_device,
        mesh=mesh,
        in_specs=(
            P(BOTH, None),
            P(),
            P(BOTH, None),
            P("rep", "blk", None, None),
            P("rep", "blk", None, None),
            P("rep", "blk", None),
            P("rep", "blk", None, None, None, None),
        ),
        out_specs=(P(BOTH, None), P(), P(BOTH, None)),
        check_vma=False,
    )
```

time: 305 us -> 83.7 us (0.27)
  waiting for transfers between devices: 206 us -> 32.1 us
  matrix products: 18.3 us -> 0 us
  between operations: 14.7 us -> 0.89 us
  local copies, waits for them, and re-layouts: 15.2 us -> 3.39 us
  blocking collectives: 11.2 us -> 0 us
  Pallas kernels: 0 us -> 7.21 us
  starting transfers between devices: 34.5 us -> 37.6 us
    psum x1 -> x0, waiting for transfers between devices: 120 us -> none  [on_device(): lax.psum(local_grad, ('rep', 'blk')) * (1.0 / math.sqrt(total_nodes))]
    ppermute x16 -> x24, waiting for transfers between devices: 66.7 us -> 32.1 us  [the longest x8 12.7 us: on_device(): held += [lax.ppermute(slab, BOTH, pairs) for slab in slabs]]
    reduce_scatter x2 -> x0, waiting for transfers between devices: 19.5 us -> none  [the longest x1 10.5 us: on_device(): lax.psum_scatter(carried.reshape(-1, width).astype(jnp.bfloat16), 'rep',...]
    dot_general x35 -> x0, matrix products: 18.3 us -> none  [the longest x8 5.09 us: forward_terms(): jnp.einsum('kc,kif->cif', select_rows, product, precision=lax.Precision.H...]
    all_gather x2 -> x0, blocking collectives: 11.2 us -> none  [the longest x1 6.24 us: on_device(): panel = lax.all_gather(features, 'rep', axis=0, tiled=True)]
    gather x16 -> x0, local copies, waits for them, and re-layouts: 9 us -> none  [the longest x8 4.51 us: backward_terms(): picked = jnp.take(panel, rows_local, axis=0)]
    pallas_call x0 -> x4, Pallas kernels: none -> 7.21 us  [the longest x1 5.09 us: place_tiles(): pl.pallas_call(place_kernel, grid_spec=pltpu.PrefetchScalarGridSpec(num_s...]
    dot_general x16 -> x0, local copies, waits for them, and re-layouts: 3.71 us -> none  [the longest x8 1.86 us: backward_terms(): jnp.einsum('kji,kjf->kif', tiles, picked, preferred_element_type=jnp.floa...]
  transfers between devices with their start and end apart: 19 -> 24, of which waited for: 19 -> 12; matrix products, arithmetic and copies ran while one was open for 7% -> 1% of each run, Pallas kernels for 0% -> 1%
where the time goes in v1:
time: 83.7 us; the launch traced here: 83.3 us
  starting transfers between devices  37.6 us (45%)
  waiting for transfers between devices  32.1 us (38%)
  Pallas kernels  7.21 us (9%)
  local copies, waits for them, and re-layouts  3.39 us (4%)
  other arithmetic  2.09 us (2%)
  between operations  0.89 us (1%)
    ppermute x4, starting transfers between devices, across(): return lax.ppermute(array, 'rep', xor_pairs(groups, bit))  19.6 us
    ppermute x8, waiting for transfers between devices, on_device(): held += [lax.ppermute(slab, BOTH, pairs) for slab in slabs]  12.7 us
    ppermute x8, starting transfers between devices, on_device(): held += [lax.ppermute(slab, BOTH, pairs) for slab in slabs]  8.28 us
    ppermute x4, waiting for transfers between devices, across(): return lax.ppermute(array, 'rep', xor_pairs(groups, bit))  7.27 us
    ppermute x4, waiting for transfers between devices, on_device(): lax.ppermute(part, BOTH, [(b, a) for a, b in pairs]).astype(jnp.float32)  6.18 us
    ppermute x8, waiting for transfers between devices, along(): return lax.ppermute(array, 'blk', xor_pairs(panels, bit))  5.93 us
    ppermute x4, starting transfers between devices, on_device(): lax.ppermute(part, BOTH, [(b, a) for a, b in pairs]).astype(jnp.float32)  5.73 us
    pallas_call x1, Pallas kernels, place_tiles(): pl.pallas_call(place_kernel, grid_spec=pltpu.PrefetchScalarGridSpec(num_s...  5.09 us
  transfers between devices with their start and end apart: 24, of which 12 were waited for; matrix products, arithmetic and copies ran while one was open for 1% of the time, Pallas kernels for 1%

profile of v1, /device:TPU:0, one launch (start us, length us, event | category | flops | bytes accessed | tf_op | source)
XLA Modules:
  0.0 83.3 jit_solution(5318041571348798376)
XLA Ops:
  0.8 0.0 copy-start.5
  0.8 0.7 copy-done.5
  1.5 0.1 copy.12
  1.5 0.1 squeeze.14
  1.6 0.6 copy-done.6
  2.2 0.1 copy.13
  2.3 0.1 squeeze.15
  2.4 0.5 fusion.1
  2.9 0.7 stack.43.step_of
  3.6 5.1 %place_tiles.1 = (bf16[5,256,256]{2,1,0:T(8,128)(2,1)}, bf16[5,256,256]{2,1,0:T(8,128)(2,1)}) custom-call(s32[10]{0:T(128)} %stack.43.step_of, s32[32]{0:T(128)} %get-tuple-element.29.rows, s32[32]{0:T(128)} %get-tuple-element.30.cols, s32[8]{0:T(128)} %bitcast.19, bf16[8,4,128,128]{3,2,1,0:T(8,128)(2,1)} %bitcast.17, bf16[8,4,128,128]{3,2,1,0:T(8,128)(2,1)} %bitcast.18), custom_call_target="tpu_custom_call" | custom-call | bytes 2621440 | tf_op jit(solution)/shard_map/place_tiles/pallas_call | solution.py:88
  8.7 0.4 collective-permute-start
  9.1 2.5 %collective-permute-start.1 = (bf16[128,256]{1,0:T(8,128)(2,1)S(1)}, bf16[128,256]{1,0:T(8,128)(2,1)S(1)}, u32[]{:S(2)}, u32[]{:S(2)}) collective-permute-start(bf16[128,256]{1,0:T(8,128)(2,1)S(1)} %copy-done.3), channel_id=1, source_target_pairs={{0,16},{16,0},{1,17},{17,1},{2,18},{18,2},{3,19},{19,3},{4,20},{20... | collective-permute-start | bytes 196616 | tf_op jit(solution)/shard_map/ppermute | solution.py:230
  11.7 0.7 collective-permute-start.2
  12.3 1.7 %collective-permute-start.4 = (bf16[128,256]{1,0:T(8,128)(2,1)S(1)}, bf16[128,256]{1,0:T(8,128)(2,1)S(1)}, u32[]{:S(2)}, u32[]{:S(2)}) collective-permute-start(bf16[128,256]{1,0:T(8,128)(2,1)S(1)} %copy-done.3), channel_id=1, source_target_pairs={{0,2},{1,3},{2,4},{3,5},{4,6},{5,7},{6,8},{7,9},{8,10},{9,11},{10,... | collective-permute-start | bytes 196616 | tf_op jit(solution)/shard_map/ppermute | solution.py:257
  14.0 1.5 %collective-permute-start.6 = (bf16[128,256]{1,0:T(8,128)(2,1)S(1)}, bf16[128,256]{1,0:T(8,128)(2,1)S(1)}, u32[]{:S(2)}, u32[]{:S(2)}) collective-permute-start(bf16[128,256]{1,0:T(8,128)(2,1)S(1)} %copy-done.3), channel_id=1, source_target_pairs={{0,4},{1,5},{2,6},{3,7},{4,8},{5,9},{6,10},{7,11},{8,12},{9,13},{1... | collective-permute-start | bytes 196616 | tf_op jit(solution)/shard_map/ppermute | solution.py:257
  15.5 0.0 collective-permute-done.1.refs_1_
  15.5 2.5 %collective-permute-start.8 = (bf16[128,256]{1,0:T(8,128)(2,1)S(1)}, bf16[128,256]{1,0:T(8,128)(2,1)S(1)}, u32[]{:S(2)}, u32[]{:S(2)}) collective-permute-start(bf16[128,256]{1,0:T(8,128)(2,1)S(1)} %copy-done.3), channel_id=1, source_target_pairs={{0,6},{1,7},{2,8},{3,9},{4,10},{5,11},{6,12},{7,13},{8,14},{9,15},... | collective-permute-start | bytes 196616 | tf_op jit(solution)/shard_map/ppermute | solution.py:257
  18.0 0.0 collective-permute-done.2.refs_2_
  18.0 0.7 collective-permute-start.3
  18.7 1.0 %collective-permute-done.4.refs_4_ = bf16[128,256]{1,0:T(8,128)(2,1)S(1)} collective-permute-done((bf16[128,256]{1,0:T(8,128)(2,1)S(1)}, bf16[128,256]{1,0:T(8,128)(2,1)S(1)}, u32[]{:S(2)}, u32[]{:S(2)}) %collective-permute-start.4) | collective-permute-done | bytes 65568 | tf_op jit(solution)/shard_map/ppermute | solution.py:257
  19.7 0.5 collective-permute-start.5
  20.3 0.0 collective-permute-done.6.refs_6_
  20.3 0.8 collective-permute-start.7
  21.0 3.8 %collective-permute-done.8.refs_8_ = bf16[128,256]{1,0:T(8,128)(2,1)S(1)} collective-permute-done((bf16[128,256]{1,0:T(8,128)(2,1)S(1)}, bf16[128,256]{1,0:T(8,128)(2,1)S(1)}, u32[]{:S(2)}, u32[]{:S(2)}) %collective-permute-start.8) | collective-permute-done | bytes 65568 | tf_op jit(solution)/shard_map/ppermute | solution.py:257
  24.8 0.0 collective-permute-start.9
  24.8 0.0 collective-permute-done.3.refs_3_
  24.8 1.9 %collective-permute-done.5.refs_5_ = bf16[128,256]{1,0:T(8,128)(2,1)S(1)} collective-permute-done((bf16[128,256]{1,0:T(8,128)(2,1)S(1)}, bf16[128,256]{1,0:T(8,128)(2,1)S(1)}, u32[]{:S(2)}, u32[]{:S(2)}) %collective-permute-start.5) | collective-permute-done | bytes 65568 | tf_op jit(solution)/shard_map/ppermute | solution.py:257
  26.7 0.0 collective-permute-done.7.refs_7_
  26.7 6.0 %collective-permute-done.9.refs_9_ = bf16[128,256]{1,0:T(8,128)(2,1)S(1)} collective-permute-done((bf16[128,256]{1,0:T(8,128)(2,1)S(1)}, bf16[128,256]{1,0:T(8,128)(2,1)S(1)}, u32[]{:S(2)}, u32[]{:S(2)}) %collective-permute-start.9) | collective-permute-done | bytes 65568 | tf_op jit(solution)/shard_map/ppermute | solution.py:257
  32.7 0.0 collective-permute-done.sib_a
  32.7 1.1 %copy-done = bf16[5,256,256]{2,1,0:T(8,128)(2,1)S(1)} copy-done((bf16[5,256,256]{2,1,0:T(8,128)(2,1)S(1)}, bf16[5,256,256]{2,1,0:T(8,128)(2,1)}, u32[]{:S(2)}) %copy-start) | copy-done | bytes 655384
  33.8 0.5 forward_product.1
  34.3 0.2 collective-permute-start.10
  34.5 1.2 %collective-permute-done.10 = bf16[256,256]{1,0:T(8,128)(2,1)S(1)} collective-permute-done((bf16[256,256]{1,0:T(8,128)(2,1)S(1)}, bf16[256,256]{1,0:T(8,128)(2,1)S(1)}, u32[]{:S(2)}, u32[]{:S(2)}) %collective-permute-start.10) | collective-permute-done | bytes 131104 | tf_op jit(solution)/shard_map/ppermute | solution.py:233
  35.8 4.3 %collective-permute-start.11 = (bf16[256,256]{1,0:T(8,128)(2,1)S(1)}, bf16[256,256]{1,0:T(8,128)(2,1)S(1)}, u32[]{:S(2)}, u32[]{:S(2)}) collective-permute-start(bf16[256,256]{1,0:T(8,128)(2,1)S(1)} %add_convert_fusion.first), channel_id=1, source_target_pairs={{0,16},{16,0},{1,17},{17,1},{2,18},{18,2},{3,19},{19,3},{4,20},{20... | collective-permute-start | bytes 393224 | tf_op jit(solution)/shard_map/ppermute | solution.py:230
  40.1 0.1 collective-permute-start.12
  40.2 5.1 %collective-permute-done.12.refs_1_ = bf16[128,256]{1,0:T(8,128)(2,1)S(1)} collective-permute-done((bf16[128,256]{1,0:T(8,128)(2,1)S(1)}, bf16[128,256]{1,0:T(8,128)(2,1)S(1)}, u32[]{:S(2)}, u32[]{:S(2)}) %collective-permute-start.12) | collective-permute-done | bytes 65568 | tf_op jit(solution)/shard_map/ppermute | solution.py:230
  45.3 0.0 collective-permute-done.11.second
  45.3 1.1 %layer.1 = (bf16[128,256]{1,0:T(8,128)(2,1)}, bf16[128,256]{1,0:T(8,128)(2,1)S(1)}, bf16[128,256]{1,0:T(8,128)(2,1)S(1)}, bf16[256,256]{1,0:T(8,128)(2,1)S(1)}) custom-call(s32[1]{0:T(128)} %bitcast.core, bf16[256,256]{1,0:T(8,128)(2,1)S(1)} %add_convert_fusion.first, bf16[256,256]{1,0:T(8,128)(2,1)S(1)} %collective-permute-done.11.second, ...), custom_call_target="tpu_custom_call" | custom-call | flops 100663296 | bytes 524288 | tf_op jit(solution)/shard_map/layer/pallas_call | solution.py:169
  46.4 0.0 collective-permute-start.13
  46.4 1.3 %collective-permute-done.13 = bf16[128,256]{1,0:T(8,128)(2,1)S(1)} collective-permute-done((bf16[128,256]{1,0:T(8,128)(2,1)S(1)}, bf16[128,256]{1,0:T(8,128)(2,1)S(1)}, u32[]{:S(2)}, u32[]{:S(2)}) %collective-permute-start.13) | collective-permute-done | bytes 65568 | tf_op jit(solution)/shard_map/ppermute | solution.py:233
  47.7 0.9 %collective-permute-start.14 = (bf16[128,256]{1,0:T(8,128)(2,1)S(1)}, bf16[128,256]{1,0:T(8,128)(2,1)S(1)}, u32[]{:S(2)}, u32[]{:S(2)}) collective-permute-start(bf16[128,256]{1,0:T(8,128)(2,1)S(1)} %add_convert_fusion.4), channel_id=1, source_target_pairs={{0,2},{1,3},{2,0},{3,1},{4,6},{5,7},{6,4},{7,5},{8,10},{9,11},{10,... | collective-permute-start | bytes 196616 | tf_op jit(solution)/shard_map/ppermute | solution.py:233
  48.6 0.0 collective-permute-start.18
  48.6 3.4 %collective-permute-done.14 = bf16[128,256]{1,0:T(8,128)(2,1)S(1)} collective-permute-done((bf16[128,256]{1,0:T(8,128)(2,1)S(1)}, bf16[128,256]{1,0:T(8,128)(2,1)S(1)}, u32[]{:S(2)}, u32[]{:S(2)}) %collective-permute-start.14) | collective-permute-done | bytes 65568 | tf_op jit(solution)/shard_map/ppermute | solution.py:233
  52.0 1.1 %collective-permute-start.15 = (bf16[128,256]{1,0:T(8,128)(2,1)S(1)}, bf16[128,256]{1,0:T(8,128)(2,1)S(1)}, u32[]{:S(2)}, u32[]{:S(2)}) collective-permute-start(bf16[128,256]{1,0:T(8,128)(2,1)S(1)} %add_convert_fusion.3), channel_id=1, source_target_pairs={{0,4},{1,5},{2,6},{3,7},{4,0},{5,1},{6,2},{7,3},{8,12},{9,13},{10,... | collective-permute-start | bytes 196616 | tf_op jit(solution)/shard_map/ppermute | solution.py:233
  53.1 0.0 collective-permute-done.18.sib_rows
  53.1 0.6 backward_product.1
  53.7 0.7 collective-permute-start.19
  54.3 3.1 %collective-permute-start.20 = (bf16[256,256]{1,0:T(8,128)(2,1)S(1)}, bf16[256,256]{1,0:T(8,128)(2,1)S(1)}, u32[]{:S(2)}, u32[]{:S(2)}) collective-permute-start(bf16[256,256]{1,0:T(8,128)(2,1)S(1)} %get-tuple-element.26), channel_id=1, source_target_pairs={{2,0},{3,1},{4,2},{5,3},{6,4},{7,5},{8,6},{9,7},{10,8},{11,9},{12,... | collective-permute-start | bytes 393224 | tf_op jit(solution)/shard_map/ppermute | solution.py:289
  57.4 2.0 %collective-permute-start.21 = (bf16[256,256]{1,0:T(8,128)(2,1)S(1)}, bf16[256,256]{1,0:T(8,128)(2,1)S(1)}, u32[]{:S(2)}, u32[]{:S(2)}) collective-permute-start(bf16[256,256]{1,0:T(8,128)(2,1)S(1)} %get-tuple-element.27), channel_id=1, source_target_pairs={{4,0},{5,1},{6,2},{7,3},{8,4},{9,5},{10,6},{11,7},{12,8},{13,9},{1... | collective-permute-start | bytes 393224 | tf_op jit(solution)/shard_map/ppermute | solution.py:289
  59.4 0.0 collective-permute-start.22
  59.4 0.0 collective-permute-done.15
  59.4 1.3 %collective-permute-start.16 = (bf16[128,256]{1,0:T(8,128)(2,1)S(1)}, bf16[128,256]{1,0:T(8,128)(2,1)S(1)}, u32[]{:S(2)}, u32[]{:S(2)}) collective-permute-start(bf16[128,256]{1,0:T(8,128)(2,1)S(1)} %add_convert_fusion.2), channel_id=1, source_target_pairs={{0,8},{1,9},{2,10},{3,11},{4,12},{5,13},{6,14},{7,15},{8,0},{9,1},... | collective-permute-start | bytes 196616 | tf_op jit(solution)/shard_map/ppermute | solution.py:233
  60.8 0.0 collective-permute-done.19
  60.8 0.6 collective-permute-done.20
  61.3 4.2 %collective-permute-done.21 = bf16[256,256]{1,0:T(8,128)(2,1)S(1)} collective-permute-done((bf16[256,256]{1,0:T(8,128)(2,1)S(1)}, bf16[256,256]{1,0:T(8,128)(2,1)S(1)}, u32[]{:S(2)}, u32[]{:S(2)}) %collective-permute-start.21) | collective-permute-done | bytes 131104 | tf_op jit(solution)/shard_map/ppermute | solution.py:289
  65.6 1.4 %collective-permute-done.22 = bf16[256,256]{1,0:T(8,128)(2,1)S(1)} collective-permute-done((bf16[256,256]{1,0:T(8,128)(2,1)S(1)}, bf16[256,256]{1,0:T(8,128)(2,1)S(1)}, u32[]{:S(2)}, u32[]{:S(2)}) %collective-permute-start.22) | collective-permute-done | bytes 131104 | tf_op jit(solution)/shard_map/ppermute | solution.py:289
  66.9 0.1 convert_add_fusion
  67.0 12.6 %collective-permute-start.23 = (bf16[128,256]{1,0:T(8,128)(2,1)S(1)}, bf16[128,256]{1,0:T(8,128)(2,1)S(1)}, u32[]{:S(2)}, u32[]{:S(2)}) collective-permute-start(bf16[128,256]{1,0:T(8,128)(2,1)S(1)} %slice.17), channel_id=1, source_target_pairs={{0,16},{16,0},{1,17},{17,1},{2,18},{18,2},{3,19},{19,3},{4,20},{20... | collective-permute-start | bytes 196616 | tf_op jit(solution)/shard_map/ppermute | solution.py:230
  79.7 0.1 collective-permute-start.17
  79.8 2.1 %collective-permute-done.23 = bf16[128,256]{1,0:T(8,128)(2,1)S(1)} collective-permute-done((bf16[128,256]{1,0:T(8,128)(2,1)S(1)}, bf16[128,256]{1,0:T(8,128)(2,1)S(1)}, u32[]{:S(2)}, u32[]{:S(2)}) %collective-permute-start.23) | collective-permute-done | bytes 65568 | tf_op jit(solution)/shard_map/ppermute | solution.py:230
  81.9 0.6 fusion
  82.6 0.0 collective-permute-done.17
  82.6 0.7 convert_multiply_fusion
  (17 shorter events, 0.1 us)
Async XLA Ops:
  0.8 0.7 copy-start.5
  1.5 0.7 copy-start.6
  3.6 5.5 %copy-start.3 = (bf16[128,256]{1,0:T(8,128)(2,1)S(1)}, bf16[128,256]{1,0:T(8,128)(2,1)}, u32[]{:S(2)}) copy-start(bf16[128,256]{1,0:T(8,128)(2,1)} %refs_0_.2) | copy-start | bytes 196612
  8.7 24.0 %collective-permute-start = (bf16[5,256,256]{2,1,0:T(8,128)(2,1)}, bf16[5,256,256]{2,1,0:T(8,128)(2,1)S(1)}, u32[]{:S(2)}, u32[]{:S(2)}) collective-permute-start(bf16[5,256,256]{2,1,0:T(8,128)(2,1)} %get-tuple-element.17), channel_id=1, source_target_pairs={{0,1},{1,0},{2,3},{3,2},{4,5},{5,4},{6,7},{7,6},{8,9},{9,8},{10,11... | collective-permute-start | bytes 1966088 | tf_op jit(solution)/shard_map/ppermute | solution.py:233
  9.1 6.3 %collective-permute-start.1 = (bf16[128,256]{1,0:T(8,128)(2,1)S(1)}, bf16[128,256]{1,0:T(8,128)(2,1)S(1)}, u32[]{:S(2)}, u32[]{:S(2)}) collective-permute-start(bf16[128,256]{1,0:T(8,128)(2,1)S(1)} %copy-done.3), channel_id=1, source_target_pairs={{0,16},{16,0},{1,17},{17,1},{2,18},{18,2},{3,19},{19,3},{4,20},{20... | collective-permute-start | bytes 196616 | tf_op jit(solution)/shard_map/ppermute | solution.py:230
  11.7 6.3 %collective-permute-start.2 = (bf16[128,256]{1,0:T(8,128)(2,1)S(1)}, bf16[128,256]{1,0:T(8,128)(2,1)S(1)}, u32[]{:S(2)}, u32[]{:S(2)}) collective-permute-start(bf16[128,256]{1,0:T(8,128)(2,1)S(1)} %copy-done.3), channel_id=1, source_target_pairs={{16,24},{17,25},{18,26},{19,27},{20,28},{21,29},{22,30},{23,31},{2... | collective-permute-start | bytes 196616 | tf_op jit(solution)/shard_map/ppermute | solution.py:257
  12.3 7.4 %collective-permute-start.4 = (bf16[128,256]{1,0:T(8,128)(2,1)S(1)}, bf16[128,256]{1,0:T(8,128)(2,1)S(1)}, u32[]{:S(2)}, u32[]{:S(2)}) collective-permute-start(bf16[128,256]{1,0:T(8,128)(2,1)S(1)} %copy-done.3), channel_id=1, source_target_pairs={{0,2},{1,3},{2,4},{3,5},{4,6},{5,7},{6,8},{7,9},{8,10},{9,11},{10,... | collective-permute-start | bytes 196616 | tf_op jit(solution)/shard_map/ppermute | solution.py:257
  14.0 6.3 %collective-permute-start.6 = (bf16[128,256]{1,0:T(8,128)(2,1)S(1)}, bf16[128,256]{1,0:T(8,128)(2,1)S(1)}, u32[]{:S(2)}, u32[]{:S(2)}) collective-permute-start(bf16[128,256]{1,0:T(8,128)(2,1)S(1)} %copy-done.3), channel_id=1, source_target_pairs={{0,4},{1,5},{2,6},{3,7},{4,8},{5,9},{6,10},{7,11},{8,12},{9,13},{1... | collective-permute-start | bytes 196616 | tf_op jit(solution)/shard_map/ppermute | solution.py:257
  15.5 9.3 %collective-permute-start.8 = (bf16[128,256]{1,0:T(8,128)(2,1)S(1)}, bf16[128,256]{1,0:T(8,128)(2,1)S(1)}, u32[]{:S(2)}, u32[]{:S(2)}) collective-permute-start(bf16[128,256]{1,0:T(8,128)(2,1)S(1)} %copy-done.3), channel_id=1, source_target_pairs={{0,6},{1,7},{2,8},{3,9},{4,10},{5,11},{6,12},{7,13},{8,14},{9,15},... | collective-permute-start | bytes 196616 | tf_op jit(solution)/shard_map/ppermute | solution.py:257
  18.0 6.8 %collective-permute-start.3 = (bf16[128,256]{1,0:T(8,128)(2,1)S(1)}, bf16[128,256]{1,0:T(8,128)(2,1)S(1)}, u32[]{:S(2)}, u32[]{:S(2)}) collective-permute-start(bf16[128,256]{1,0:T(8,128)(2,1)S(1)} %collective-permute-done.1.refs_1_), channel_id=1, source_target_pairs={{16,24},{17,25},{18,26},{19,27},{20,28},{21,29},{22,30},{23,31},{2... | collective-permute-start | bytes 196616 | tf_op jit(solution)/shard_map/ppermute | solution.py:257
  19.7 7.0 %collective-permute-start.5 = (bf16[128,256]{1,0:T(8,128)(2,1)S(1)}, bf16[128,256]{1,0:T(8,128)(2,1)S(1)}, u32[]{:S(2)}, u32[]{:S(2)}) collective-permute-start(bf16[128,256]{1,0:T(8,128)(2,1)S(1)} %collective-permute-done.1.refs_1_), channel_id=1, source_target_pairs={{0,2},{1,3},{2,4},{3,5},{4,6},{5,7},{6,8},{7,9},{8,10},{9,11},{10,... | collective-permute-start | bytes 196616 | tf_op jit(solution)/shard_map/ppermute | solution.py:257
  20.3 6.5 %collective-permute-start.7 = (bf16[128,256]{1,0:T(8,128)(2,1)S(1)}, bf16[128,256]{1,0:T(8,128)(2,1)S(1)}, u32[]{:S(2)}, u32[]{:S(2)}) collective-permute-start(bf16[128,256]{1,0:T(8,128)(2,1)S(1)} %collective-permute-done.1.refs_1_), channel_id=1, source_target_pairs={{0,4},{1,5},{2,6},{3,7},{4,8},{5,9},{6,10},{7,11},{8,12},{9,13},{1... | collective-permute-start | bytes 196616 | tf_op jit(solution)/shard_map/ppermute | solution.py:257
  24.8 8.0 %collective-permute-start.9 = (bf16[128,256]{1,0:T(8,128)(2,1)S(1)}, bf16[128,256]{1,0:T(8,128)(2,1)S(1)}, u32[]{:S(2)}, u32[]{:S(2)}) collective-permute-start(bf16[128,256]{1,0:T(8,128)(2,1)S(1)} %collective-permute-done.1.refs_1_), channel_id=1, source_target_pairs={{0,6},{1,7},{2,8},{3,9},{4,10},{5,11},{6,12},{7,13},{8,14},{9,15},... | collective-permute-start | bytes 196616 | tf_op jit(solution)/shard_map/ppermute | solution.py:257
  32.7 1.1 %copy-start = (bf16[5,256,256]{2,1,0:T(8,128)(2,1)S(1)}, bf16[5,256,256]{2,1,0:T(8,128)(2,1)}, u32[]{:S(2)}) copy-start(bf16[5,256,256]{2,1,0:T(8,128)(2,1)} %get-tuple-element.16.own_a) | copy-start | bytes 1966084
  33.8 6.3 %copy-start.4 = (bf16[128,256]{1,0:T(8,128)(2,1)S(1)}, bf16[128,256]{1,0:T(8,128)(2,1)}, u32[]{:S(2)}) copy-start(bf16[128,256]{1,0:T(8,128)(2,1)} %refs_0_.3) | copy-start | bytes 196612
  33.8 11.5 %copy-start.2 = (bf16[256,256]{1,0:T(8,128)(2,1)S(1)}, bf16[256,256]{1,0:T(8,128)(2,1)}, u32[]{:S(2)}) copy-start(bf16[256,256]{1,0:T(8,128)(2,1)} %weight.1) | copy-start | bytes 393220
  34.3 1.4 %collective-permute-start.10 = (bf16[256,256]{1,0:T(8,128)(2,1)S(1)}, bf16[256,256]{1,0:T(8,128)(2,1)S(1)}, u32[]{:S(2)}, u32[]{:S(2)}) collective-permute-start(bf16[256,256]{1,0:T(8,128)(2,1)S(1)} %get-tuple-element.19), channel_id=1, source_target_pairs={{0,1},{1,0},{2,3},{3,2},{4,5},{5,4},{6,7},{7,6},{8,9},{9,8},{10,11... | collective-permute-start | bytes 393224 | tf_op jit(solution)/shard_map/ppermute | solution.py:233
  35.7 17.4 %copy-start.1 = (bf16[5,256,256]{2,1,0:T(8,128)(2,1)S(1)}, bf16[5,256,256]{2,1,0:T(8,128)(2,1)}, u32[]{:S(2)}) copy-start(bf16[5,256,256]{2,1,0:T(8,128)(2,1)} %get-tuple-element.16.own_a) | copy-start | bytes 1966084
  35.8 9.6 %collective-permute-start.11 = (bf16[256,256]{1,0:T(8,128)(2,1)S(1)}, bf16[256,256]{1,0:T(8,128)(2,1)S(1)}, u32[]{:S(2)}, u32[]{:S(2)}) collective-permute-start(bf16[256,256]{1,0:T(8,128)(2,1)S(1)} %add_convert_fusion.first), channel_id=1, source_target_pairs={{0,16},{16,0},{1,17},{17,1},{2,18},{18,2},{3,19},{19,3},{4,20},{20... | collective-permute-start | bytes 393224 | tf_op jit(solution)/shard_map/ppermute | solution.py:230
  40.1 5.2 %collective-permute-start.12 = (bf16[128,256]{1,0:T(8,128)(2,1)S(1)}, bf16[128,256]{1,0:T(8,128)(2,1)S(1)}, u32[]{:S(2)}, u32[]{:S(2)}) collective-permute-start(bf16[128,256]{1,0:T(8,128)(2,1)S(1)} %copy-done.4), channel_id=1, source_target_pairs={{0,16},{16,0},{1,17},{17,1},{2,18},{18,2},{3,19},{19,3},{4,20},{20... | collective-permute-start | bytes 196616 | tf_op jit(solution)/shard_map/ppermute | solution.py:230
  46.4 1.3 %collective-permute-start.13 = (bf16[128,256]{1,0:T(8,128)(2,1)S(1)}, bf16[128,256]{1,0:T(8,128)(2,1)S(1)}, u32[]{:S(2)}, u32[]{:S(2)}) collective-permute-start(bf16[128,256]{1,0:T(8,128)(2,1)S(1)} %get-tuple-element.22), channel_id=1, source_target_pairs={{0,1},{1,0},{2,3},{3,2},{4,5},{5,4},{6,7},{7,6},{8,9},{9,8},{10,11... | collective-permute-start | bytes 196616 | tf_op jit(solution)/shard_map/ppermute | solution.py:233
  47.7 4.3 %collective-permute-start.14 = (bf16[128,256]{1,0:T(8,128)(2,1)S(1)}, bf16[128,256]{1,0:T(8,128)(2,1)S(1)}, u32[]{:S(2)}, u32[]{:S(2)}) collective-permute-start(bf16[128,256]{1,0:T(8,128)(2,1)S(1)} %add_convert_fusion.4), channel_id=1, source_target_pairs={{0,2},{1,3},{2,0},{3,1},{4,6},{5,7},{6,4},{7,5},{8,10},{9,11},{10,... | collective-permute-start | bytes 196616 | tf_op jit(solution)/shard_map/ppermute | solution.py:233
  48.6 4.5 %collective-permute-start.18 = (bf16[256,256]{1,0:T(8,128)(2,1)S(1)}, bf16[256,256]{1,0:T(8,128)(2,1)S(1)}, u32[]{:S(2)}, u32[]{:S(2)}) collective-permute-start(bf16[256,256]{1,0:T(8,128)(2,1)S(1)} %get-tuple-element.23.own_rows), channel_id=1, source_target_pairs={{0,1},{1,0},{2,3},{3,2},{4,5},{5,4},{6,7},{7,6},{8,9},{9,8},{10,11... | collective-permute-start | bytes 393224 | tf_op jit(solution)/shard_map/ppermute | solution.py:233
  52.0 7.4 %collective-permute-start.15 = (bf16[128,256]{1,0:T(8,128)(2,1)S(1)}, bf16[128,256]{1,0:T(8,128)(2,1)S(1)}, u32[]{:S(2)}, u32[]{:S(2)}) collective-permute-start(bf16[128,256]{1,0:T(8,128)(2,1)S(1)} %add_convert_fusion.3), channel_id=1, source_target_pairs={{0,4},{1,5},{2,6},{3,7},{4,0},{5,1},{6,2},{7,3},{8,12},{9,13},{10,... | collective-permute-start | bytes 196616 | tf_op jit(solution)/shard_map/ppermute | solution.py:233
  53.7 7.1 %collective-permute-start.19 = (bf16[256,256]{1,0:T(8,128)(2,1)S(1)}, bf16[256,256]{1,0:T(8,128)(2,1)S(1)}, u32[]{:S(2)}, u32[]{:S(2)}) collective-permute-start(bf16[256,256]{1,0:T(8,128)(2,1)S(1)} %get-tuple-element.25), channel_id=1, source_target_pairs={{24,16},{25,17},{26,18},{27,19},{28,20},{29,21},{30,22},{31,23},{1... | collective-permute-start | bytes 393224 | tf_op jit(solution)/shard_map/ppermute | solution.py:289
  54.3 7.0 %collective-permute-start.20 = (bf16[256,256]{1,0:T(8,128)(2,1)S(1)}, bf16[256,256]{1,0:T(8,128)(2,1)S(1)}, u32[]{:S(2)}, u32[]{:S(2)}) collective-permute-start(bf16[256,256]{1,0:T(8,128)(2,1)S(1)} %get-tuple-element.26), channel_id=1, source_target_pairs={{2,0},{3,1},{4,2},{5,3},{6,4},{7,5},{8,6},{9,7},{10,8},{11,9},{12,... | collective-permute-start | bytes 393224 | tf_op jit(solution)/shard_map/ppermute | solution.py:289
  57.4 8.2 %collective-permute-start.21 = (bf16[256,256]{1,0:T(8,128)(2,1)S(1)}, bf16[256,256]{1,0:T(8,128)(2,1)S(1)}, u32[]{:S(2)}, u32[]{:S(2)}) collective-permute-start(bf16[256,256]{1,0:T(8,128)(2,1)S(1)} %get-tuple-element.27), channel_id=1, source_target_pairs={{4,0},{5,1},{6,2},{7,3},{8,4},{9,5},{10,6},{11,7},{12,8},{13,9},{1... | collective-permute-start | bytes 393224 | tf_op jit(solution)/shard_map/ppermute | solution.py:289
  59.4 7.5 %collective-permute-start.22 = (bf16[256,256]{1,0:T(8,128)(2,1)S(1)}, bf16[256,256]{1,0:T(8,128)(2,1)S(1)}, u32[]{:S(2)}, u32[]{:S(2)}) collective-permute-start(bf16[256,256]{1,0:T(8,128)(2,1)S(1)} %get-tuple-element.28), channel_id=1, source_target_pairs={{6,0},{7,1},{8,2},{9,3},{10,4},{11,5},{12,6},{13,7},{14,8},{15,9},... | collective-permute-start | bytes 393224 | tf_op jit(solution)/shard_map/ppermute | solution.py:289
  59.4 20.3 %collective-permute-start.16 = (bf16[128,256]{1,0:T(8,128)(2,1)S(1)}, bf16[128,256]{1,0:T(8,128)(2,1)S(1)}, u32[]{:S(2)}, u32[]{:S(2)}) collective-permute-start(bf16[128,256]{1,0:T(8,128)(2,1)S(1)} %add_convert_fusion.2), channel_id=1, source_target_pairs={{0,8},{1,9},{2,10},{3,11},{4,12},{5,13},{6,14},{7,15},{8,0},{9,1},... | collective-permute-start | bytes 196616 | tf_op jit(solution)/shard_map/ppermute | solution.py:233
  67.0 14.9 %collective-permute-start.23 = (bf16[128,256]{1,0:T(8,128)(2,1)S(1)}, bf16[128,256]{1,0:T(8,128)(2,1)S(1)}, u32[]{:S(2)}, u32[]{:S(2)}) collective-permute-start(bf16[128,256]{1,0:T(8,128)(2,1)S(1)} %slice.17), channel_id=1, source_target_pairs={{0,16},{16,0},{1,17},{17,1},{2,18},{18,2},{3,19},{19,3},{4,20},{20... | collective-permute-start | bytes 196616 | tf_op jit(solution)/shard_map/ppermute | solution.py:230
  79.7 2.9 %collective-permute-start.17 = (bf16[128,256]{1,0:T(8,128)(2,1)S(1)}, bf16[128,256]{1,0:T(8,128)(2,1)S(1)}, u32[]{:S(2)}, u32[]{:S(2)}) collective-permute-start(bf16[128,256]{1,0:T(8,128)(2,1)S(1)} %add_convert_fusion.1), channel_id=1, source_target_pairs={{0,1},{1,0},{2,3},{3,2},{4,5},{5,4},{6,7},{7,6},{8,9},{9,8},{10,11... | collective-permute-start | bytes 196616 | tf_op jit(solution)/shard_map/ppermute | solution.py:233

commit v2 on v1

v2 whole, which is shorter than its diff:
```python
import functools
import math

import jax
import jax.numpy as jnp
from jax import lax
from jax.experimental import pallas as pl
from jax.experimental.pallas import tpu as pltpu
from jax.sharding import PartitionSpec as P

BOTH = ("rep", "blk")


def xor_pairs(count, bit):
    return [(i, i ^ bit) for i in range(count)]


def tree_sum(terms):
    terms = list(terms)
    while len(terms) > 1:
        terms = [terms[i] + terms[i + 1] for i in range(0, len(terms), 2)]
    return terms[0]


def limit_for(*arrays):
    total = sum(math.prod(a.shape) * a.dtype.itemsize for a in arrays)
    return int(2 * total + (8 << 20))


def like(shape, dtype):
    return jax.ShapeDtypeStruct(shape, dtype)


def after(value, *others):
    return lax.optimization_barrier((value,) + others)[0]


def pairs_of(groups, panels, target, members=None, odd_only=False):
    return [
        (m * panels + p, m * panels + target(m, p) % panels)
        for m in (range(groups) if members is None else members)
        for p in range(panels)
        if not (odd_only and p % 2 == 0)
    ]


def back(pairs):
    return [(b, a) for a, b in pairs]


def move(array, pairs):
    return lax.ppermute(array, BOTH, pairs)


def across(array, bit):
    return lax.ppermute(array, "rep", xor_pairs(lax.axis_size("rep"), bit))


def along(array, bit):
    return lax.ppermute(array, "blk", xor_pairs(lax.axis_size("blk"), bit))


class Direct:
    def __init__(self, groups, panels):
        self.groups, steps = groups, panels // groups
        self.steps = steps
        first = pairs_of(groups, panels, lambda m, p: p + steps * m, range(1, groups))
        last = pairs_of(
            groups, panels, lambda m, p: p + steps * (m + 1), range(groups - 1), odd_only=True
        )
        self.moves = [first, last] + [
            pairs_of(groups, panels, functools.partial(lambda k, m, p: p + steps * m + 2 * k, k))
            for k in range(1, steps // 2)
        ]

    def shifts(self, member, panel):
        steps, groups = self.steps, self.groups
        return [
            (0, True),
            (steps * member, member >= 1),
            (steps * (member + 1), member <= groups - 2),
        ] + [(steps * member + 2 * k, True) for k in range(1, steps // 2)]

    def gather(self, slab, early, placed):
        slabs = [slab] + [across(slab, i) for i in range(1, self.groups)]
        return [slabs] + [[move(part, pairs) for part in slabs] for pairs in self.moves]

    def part_types(self):
        return [jnp.float32] + [jnp.bfloat16] * len(self.moves)

    def scatter(self, parts, size):
        column = parts[0]
        for pairs, part in zip(self.moves, parts[1:]):
            column = column + move(part, back(pairs)).astype(jnp.float32)
        total = column[:size]
        for i in range(1, self.groups):
            piece = column[i * size : (i + 1) * size].astype(jnp.bfloat16)
            total = total + across(piece, i).astype(jnp.float32)
        return total, column


class Halves:
    def __init__(self, groups, panels):
        self.panels = panels
        self.ahead = pairs_of(groups, panels, lambda m, p: p + 4 * (1 - 2 * m))
        self.cross = pairs_of(groups, panels, lambda m, p: (p ^ 2) + 4 * (1 - 2 * m))
        self.half = pairs_of(groups, panels, lambda m, p: p + panels // 2)

    @staticmethod
    def fits(groups, panels):
        return groups == 2 and panels == 8 * groups

    def shifts(self, member, panel):
        turn = 1 - 2 * member
        other = 1 - 2 * ((panel // 2) % 2)
        crossed = 4 * turn - 2 * other
        last = jnp.where(other == turn, 8 - 2 * other, -2 * other)
        return [(0, True), (self.panels // 2, True), (4 * turn, True), (crossed, True), (last, True)]

    def sends_own(self):
        return (lax.axis_index("blk") // 2) % 2 == lax.axis_index("rep")

    def gather(self, slab, early, placed):
        mate = across(slab, 1)
        far = after(move(slab, self.half), *early)
        both = jnp.concatenate([slab, mate])
        ahead = move(both, self.ahead)
        cross = move(both, self.cross)
        far_mate = across(far, 1)
        last = jnp.where(self.sends_own(), both, jnp.concatenate([far, far_mate]))
        last = along(last, 2)
        return [[both], [far, far_mate], [ahead], [cross], [last]]

    def part_types(self):
        return [jnp.float32, jnp.float32, jnp.bfloat16, jnp.bfloat16, jnp.bfloat16]

    def scatter(self, parts, size):
        own, far, ahead, cross, last = parts
        came = along(last, 2)
        ahead = move(ahead, back(self.ahead))
        cross = move(cross, back(self.cross))
        kept = self.sends_own()
        far = far + jnp.where(kept, 0.0, came.astype(jnp.float32))
        far_pass = far[size:].astype(jnp.bfloat16)
        far_sum = far[:size] + across(far_pass, 1).astype(jnp.float32)
        far_back = move(far_sum.astype(jnp.bfloat16), back(self.half))
        column = own + jnp.where(kept, after(came, far_pass).astype(jnp.float32), 0.0)
        column = column + ahead.astype(jnp.float32) + cross.astype(jnp.float32)
        mate = across(column[size:].astype(jnp.bfloat16), 1).astype(jnp.float32)
        return column[:size] + mate + far_back.astype(jnp.float32), came


def place_kernel(plan, groups, panels, *refs):
    member, panel = lax.axis_index("rep"), lax.axis_index("blk")
    shifts = plan.shifts(member, panel)
    offsets = (0, 1 - 2 * (panel % 2))
    for offset, (rows, cols, counts, tiles), out in zip(offsets, (refs[:4], refs[4:8]), refs[8:]):
        steps, cap, size, _ = tiles.shape
        for slot, (shift, had) in enumerate(shifts):
            step = lax.rem(shift - steps * member + offset + 4 * panels, panels)
            live = step < steps if had is True else (step < steps) & had
            there = jnp.where(live, step, 0)
            count = jnp.where(live, counts[there], 0)
            out[slot] = jnp.zeros(out.shape[1:], out.dtype)
            for k in range(cap):

                @pl.when(k < count)
                def _():
                    row = lax.rem(rows[k, there], groups) ^ member
                    col = lax.rem(cols[k, there], groups) ^ member
                    row = pl.multiple_of(row * size, size)
                    col = pl.multiple_of(col * size, size)
                    out[slot, pl.ds(row, size), pl.ds(col, size)] = tiles[there, k]


def place_tiles(plan, slots, own, sib, span):
    tiles = own[3]
    out = like((slots, span, span), tiles.dtype)
    scalars = pl.BlockSpec(memory_space=pltpu.SMEM)
    whole = pl.BlockSpec(memory_space=pltpu.VMEM)
    return pl.pallas_call(
        functools.partial(place_kernel, plan, lax.axis_size("rep"), lax.axis_size("blk")),
        in_specs=([scalars] * 3 + [whole]) * 2,
        out_specs=[whole] * 2,
        out_shape=[out, out],
        compiler_params=pltpu.CompilerParams(vmem_limit_bytes=limit_for(out, tiles)),
        cost_estimate=pl.CostEstimate(
            flops=0, bytes_accessed=4 * slots * span * span * 2, transcendentals=0
        ),
        name="place_tiles",
    )(*own, *sib)


def gather_kernel(counts, own_a, sib_a, *refs):
    slabs, (own_out, sib_out) = refs[:-2], refs[-2:]
    own = sib = None
    start = 0
    for s, count in enumerate(counts):
        panel = [slab[...] for slab in slabs[start : start + count]]
        start += count
        panel = panel[0] if count == 1 else jnp.concatenate(panel, axis=0)
        a = jnp.dot(own_a[s], panel, preferred_element_type=jnp.float32)
        b = jnp.dot(sib_a[s], panel, preferred_element_type=jnp.float32)
        own = a if own is None else own + a
        sib = b if sib is None else sib + b
    own_out[...] = own
    sib_out[...] = sib.astype(sib_out.dtype)


def forward_product(own_a, sib_a, held):
    slots, span, _ = own_a.shape
    slabs = [slab for slot in held for slab in slot]
    width = slabs[0].shape[1]
    return pl.pallas_call(
        functools.partial(gather_kernel, [len(slot) for slot in held]),
        out_shape=[like((span, width), jnp.float32), like((span, width), jnp.bfloat16)],
        compiler_params=pltpu.CompilerParams(vmem_limit_bytes=limit_for(own_a, sib_a, *slabs)),
        cost_estimate=pl.CostEstimate(
            flops=4 * slots * span * span * width,
            bytes_accessed=4 * slots * span * span,
            transcendentals=0,
        ),
        name="forward_product",
    )(own_a, sib_a, *slabs)


def layer_kernel(groups, first, second, weight, *refs):
    core = lax.axis_index("blk") % 2
    cots, (act_out, keep_out, pass_out, back_out, grad) = refs[:groups], refs[groups:]
    size = cots[0].shape[0]
    half = keep_out.shape[0]
    grads = []
    for i in range(groups):
        here = pl.ds(i * size, size)
        there = pl.ds((i ^ (groups // 2)) * size, size)
        total = first[here, :].astype(jnp.float32) + second[there, :].astype(jnp.float32)
        aggregated = total.astype(jnp.bfloat16)
        preact = jnp.dot(aggregated, weight[...], preferred_element_type=jnp.float32)
        s = 1.0 / (1.0 + jnp.exp(-preact))
        if i == 0:
            act_out[...] = (preact * s).astype(act_out.dtype)
        slope = cots[i][...].astype(jnp.float32) * s * (1.0 + preact * (1.0 - s))
        slope = slope.astype(jnp.bfloat16)
        grads.append(
            lax.dot_general(
                aggregated, slope, (((0,), (0,)), ((), ())), preferred_element_type=jnp.float32
            )
        )
        back = lax.dot_general(
            slope, weight[...], (((1,), (1,)), ((), ())), preferred_element_type=jnp.float32
        )
        back_out[here, :] = back.astype(back_out.dtype)
    grad[...] = tree_sum(grads)
    keep = pl.multiple_of(core * half, half)
    away = pl.multiple_of((1 - core) * half, half)
    keep_out[...] = grad[pl.ds(keep, half), :].astype(keep_out.dtype)
    pass_out[...] = grad[pl.ds(away, half), :].astype(pass_out.dtype)


def layer(first, second, weight, cots, groups):
    span, width = first.shape
    size = cots[0].shape[0]
    return pl.pallas_call(
        functools.partial(layer_kernel, groups),
        out_shape=[
            like((size, width), jnp.bfloat16),
            like((width // 2, width), jnp.bfloat16),
            like((width // 2, width), jnp.bfloat16),
            like((span, width), jnp.bfloat16),
        ],
        scratch_shapes=[pltpu.VMEM((width, width), jnp.float32)],
        compiler_params=pltpu.CompilerParams(vmem_limit_bytes=limit_for(first, second, *cots)),
        cost_estimate=pl.CostEstimate(
            flops=6 * span * width * width,
            bytes_accessed=8 * span * width,
            transcendentals=span * width,
        ),
        name="layer",
    )(first, second, weight, *cots)


def scatter_kernel(own_a, sib_a, own_rows, sib_rows, *outs):
    turned = (((0,), (0,)), ((), ()))
    for s, out in enumerate(outs):
        total = lax.dot_general(
            own_a[s], own_rows[...], turned, preferred_element_type=jnp.float32
        ) + lax.dot_general(sib_a[s], sib_rows[...], turned, preferred_element_type=jnp.float32)
        out[...] = total.astype(out.dtype)


def backward_product(own_a, sib_a, own_rows, sib_rows, types):
    slots, span, _ = own_a.shape
    width = own_rows.shape[1]
    return pl.pallas_call(
        scatter_kernel,
        out_shape=[like((span, width), kind) for kind in types],
        compiler_params=pltpu.CompilerParams(
            vmem_limit_bytes=limit_for(own_a, sib_a) + slots * span * width * 8
        ),
        cost_estimate=pl.CostEstimate(
            flops=4 * slots * span * span * width,
            bytes_accessed=4 * slots * span * span,
            transcendentals=0,
        ),
        name="backward_product",
    )(own_a, sib_a, own_rows, sib_rows)


def on_device(features, weight, cotangent, tile_row, tile_col, tile_count, tile_vals):
    size, width = features.shape
    groups = lax.axis_size("rep")
    panels = lax.axis_size("blk")
    span = groups * size
    core = lax.axis_index("blk") % 2
    plan = (Halves if Halves.fits(groups, panels) else Direct)(groups, panels)
    types = plan.part_types()

    tiles = (tile_row[0, 0].T, tile_col[0, 0].T, tile_count[0, 0], tile_vals[0, 0])
    sib_tiles = [along(t, 1) for t in tiles]
    own_a, sib_a = place_tiles(plan, len(types), tiles, sib_tiles, span)
    cots = [cotangent] + [across(cotangent, i) for i in range(1, groups)]
    held = plan.gather(features, sib_tiles + cots[1:], [own_a])

    own_part, sib_part = forward_product(own_a, sib_a, held)
    total = (own_part + along(sib_part, 1).astype(jnp.float32)).astype(jnp.bfloat16)
    bit = 1
    while 2 * bit < groups:
        moved = across(total, bit).reshape(groups, size, width)
        moved = moved[jnp.arange(groups) ^ bit].reshape(span, width)
        total = (total.astype(jnp.float32) + moved.astype(jnp.float32)).astype(jnp.bfloat16)
        bit *= 2
    other = across(total, bit)

    activations, grad_keep, grad_pass, back_rows = layer(total, other, weight, cots, groups)
    sib_rows = along(back_rows, 1)
    parts = backward_product(own_a, sib_a, back_rows, sib_rows, types)
    feature_grad, came = plan.scatter(parts, size)

    grad_pass = after(grad_pass, parts[0])
    grad = (grad_keep.astype(jnp.float32) + along(grad_pass, 1).astype(jnp.float32)).astype(
        jnp.bfloat16
    )
    grad = after(grad, came)
    bit = 2
    while bit < panels:
        grad = (grad.astype(jnp.float32) + along(grad, bit).astype(jnp.float32)).astype(
            jnp.bfloat16
        )
        bit *= 2
    mate = along(grad, 1)
    weight_grad = jnp.where(
        core == 0, jnp.concatenate([grad, mate]), jnp.concatenate([mate, grad])
    ).astype(jnp.float32) * (1.0 / math.sqrt(size * groups * panels))
    return activations, weight_grad, feature_grad.astype(jnp.bfloat16)


def solution(mesh):
    return jax.shard_map(
        on_device,
        mesh=mesh,
        in_specs=(
            P(BOTH, None),
            P(),
            P(BOTH, None),
            P("rep", "blk", None, None),
            P("rep", "blk", None, None),
            P("rep", "blk", None),
            P("rep", "blk", None, None, None, None),
        ),
        out_specs=(P(BOTH, None), P(), P(BOTH, None)),
        check_vma=False,
    )
```

time: 83.7 us -> 59.8 us (0.71)
  starting transfers between devices: 37.6 us -> 24.9 us
  waiting for transfers between devices: 32.1 us -> 27 us
  Pallas kernels: 7.21 us -> 3.19 us
  local copies, waits for them, and re-layouts: 3.39 us -> 2.12 us
    ppermute x24 -> x25, starting transfers between devices: 37.6 us -> 24.9 us  [the longest x6 9.88 us: move(): return lax.ppermute(array, BOTH, pairs)]
    ppermute x24 -> x25, waiting for transfers between devices: 32.1 us -> 27 us  [the longest x13 17.2 us: along(): return lax.ppermute(array, 'blk', xor_pairs(lax.axis_size('blk'), bit))]
    pallas_call x4, Pallas kernels: 7.21 us -> 3.19 us  [the longest x1 1.23 us: place_tiles(): pl.pallas_call(functools.partial(place_kernel, plan, lax.axis_size('rep')...]
    unnamed x16 -> x13, local copies, waits for them, and re-layouts: 2.54 us -> 2.1 us
  transfers between devices with their start and end apart: 24 -> 25, of which waited for: 12 -> 15; matrix products, arithmetic and copies ran while one was open for 1% -> 3% of each run, Pallas kernels for 1% -> 2%
where the time goes in v2:
time: 59.8 us; the launch traced here: 59.6 us
  waiting for transfers between devices  27 us (45%)
  starting transfers between devices  24.9 us (42%)
  Pallas kernels  3.19 us (5%)
  local copies, waits for them, and re-layouts  2.12 us (4%)
  other arithmetic  1.65 us (3%)
  between operations  0.78 us (1%)
    ppermute x13, waiting for transfers between devices, along(): return lax.ppermute(array, 'blk', xor_pairs(lax.axis_size('blk'), bit))  17.2 us
    ppermute x6, starting transfers between devices, move(): return lax.ppermute(array, BOTH, pairs)  9.88 us
    ppermute x13, starting transfers between devices, along(): return lax.ppermute(array, 'blk', xor_pairs(lax.axis_size('blk'), bit))  8.06 us
    ppermute x6, starting transfers between devices, across(): return lax.ppermute(array, 'rep', xor_pairs(lax.axis_size('rep'), bit))  6.93 us
    ppermute x6, waiting for transfers between devices, across(): return lax.ppermute(array, 'rep', xor_pairs(lax.axis_size('rep'), bit))  5.49 us
    ppermute x6, waiting for transfers between devices, move(): return lax.ppermute(array, BOTH, pairs)  4.35 us
    unnamed x13, local copies, waits for them, and re-layouts  2.1 us
    pallas_call x1, Pallas kernels, place_tiles(): pl.pallas_call(functools.partial(place_kernel, plan, lax.axis_size('rep')...  1.23 us
  transfers between devices with their start and end apart: 25, of which 15 were waited for; matrix products, arithmetic and copies ran while one was open for 3% of the time, Pallas kernels for 2%

profile of v2, /device:TPU:0, one launch (start us, length us, event | category | flops | bytes accessed | tf_op | source)
XLA Modules:
  0.0 59.6 jit_solution(12077268527559486646)
XLA Ops:
  0.6 0.0 copy-start.5
  0.6 0.5 collective-permute-start.3
  1.2 2.6 %collective-permute-start.4 = (bf16[128,256]{1,0:T(8,128)(2,1)}, bf16[128,256]{1,0:T(8,128)(2,1)S(1)}, u32[]{:S(2)}, u32[]{:S(2)}) collective-permute-start(bf16[128,256]{1,0:T(8,128)(2,1)} %param.7), channel_id=1, source_target_pairs={{0,16},{16,0},{1,17},{17,1},{2,18},{18,2},{3,19},{19,3},{4,20},{20... | collective-permute-start | bytes 196616 | tf_op jit(solution)/shard_map/ppermute | solution.py:56
  3.7 2.6 %collective-permute-start.5 = (bf16[128,256]{1,0:T(8,128)(2,1)}, bf16[128,256]{1,0:T(8,128)(2,1)S(1)}, u32[]{:S(2)}, u32[]{:S(2)}) collective-permute-start(bf16[128,256]{1,0:T(8,128)(2,1)} %param.7), channel_id=1, source_target_pairs={{0,8},{1,9},{2,10},{3,11},{4,12},{5,13},{6,14},{7,15},{8,0},{9,1},... | collective-permute-start | bytes 196616 | tf_op jit(solution)/shard_map/ppermute | solution.py:52
  6.3 0.0 copy-done.5
  6.3 0.0 collective-permute-start.2
  6.3 0.5 collective-permute-start.6
  6.9 0.9 %constant_dynamic-update-slice_fusion.1 = bf16[256,256]{1,0:T(8,128)(2,1)S(1)} fusion(bf16[128,256]{1,0:T(8,128)(2,1)} %param.7), kind=kLoop, calls=%fused_computation.18 | loop fusion | bytes 131072
  7.7 0.0 collective-permute-done.2.refs_6_
  7.7 0.0 copy-done.3
  7.7 0.3 collective-permute-start
  8.0 0.9 %collective-permute-done.refs_4_ = s32[4,8]{1,0:T(4,128)S(1)} collective-permute-done((s32[4,8]{1,0:T(4,128)S(1)}, s32[4,8]{1,0:T(4,128)S(1)}, u32[]{:S(2)}, u32[]{:S(2)}) %collective-permute-start) | collective-permute-done | bytes 160 | tf_op jit(solution)/shard_map/ppermute | solution.py:60
  8.9 0.0 copy-done.4
  8.9 0.2 collective-permute-start.1
  9.2 0.9 %collective-permute-done.1.refs_5_ = s32[4,8]{1,0:T(4,128)S(1)} collective-permute-done((s32[4,8]{1,0:T(4,128)S(1)}, s32[4,8]{1,0:T(4,128)S(1)}, u32[]{:S(2)}, u32[]{:S(2)}) %collective-permute-start.1) | collective-permute-done | bytes 160 | tf_op jit(solution)/shard_map/ppermute | solution.py:60
  10.1 0.4 collective-permute-done.5.refs_1_
  10.5 0.5 collective-permute-done.6.refs_1_
  11.0 0.0 collective-permute-done.3.refs_7_
  11.0 0.6 %collective-permute-start.7 = (bf16[128,256]{1,0:T(8,128)(2,1)S(1)}, bf16[128,256]{1,0:T(8,128)(2,1)S(1)}, u32[]{:S(2)}, u32[]{:S(2)}) collective-permute-start(bf16[128,256]{1,0:T(8,128)(2,1)S(1)} %collective-permute-done.5.refs_1_), channel_id=1, source_target_pairs={{0,16},{16,0},{1,17},{17,1},{2,18},{18,2},{3,19},{19,3},{4,20},{20... | collective-permute-start | bytes 196616 | tf_op jit(solution)/shard_map/ppermute | solution.py:56
  11.7 0.0 collective-permute-done.4
  11.7 1.6 %collective-permute-start.8 = (bf16[256,256]{1,0:T(8,128)(2,1)S(1)}, bf16[256,256]{1,0:T(8,128)(2,1)S(1)}, u32[]{:S(2)}, u32[]{:S(2)}) collective-permute-start(bf16[256,256]{1,0:T(8,128)(2,1)S(1)} %constant_dynamic-update-slice_fusion.refs_0_), channel_id=1, source_target_pairs={{0,4},{1,5},{2,6},{3,7},{4,8},{5,9},{6,10},{7,11},{8,12},{9,13},{1... | collective-permute-start | bytes 393224 | tf_op jit(solution)/shard_map/ppermute | solution.py:52
  13.3 1.0 %collective-permute-start.9 = (bf16[256,256]{1,0:T(8,128)(2,1)S(1)}, bf16[256,256]{1,0:T(8,128)(2,1)S(1)}, u32[]{:S(2)}, u32[]{:S(2)}) collective-permute-start(bf16[256,256]{1,0:T(8,128)(2,1)S(1)} %constant_dynamic-update-slice_fusion.refs_0_), channel_id=1, source_target_pairs={{0,6},{1,7},{2,4},{3,5},{4,10},{5,11},{6,8},{7,9},{8,14},{9,15},{1... | collective-permute-start | bytes 393224 | tf_op jit(solution)/shard_map/ppermute | solution.py:52
  14.3 1.0 %collective-permute-done.7.refs_2_ = bf16[128,256]{1,0:T(8,128)(2,1)S(1)} collective-permute-done((bf16[128,256]{1,0:T(8,128)(2,1)S(1)}, bf16[128,256]{1,0:T(8,128)(2,1)S(1)}, u32[]{:S(2)}, u32[]{:S(2)}) %collective-permute-start.7) | collective-permute-done | bytes 65568 | tf_op jit(solution)/shard_map/ppermute | solution.py:56
  15.3 1.6 %collective-permute-start.10 = (bf16[256,256]{1,0:T(8,128)(2,1)S(1)}, bf16[256,256]{1,0:T(8,128)(2,1)S(1)}, u32[]{:S(2)}, u32[]{:S(2)}) collective-permute-start(bf16[256,256]{1,0:T(8,128)(2,1)S(1)} %maximum_select_fusion), channel_id=1, source_target_pairs={{0,2},{1,3},{2,0},{3,1},{4,6},{5,7},{6,4},{7,5},{8,10},{9,11},{10,... | collective-permute-start | bytes 393224 | tf_op jit(solution)/shard_map/ppermute | solution.py:60
  16.9 1.2 %copy-done = bf16[1,1,8,4,128,128]{5,4,3,2,1,0:T(8,128)(2,1)S(1)} copy-done((bf16[1,1,8,4,128,128]{5,4,3,2,1,0:T(8,128)(2,1)S(1)}, bf16[1,1,8,4,128,128]{5,4,3,2,1,0:T(8,128)(2,1)}, u32[]{:S(2)}) %copy-start) | copy-done | bytes 1048600
  18.2 1.2 %place_tiles.1 = (bf16[5,256,256]{2,1,0:T(8,128)(2,1)S(1)}, bf16[5,256,256]{2,1,0:T(8,128)(2,1)S(1)}) custom-call(s32[4,8]{1,0:T(4,128)S(1)} %bitcast.11, s32[4,8]{1,0:T(4,128)S(1)} %bitcast.13, s32[8]{0:T(128)S(1)} %bitcast.15, bf16[8,4,128,128]{3,2,1,0:T(8,128)(2,1)S(1)} %bitcast.9, s32[4,8]{1,0:T(4,128)S(1)} %collective-permute-done.refs_4_, ...), custom_call_target="tpu_custom_call" | custom-call | bytes 2621440 | tf_op jit(solution)/shard_map/place_tiles/pallas_call | solution.py:181
  19.4 0.0 collective-permute-done.8.refs_3_
  19.4 3.3 %collective-permute-done.9.refs_4_ = bf16[256,256]{1,0:T(8,128)(2,1)S(1)} collective-permute-done((bf16[256,256]{1,0:T(8,128)(2,1)S(1)}, bf16[256,256]{1,0:T(8,128)(2,1)S(1)}, u32[]{:S(2)}, u32[]{:S(2)}) %collective-permute-start.9) | collective-permute-done | bytes 131104 | tf_op jit(solution)/shard_map/ppermute | solution.py:52
  22.8 0.4 collective-permute-done.10.refs_5_
  23.1 0.5 forward_product.1
  23.6 0.1 collective-permute-start.11
  23.7 1.3 %collective-permute-done.11 = bf16[256,256]{1,0:T(8,128)(2,1)S(1)} collective-permute-done((bf16[256,256]{1,0:T(8,128)(2,1)S(1)}, bf16[256,256]{1,0:T(8,128)(2,1)S(1)}, u32[]{:S(2)}, u32[]{:S(2)}) %collective-permute-start.11) | collective-permute-done | bytes 131104 | tf_op jit(solution)/shard_map/ppermute | solution.py:60
  25.1 1.6 %collective-permute-start.12 = (bf16[256,256]{1,0:T(8,128)(2,1)S(1)}, bf16[256,256]{1,0:T(8,128)(2,1)S(1)}, u32[]{:S(2)}, u32[]{:S(2)}) collective-permute-start(bf16[256,256]{1,0:T(8,128)(2,1)S(1)} %add_convert_fusion.first), channel_id=1, source_target_pairs={{0,16},{16,0},{1,17},{17,1},{2,18},{18,2},{3,19},{19,3},{4,20},{20... | collective-permute-start | bytes 393224 | tf_op jit(solution)/shard_map/ppermute | solution.py:56
  26.7 4.0 %collective-permute-done.12.second = bf16[256,256]{1,0:T(8,128)(2,1)S(1)} collective-permute-done((bf16[256,256]{1,0:T(8,128)(2,1)S(1)}, bf16[256,256]{1,0:T(8,128)(2,1)S(1)}, u32[]{:S(2)}, u32[]{:S(2)}) %collective-permute-start.12) | collective-permute-done | bytes 131104 | tf_op jit(solution)/shard_map/ppermute | solution.py:56
  30.7 0.0 copy-done.2
  30.7 0.9 %layer.1 = (bf16[128,256]{1,0:T(8,128)(2,1)}, bf16[128,256]{1,0:T(8,128)(2,1)S(1)}, bf16[128,256]{1,0:T(8,128)(2,1)S(1)}, bf16[256,256]{1,0:T(8,128)(2,1)S(1)}) custom-call(bf16[256,256]{1,0:T(8,128)(2,1)S(1)} %add_convert_fusion.first, bf16[256,256]{1,0:T(8,128)(2,1)S(1)} %collective-permute-done.12.second, bf16[256,256]{1,0:T(8,128)(2,1)S(1)} %copy-done.1, ...), custom_call_target="tpu_custom_call" | custom-call | flops 100663296 | bytes 524288 | tf_op jit(solution)/shard_map/layer/pallas_call | solution.py:263
  31.6 0.0 collective-permute-start.13
  31.6 1.3 %collective-permute-done.13.sib_rows = bf16[256,256]{1,0:T(8,128)(2,1)S(1)} collective-permute-done((bf16[256,256]{1,0:T(8,128)(2,1)S(1)}, bf16[256,256]{1,0:T(8,128)(2,1)S(1)}, u32[]{:S(2)}, u32[]{:S(2)}) %collective-permute-start.13) | collective-permute-done | bytes 131104 | tf_op jit(solution)/shard_map/ppermute | solution.py:60
  32.9 0.6 backward_product.1
  33.5 0.2 collective-permute-start.14
  33.7 1.3 %collective-permute-start.15 = (bf16[256,256]{1,0:T(8,128)(2,1)S(1)}, bf16[256,256]{1,0:T(8,128)(2,1)S(1)}, u32[]{:S(2)}, u32[]{:S(2)}) collective-permute-start(bf16[256,256]{1,0:T(8,128)(2,1)S(1)} %get-tuple-element.31), channel_id=1, source_target_pairs={{0,2},{1,3},{2,0},{3,1},{4,6},{5,7},{6,4},{7,5},{8,10},{9,11},{10,... | collective-permute-start | bytes 393224 | tf_op jit(solution)/shard_map/ppermute | solution.py:60
  35.0 2.5 %collective-permute-start.21 = (bf16[256,256]{1,0:T(8,128)(2,1)S(1)}, bf16[256,256]{1,0:T(8,128)(2,1)S(1)}, u32[]{:S(2)}, u32[]{:S(2)}) collective-permute-start(bf16[256,256]{1,0:T(8,128)(2,1)S(1)} %get-tuple-element.36), channel_id=1, source_target_pairs={{6,0},{7,1},{4,2},{5,3},{10,4},{11,5},{8,6},{9,7},{14,8},{15,9},{1... | collective-permute-start | bytes 393224 | tf_op jit(solution)/shard_map/ppermute | solution.py:52
  37.5 0.6 %collective-permute-start.20 = (bf16[256,256]{1,0:T(8,128)(2,1)S(1)}, bf16[256,256]{1,0:T(8,128)(2,1)S(1)}, u32[]{:S(2)}, u32[]{:S(2)}) collective-permute-start(bf16[256,256]{1,0:T(8,128)(2,1)S(1)} %get-tuple-element.35), channel_id=1, source_target_pairs={{4,0},{5,1},{6,2},{7,3},{8,4},{9,5},{10,6},{11,7},{12,8},{13,9},{1... | collective-permute-start | bytes 393224 | tf_op jit(solution)/shard_map/ppermute | solution.py:52
  38.1 0.0 collective-permute-done.14
  38.1 4.2 %collective-permute-done.15 = bf16[256,256]{1,0:T(8,128)(2,1)S(1)} collective-permute-done((bf16[256,256]{1,0:T(8,128)(2,1)S(1)}, bf16[256,256]{1,0:T(8,128)(2,1)S(1)}, u32[]{:S(2)}, u32[]{:S(2)}) %collective-permute-start.15) | collective-permute-done | bytes 131104 | tf_op jit(solution)/shard_map/ppermute | solution.py:60
  42.3 1.3 %collective-permute-start.16 = (bf16[128,256]{1,0:T(8,128)(2,1)S(1)}, bf16[128,256]{1,0:T(8,128)(2,1)S(1)}, u32[]{:S(2)}, u32[]{:S(2)}) collective-permute-start(bf16[128,256]{1,0:T(8,128)(2,1)S(1)} %add_convert_fusion.4), channel_id=1, source_target_pairs={{0,2},{1,3},{2,0},{3,1},{4,6},{5,7},{6,4},{7,5},{8,10},{9,11},{10,... | collective-permute-start | bytes 196616 | tf_op jit(solution)/shard_map/ppermute | solution.py:60
  43.6 0.1 collective-permute-start.23
  43.7 2.9 %collective-permute-done.16 = bf16[128,256]{1,0:T(8,128)(2,1)S(1)} collective-permute-done((bf16[128,256]{1,0:T(8,128)(2,1)S(1)}, bf16[128,256]{1,0:T(8,128)(2,1)S(1)}, u32[]{:S(2)}, u32[]{:S(2)}) %collective-permute-start.16) | collective-permute-done | bytes 65568 | tf_op jit(solution)/shard_map/ppermute | solution.py:60
  46.6 1.0 %collective-permute-start.17 = (bf16[128,256]{1,0:T(8,128)(2,1)S(1)}, bf16[128,256]{1,0:T(8,128)(2,1)S(1)}, u32[]{:S(2)}, u32[]{:S(2)}) collective-permute-start(bf16[128,256]{1,0:T(8,128)(2,1)S(1)} %add_convert_fusion.3), channel_id=1, source_target_pairs={{0,4},{1,5},{2,6},{3,7},{4,0},{5,1},{6,2},{7,3},{8,12},{9,13},{10,... | collective-permute-start | bytes 196616 | tf_op jit(solution)/shard_map/ppermute | solution.py:60
  47.6 0.0 collective-permute-done.21
  47.6 0.0 collective-permute-done.20
  47.6 0.1 convert_add_fusion
  47.7 1.5 %collective-permute-start.22 = (bf16[128,256]{1,0:T(8,128)(2,1)S(1)}, bf16[128,256]{1,0:T(8,128)(2,1)S(1)}, u32[]{:S(2)}, u32[]{:S(2)}) collective-permute-start(bf16[128,256]{1,0:T(8,128)(2,1)S(1)} %slice.32), channel_id=1, source_target_pairs={{0,16},{16,0},{1,17},{17,1},{2,18},{18,2},{3,19},{19,3},{4,20},{20... | collective-permute-start | bytes 196616 | tf_op jit(solution)/shard_map/ppermute | solution.py:56
  49.2 1.7 %collective-permute-done.17 = bf16[128,256]{1,0:T(8,128)(2,1)S(1)} collective-permute-done((bf16[128,256]{1,0:T(8,128)(2,1)S(1)}, bf16[128,256]{1,0:T(8,128)(2,1)S(1)}, u32[]{:S(2)}, u32[]{:S(2)}) %collective-permute-start.17) | collective-permute-done | bytes 65568 | tf_op jit(solution)/shard_map/ppermute | solution.py:60
  50.9 1.5 %collective-permute-start.18 = (bf16[128,256]{1,0:T(8,128)(2,1)S(1)}, bf16[128,256]{1,0:T(8,128)(2,1)S(1)}, u32[]{:S(2)}, u32[]{:S(2)}) collective-permute-start(bf16[128,256]{1,0:T(8,128)(2,1)S(1)} %add_convert_fusion.2), channel_id=1, source_target_pairs={{0,8},{1,9},{2,10},{3,11},{4,12},{5,13},{6,14},{7,15},{8,0},{9,1},... | collective-permute-start | bytes 196616 | tf_op jit(solution)/shard_map/ppermute | solution.py:60
  52.4 0.0 collective-permute-done.23
  52.4 1.6 %collective-permute-start.24 = (bf16[128,256]{1,0:T(8,128)(2,1)S(1)}, bf16[128,256]{1,0:T(8,128)(2,1)S(1)}, u32[]{:S(2)}, u32[]{:S(2)}) collective-permute-start(bf16[128,256]{1,0:T(8,128)(2,1)S(1)} %fusion), channel_id=1, source_target_pairs={{8,0},{9,1},{10,2},{11,3},{12,4},{13,5},{14,6},{15,7},{0,8},{1,9},... | collective-permute-start | bytes 196616 | tf_op jit(solution)/shard_map/ppermute | solution.py:52
  54.0 3.6 %collective-permute-done.18 = bf16[128,256]{1,0:T(8,128)(2,1)S(1)} collective-permute-done((bf16[128,256]{1,0:T(8,128)(2,1)S(1)}, bf16[128,256]{1,0:T(8,128)(2,1)S(1)}, u32[]{:S(2)}, u32[]{:S(2)}) %collective-permute-start.18) | collective-permute-done | bytes 65568 | tf_op jit(solution)/shard_map/ppermute | solution.py:60
  57.6 0.1 collective-permute-start.19
  57.7 0.0 collective-permute-done.22
  57.7 0.6 collective-permute-done.24
  58.3 0.7 %fusion.2 = bf16[128,256]{1,0:T(8,128)(2,1)} fusion(f32[256,256]{1,0:T(8,128)S(1)} %convert_add_fusion, bf16[128,256]{1,0:T(8,128)(2,1)S(1)} %collective-permute-done.24, bf16[128,256]{1,0:T(8,128)(2,1)S(1)} %collective-permute-done.22), kind=kLoop, calls=%fused_computation.9 | loop fusion | flops 163840 | bytes 327680 | tf_op jit(solution)/shard_map/convert_element_type | solution.py:354
  58.9 0.0 collective-permute-done.19
  58.9 0.7 %convert_multiply_fusion = f32[256,256]{1,0:T(8,128)} fusion(bf16[128,256]{1,0:T(8,128)(2,1)S(1)} %collective-permute-done.19, bf16[128,256]{1,0:T(8,128)(2,1)S(1)} %add_convert_fusion.1, pred[]{:T(512)S(6)} %eq.12), kind=kLoop, calls=%fused_computation.2 | loop fusion | flops 720896 | bytes 393217 | tf_op jit(solution)/shard_map/mul | solution.py:351
  (17 shorter events, 0.2 us)
Async XLA Ops:
  0.6 5.7 %copy-start.5 = (s32[1,1,8]{2,1,0:T(1,128)S(1)}, s32[1,1,8]{2,1,0:T(1,128)}, u32[]{:S(2)}) copy-start(s32[1,1,8]{2,1,0:T(1,128)} %param.12) | copy-start | bytes 100
  0.6 10.4 %collective-permute-start.3 = (bf16[8,4,128,128]{3,2,1,0:T(8,128)(2,1)}, bf16[8,4,128,128]{3,2,1,0:T(8,128)(2,1)S(1)}, u32[]{:S(2)}, u32[]{:S(2)}) collective-permute-start(bf16[8,4,128,128]{3,2,1,0:T(8,128)(2,1)} %bitcast.8), channel_id=1, source_target_pairs={{0,1},{1,0},{2,3},{3,2},{4,5},{5,4},{6,7},{7,6},{8,9},{9,8},{10,11... | collective-permute-start | bytes 3145736 | tf_op jit(solution)/shard_map/ppermute | solution.py:60
  1.2 10.5 %collective-permute-start.4 = (bf16[128,256]{1,0:T(8,128)(2,1)}, bf16[128,256]{1,0:T(8,128)(2,1)S(1)}, u32[]{:S(2)}, u32[]{:S(2)}) collective-permute-start(bf16[128,256]{1,0:T(8,128)(2,1)} %param.7), channel_id=1, source_target_pairs={{0,16},{16,0},{1,17},{17,1},{2,18},{18,2},{3,19},{19,3},{4,20},{20... | collective-permute-start | bytes 196616 | tf_op jit(solution)/shard_map/ppermute | solution.py:56
  3.7 6.8 %collective-permute-start.5 = (bf16[128,256]{1,0:T(8,128)(2,1)}, bf16[128,256]{1,0:T(8,128)(2,1)S(1)}, u32[]{:S(2)}, u32[]{:S(2)}) collective-permute-start(bf16[128,256]{1,0:T(8,128)(2,1)} %param.7), channel_id=1, source_target_pairs={{0,8},{1,9},{2,10},{3,11},{4,12},{5,13},{6,14},{7,15},{8,0},{9,1},... | collective-permute-start | bytes 196616 | tf_op jit(solution)/shard_map/ppermute | solution.py:52
  6.3 1.4 %collective-permute-start.2 = (s32[8]{0:T(128)S(1)}, s32[8]{0:T(128)S(1)}, u32[]{:S(2)}, u32[]{:S(2)}) collective-permute-start(s32[8]{0:T(128)S(1)} %bitcast.14), channel_id=1, source_target_pairs={{0,1},{1,0},{2,3},{3,2},{4,5},{5,4},{6,7},{7,6},{8,9},{9,8},{10,11... | collective-permute-start | bytes 104 | tf_op jit(solution)/shard_map/ppermute | solution.py:60
  6.3 4.7 %collective-permute-start.6 = (bf16[128,256]{1,0:T(8,128)(2,1)}, bf16[128,256]{1,0:T(8,128)(2,1)S(1)}, u32[]{:S(2)}, u32[]{:S(2)}) collective-permute-start(bf16[128,256]{1,0:T(8,128)(2,1)} %refs_0_.1), channel_id=1, source_target_pairs={{0,16},{16,0},{1,17},{17,1},{2,18},{18,2},{3,19},{19,3},{4,20},{20... | collective-permute-start | bytes 196616 | tf_op jit(solution)/shard_map/ppermute | solution.py:56
  6.9 0.9 %copy-start.3 = (s32[1,1,8,4]{2,3,1,0:T(4,128)S(1)}, s32[1,1,8,4]{2,3,1,0:T(4,128)}, u32[]{:S(2)}) copy-start(s32[1,1,8,4]{2,3,1,0:T(4,128)} %param.10) | copy-start | bytes 388
  7.7 1.2 %collective-permute-start = (s32[4,8]{1,0:T(4,128)S(1)}, s32[4,8]{1,0:T(4,128)S(1)}, u32[]{:S(2)}, u32[]{:S(2)}) collective-permute-start(s32[4,8]{1,0:T(4,128)S(1)} %bitcast.10), channel_id=1, source_target_pairs={{0,1},{1,0},{2,3},{3,2},{4,5},{5,4},{6,7},{7,6},{8,9},{9,8},{10,11... | collective-permute-start | bytes 392 | tf_op jit(solution)/shard_map/ppermute | solution.py:60
  8.0 0.9 %copy-start.4 = (s32[1,1,8,4]{2,3,1,0:T(4,128)S(1)}, s32[1,1,8,4]{2,3,1,0:T(4,128)}, u32[]{:S(2)}) copy-start(s32[1,1,8,4]{2,3,1,0:T(4,128)} %param.11) | copy-start | bytes 388
  8.9 1.2 %collective-permute-start.1 = (s32[4,8]{1,0:T(4,128)S(1)}, s32[4,8]{1,0:T(4,128)S(1)}, u32[]{:S(2)}, u32[]{:S(2)}) collective-permute-start(s32[4,8]{1,0:T(4,128)S(1)} %bitcast.12), channel_id=1, source_target_pairs={{0,1},{1,0},{2,3},{3,2},{4,5},{5,4},{6,7},{7,6},{8,9},{9,8},{10,11... | collective-permute-start | bytes 392 | tf_op jit(solution)/shard_map/ppermute | solution.py:60
  11.0 4.3 %collective-permute-start.7 = (bf16[128,256]{1,0:T(8,128)(2,1)S(1)}, bf16[128,256]{1,0:T(8,128)(2,1)S(1)}, u32[]{:S(2)}, u32[]{:S(2)}) collective-permute-start(bf16[128,256]{1,0:T(8,128)(2,1)S(1)} %collective-permute-done.5.refs_1_), channel_id=1, source_target_pairs={{0,16},{16,0},{1,17},{17,1},{2,18},{18,2},{3,19},{19,3},{4,20},{20... | collective-permute-start | bytes 196616 | tf_op jit(solution)/shard_map/ppermute | solution.py:56
  11.7 7.7 %collective-permute-start.8 = (bf16[256,256]{1,0:T(8,128)(2,1)S(1)}, bf16[256,256]{1,0:T(8,128)(2,1)S(1)}, u32[]{:S(2)}, u32[]{:S(2)}) collective-permute-start(bf16[256,256]{1,0:T(8,128)(2,1)S(1)} %constant_dynamic-update-slice_fusion.refs_0_), channel_id=1, source_target_pairs={{0,4},{1,5},{2,6},{3,7},{4,8},{5,9},{6,10},{7,11},{8,12},{9,13},{1... | collective-permute-start | bytes 393224 | tf_op jit(solution)/shard_map/ppermute | solution.py:52
  13.3 9.4 %collective-permute-start.9 = (bf16[256,256]{1,0:T(8,128)(2,1)S(1)}, bf16[256,256]{1,0:T(8,128)(2,1)S(1)}, u32[]{:S(2)}, u32[]{:S(2)}) collective-permute-start(bf16[256,256]{1,0:T(8,128)(2,1)S(1)} %constant_dynamic-update-slice_fusion.refs_0_), channel_id=1, source_target_pairs={{0,6},{1,7},{2,4},{3,5},{4,10},{5,11},{6,8},{7,9},{8,14},{9,15},{1... | collective-permute-start | bytes 393224 | tf_op jit(solution)/shard_map/ppermute | solution.py:52
  15.3 7.8 %collective-permute-start.10 = (bf16[256,256]{1,0:T(8,128)(2,1)S(1)}, bf16[256,256]{1,0:T(8,128)(2,1)S(1)}, u32[]{:S(2)}, u32[]{:S(2)}) collective-permute-start(bf16[256,256]{1,0:T(8,128)(2,1)S(1)} %maximum_select_fusion), channel_id=1, source_target_pairs={{0,2},{1,3},{2,0},{3,1},{4,6},{5,7},{6,4},{7,5},{8,10},{9,11},{10,... | collective-permute-start | bytes 393224 | tf_op jit(solution)/shard_map/ppermute | solution.py:60
  16.9 1.2 %copy-start = (bf16[1,1,8,4,128,128]{5,4,3,2,1,0:T(8,128)(2,1)S(1)}, bf16[1,1,8,4,128,128]{5,4,3,2,1,0:T(8,128)(2,1)}, u32[]{:S(2)}) copy-start(bf16[1,1,8,4,128,128]{5,4,3,2,1,0:T(8,128)(2,1)} %param.13) | copy-start | bytes 3145732
  23.6 1.4 %collective-permute-start.11 = (bf16[256,256]{1,0:T(8,128)(2,1)S(1)}, bf16[256,256]{1,0:T(8,128)(2,1)S(1)}, u32[]{:S(2)}, u32[]{:S(2)}) collective-permute-start(bf16[256,256]{1,0:T(8,128)(2,1)S(1)} %get-tuple-element.24), channel_id=1, source_target_pairs={{0,1},{1,0},{2,3},{3,2},{4,5},{5,4},{6,7},{7,6},{8,9},{9,8},{10,11... | collective-permute-start | bytes 393224 | tf_op jit(solution)/shard_map/ppermute | solution.py:60
  25.0 5.7 %copy-start.1 = (bf16[256,256]{1,0:T(8,128)(2,1)S(1)}, bf16[256,256]{1,0:T(8,128)(2,1)}, u32[]{:S(2)}) copy-start(bf16[256,256]{1,0:T(8,128)(2,1)} %weight.1) | copy-start | bytes 393220
  25.0 5.7 %copy-start.2 = (bf16[128,256]{1,0:T(8,128)(2,1)S(1)}, bf16[128,256]{1,0:T(8,128)(2,1)}, u32[]{:S(2)}) copy-start(bf16[128,256]{1,0:T(8,128)(2,1)} %refs_0_.1) | copy-start | bytes 196612
  25.1 5.6 %collective-permute-start.12 = (bf16[256,256]{1,0:T(8,128)(2,1)S(1)}, bf16[256,256]{1,0:T(8,128)(2,1)S(1)}, u32[]{:S(2)}, u32[]{:S(2)}) collective-permute-start(bf16[256,256]{1,0:T(8,128)(2,1)S(1)} %add_convert_fusion.first), channel_id=1, source_target_pairs={{0,16},{16,0},{1,17},{17,1},{2,18},{18,2},{3,19},{19,3},{4,20},{20... | collective-permute-start | bytes 393224 | tf_op jit(solution)/shard_map/ppermute | solution.py:56
  31.6 1.3 %collective-permute-start.13 = (bf16[256,256]{1,0:T(8,128)(2,1)S(1)}, bf16[256,256]{1,0:T(8,128)(2,1)S(1)}, u32[]{:S(2)}, u32[]{:S(2)}) collective-permute-start(bf16[256,256]{1,0:T(8,128)(2,1)S(1)} %get-tuple-element.28.own_rows), channel_id=1, source_target_pairs={{0,1},{1,0},{2,3},{3,2},{4,5},{5,4},{6,7},{7,6},{8,9},{9,8},{10,11... | collective-permute-start | bytes 393224 | tf_op jit(solution)/shard_map/ppermute | solution.py:60
  33.5 4.6 %collective-permute-start.14 = (bf16[128,256]{1,0:T(8,128)(2,1)S(1)}, bf16[128,256]{1,0:T(8,128)(2,1)S(1)}, u32[]{:S(2)}, u32[]{:S(2)}) collective-permute-start(bf16[128,256]{1,0:T(8,128)(2,1)S(1)} %get-tuple-element.30), channel_id=1, source_target_pairs={{0,1},{1,0},{2,3},{3,2},{4,5},{5,4},{6,7},{7,6},{8,9},{9,8},{10,11... | collective-permute-start | bytes 196616 | tf_op jit(solution)/shard_map/ppermute | solution.py:60
  33.7 8.6 %collective-permute-start.15 = (bf16[256,256]{1,0:T(8,128)(2,1)S(1)}, bf16[256,256]{1,0:T(8,128)(2,1)S(1)}, u32[]{:S(2)}, u32[]{:S(2)}) collective-permute-start(bf16[256,256]{1,0:T(8,128)(2,1)S(1)} %get-tuple-element.31), channel_id=1, source_target_pairs={{0,2},{1,3},{2,0},{3,1},{4,6},{5,7},{6,4},{7,5},{8,10},{9,11},{10,... | collective-permute-start | bytes 393224 | tf_op jit(solution)/shard_map/ppermute | solution.py:60
  35.0 12.6 %collective-permute-start.21 = (bf16[256,256]{1,0:T(8,128)(2,1)S(1)}, bf16[256,256]{1,0:T(8,128)(2,1)S(1)}, u32[]{:S(2)}, u32[]{:S(2)}) collective-permute-start(bf16[256,256]{1,0:T(8,128)(2,1)S(1)} %get-tuple-element.36), channel_id=1, source_target_pairs={{6,0},{7,1},{4,2},{5,3},{10,4},{11,5},{8,6},{9,7},{14,8},{15,9},{1... | collective-permute-start | bytes 393224 | tf_op jit(solution)/shard_map/ppermute | solution.py:52
  37.5 10.2 %collective-permute-start.20 = (bf16[256,256]{1,0:T(8,128)(2,1)S(1)}, bf16[256,256]{1,0:T(8,128)(2,1)S(1)}, u32[]{:S(2)}, u32[]{:S(2)}) collective-permute-start(bf16[256,256]{1,0:T(8,128)(2,1)S(1)} %get-tuple-element.35), channel_id=1, source_target_pairs={{4,0},{5,1},{6,2},{7,3},{8,4},{9,5},{10,6},{11,7},{12,8},{13,9},{1... | collective-permute-start | bytes 393224 | tf_op jit(solution)/shard_map/ppermute | solution.py:52
  42.3 4.3 %collective-permute-start.16 = (bf16[128,256]{1,0:T(8,128)(2,1)S(1)}, bf16[128,256]{1,0:T(8,128)(2,1)S(1)}, u32[]{:S(2)}, u32[]{:S(2)}) collective-permute-start(bf16[128,256]{1,0:T(8,128)(2,1)S(1)} %add_convert_fusion.4), channel_id=1, source_target_pairs={{0,2},{1,3},{2,0},{3,1},{4,6},{5,7},{6,4},{7,5},{8,10},{9,11},{10,... | collective-permute-start | bytes 196616 | tf_op jit(solution)/shard_map/ppermute | solution.py:60
  43.6 8.8 %collective-permute-start.23 = (bf16[128,256]{1,0:T(8,128)(2,1)S(1)}, bf16[128,256]{1,0:T(8,128)(2,1)S(1)}, u32[]{:S(2)}, u32[]{:S(2)}) collective-permute-start(bf16[128,256]{1,0:T(8,128)(2,1)S(1)} %slice.33), channel_id=1, source_target_pairs={{0,16},{16,0},{1,17},{17,1},{2,18},{18,2},{3,19},{19,3},{4,20},{20... | collective-permute-start | bytes 196616 | tf_op jit(solution)/shard_map/ppermute | solution.py:56
  46.6 4.3 %collective-permute-start.17 = (bf16[128,256]{1,0:T(8,128)(2,1)S(1)}, bf16[128,256]{1,0:T(8,128)(2,1)S(1)}, u32[]{:S(2)}, u32[]{:S(2)}) collective-permute-start(bf16[128,256]{1,0:T(8,128)(2,1)S(1)} %add_convert_fusion.3), channel_id=1, source_target_pairs={{0,4},{1,5},{2,6},{3,7},{4,0},{5,1},{6,2},{7,3},{8,12},{9,13},{10,... | collective-permute-start | bytes 196616 | tf_op jit(solution)/shard_map/ppermute | solution.py:60
  47.7 10.0 %collective-permute-start.22 = (bf16[128,256]{1,0:T(8,128)(2,1)S(1)}, bf16[128,256]{1,0:T(8,128)(2,1)S(1)}, u32[]{:S(2)}, u32[]{:S(2)}) collective-permute-start(bf16[128,256]{1,0:T(8,128)(2,1)S(1)} %slice.32), channel_id=1, source_target_pairs={{0,16},{16,0},{1,17},{17,1},{2,18},{18,2},{3,19},{19,3},{4,20},{20... | collective-permute-start | bytes 196616 | tf_op jit(solution)/shard_map/ppermute | solution.py:56
  50.9 6.6 %collective-permute-start.18 = (bf16[128,256]{1,0:T(8,128)(2,1)S(1)}, bf16[128,256]{1,0:T(8,128)(2,1)S(1)}, u32[]{:S(2)}, u32[]{:S(2)}) collective-permute-start(bf16[128,256]{1,0:T(8,128)(2,1)S(1)} %add_convert_fusion.2), channel_id=1, source_target_pairs={{0,8},{1,9},{2,10},{3,11},{4,12},{5,13},{6,14},{7,15},{8,0},{9,1},... | collective-permute-start | bytes 196616 | tf_op jit(solution)/shard_map/ppermute | solution.py:60
  52.4 5.8 %collective-permute-start.24 = (bf16[128,256]{1,0:T(8,128)(2,1)S(1)}, bf16[128,256]{1,0:T(8,128)(2,1)S(1)}, u32[]{:S(2)}, u32[]{:S(2)}) collective-permute-start(bf16[128,256]{1,0:T(8,128)(2,1)S(1)} %fusion), channel_id=1, source_target_pairs={{8,0},{9,1},{10,2},{11,3},{12,4},{13,5},{14,6},{15,7},{0,8},{1,9},... | collective-permute-start | bytes 196616 | tf_op jit(solution)/shard_map/ppermute | solution.py:52
  57.6 1.3 %collective-permute-start.19 = (bf16[128,256]{1,0:T(8,128)(2,1)S(1)}, bf16[128,256]{1,0:T(8,128)(2,1)S(1)}, u32[]{:S(2)}, u32[]{:S(2)}) collective-permute-start(bf16[128,256]{1,0:T(8,128)(2,1)S(1)} %add_convert_fusion.1), channel_id=1, source_target_pairs={{0,1},{1,0},{2,3},{3,2},{4,5},{5,4},{6,7},{7,6},{8,9},{9,8},{10,11... | collective-permute-start | bytes 196616 | tf_op jit(solution)/shard_map/ppermute | solution.py:60

commit v3 on v2

--- a/solution.py
+++ b/solution.py
@@ -33,6 +33,10 @@
 
 def after(value, *others):
     return lax.optimization_barrier((value,) + others)[0]
+
+
+def add_rounded(a, b):
+    return (a.astype(jnp.float32) + b.astype(jnp.float32)).astype(a.dtype)
 
 
 def pairs_of(groups, panels, target, members=None, odd_only=False):
@@ -73,6 +77,8 @@
             for k in range(1, steps // 2)
         ]
 
+        self.batches = [list(range(1 + len(self.moves)))]
+
     def shifts(self, member, panel):
         steps, groups = self.steps, self.groups
         return [
@@ -88,7 +94,7 @@
     def part_types(self):
         return [jnp.float32] + [jnp.bfloat16] * len(self.moves)
 
-    def scatter(self, parts, size):
+    def scatter(self, parts, grad, size):
         column = parts[0]
         for pairs, part in zip(self.moves, parts[1:]):
             column = column + move(part, back(pairs)).astype(jnp.float32)
@@ -96,7 +102,70 @@
         for i in range(1, self.groups):
             piece = column[i * size : (i + 1) * size].astype(jnp.bfloat16)
             total = total + across(piece, i).astype(jnp.float32)
-        return total, column
+        bit = 2
+        while bit < lax.axis_size("blk"):
+            grad = add_rounded(grad, along(grad, bit))
+            bit *= 2
+        return total, grad
+
+
+def column_kernel(own, came, ahead, cross, keep_out, pass_out):
+    size = keep_out.shape[0]
+    kept = (lax.axis_index("blk") // 2) % 2 == lax.axis_index("rep")
+    mine = jnp.where(kept, 1.0, 0.0)
+    total = own[...] + mine * came[...].astype(jnp.float32)
+    total = total + (ahead[...].astype(jnp.float32) + cross[...].astype(jnp.float32))
+    keep_out[...] = total[:size]
+    pass_out[...] = total[size:].astype(pass_out.dtype)
+
+
+def add_column(own, came, ahead, cross, size):
+    span, width = own.shape
+    return pl.pallas_call(
+        column_kernel,
+        out_shape=[like((size, width), jnp.float32), like((span - size, width), jnp.bfloat16)],
+        compiler_params=pltpu.CompilerParams(vmem_limit_bytes=limit_for(own, came, ahead, cross)),
+        cost_estimate=pl.CostEstimate(
+            flops=3 * span * width, bytes_accessed=8 * span * width, transcendentals=0
+        ),
+        name="add_column",
+    )(own, came, ahead, cross)
+
+
+def finish_kernel(first, second, third, out):
+    total = first[...] + second[...].astype(jnp.float32) + third[...].astype(jnp.float32)
+    out[...] = total.astype(out.dtype)
+
+
+def finish(first, second, third):
+    return pl.pallas_call(
+        finish_kernel,
+        out_shape=like(first.shape, second.dtype),
+        compiler_params=pltpu.CompilerParams(vmem_limit_bytes=limit_for(first, second, third)),
+        cost_estimate=pl.CostEstimate(
+            flops=2 * first.size, bytes_accessed=8 * first.size, transcendentals=0
+        ),
+        name="finish",
+    )(first, second, third)
+
+
+def stack_kernel(first, second, out):
+    size = first.shape[0]
+    out[:size, :] = first[...]
+    out[size:, :] = second[...]
+
+
+def stack(first, second):
+    size, width = first.shape
+    return pl.pallas_call(
+        stack_kernel,
+        out_shape=like((2 * size, width), first.dtype),
+        compiler_params=pltpu.CompilerParams(vmem_limit_bytes=limit_for(first, second)),
+        cost_estimate=pl.CostEstimate(
+            flops=0, bytes_accessed=8 * size * width, transcendentals=0
+        ),
+        name="stack",
+    )(first, second)
 
 
 class Halves:
@@ -104,7 +173,10 @@
         self.panels = panels
         self.ahead = pairs_of(groups, panels, lambda m, p: p + 4 * (1 - 2 * m))
         self.cross = pairs_of(groups, panels, lambda m, p: (p ^ 2) + 4 * (1 - 2 * m))
+        self.corner = [(a, b ^ panels) for a, b in pairs_of(groups, panels, lambda m, p: p ^ 2)]
         self.half = pairs_of(groups, panels, lambda m, p: p + panels // 2)
+
+        self.batches = [[0, 2, 3], [1, 4]]
 
     @staticmethod
     def fits(groups, panels):
@@ -123,64 +195,67 @@
     def gather(self, slab, early, placed):
         mate = across(slab, 1)
         far = after(move(slab, self.half), *early)
-        both = jnp.concatenate([slab, mate])
+        both = stack(slab, mate)
         ahead = move(both, self.ahead)
         cross = move(both, self.cross)
-        far_mate = across(far, 1)
-        last = jnp.where(self.sends_own(), both, jnp.concatenate([far, far_mate]))
-        last = along(last, 2)
-        return [[both], [far, far_mate], [ahead], [cross], [last]]
+        own = self.sends_own()
+        last = along(jnp.where(own, slab, far), 2)
+        last_mate = move(jnp.where(own, far, slab), self.corner)
+        return [[both], [far, across(far, 1)], [ahead], [cross], [last, last_mate]]
 
     def part_types(self):
         return [jnp.float32, jnp.float32, jnp.bfloat16, jnp.bfloat16, jnp.bfloat16]
 
-    def scatter(self, parts, size):
+    def scatter(self, parts, grad, size):
         own, far, ahead, cross, last = parts
+        ahead = move(ahead, back(self.ahead))
         came = along(last, 2)
-        ahead = move(ahead, back(self.ahead))
-        cross = move(cross, back(self.cross))
+        grad = add_rounded(grad, after(along(grad, 2), came))
         kept = self.sends_own()
         far = far + jnp.where(kept, 0.0, came.astype(jnp.float32))
         far_pass = far[size:].astype(jnp.bfloat16)
-        far_sum = far[:size] + across(far_pass, 1).astype(jnp.float32)
-        far_back = move(far_sum.astype(jnp.bfloat16), back(self.half))
-        column = own + jnp.where(kept, after(came, far_pass).astype(jnp.float32), 0.0)
-        column = column + ahead.astype(jnp.float32) + cross.astype(jnp.float32)
-        mate = across(column[size:].astype(jnp.bfloat16), 1).astype(jnp.float32)
-        return column[:size] + mate + far_back.astype(jnp.float32), came
+        far_mate = across(after(far_pass, ahead), 1)
+        cross = move(cross, back(self.cross))
+        grad = add_rounded(grad, after(along(grad, 4), far_mate))
+        far_sum = (far[:size] + far_mate.astype(jnp.float32)).astype(jnp.bfloat16)
+        far_back = move(far_sum, back(self.half))
+        column, column_pass = add_column(own, came, ahead, cross, size)
+        mate = across(column_pass, 1)
+        grad = add_rounded(grad, after(along(grad, 8), mate, far_back))
+        return finish(column, mate, far_back), grad
 
 
 def place_kernel(plan, groups, panels, *refs):
     member, panel = lax.axis_index("rep"), lax.axis_index("blk")
     shifts = plan.shifts(member, panel)
     offsets = (0, 1 - 2 * (panel % 2))
-    for offset, (rows, cols, counts, tiles), out in zip(offsets, (refs[:4], refs[4:8]), refs[8:]):
+    for offset, (meta, tiles), out in zip(offsets, (refs[:2], refs[2:4]), refs[4:]):
         steps, cap, size, _ = tiles.shape
         for slot, (shift, had) in enumerate(shifts):
             step = lax.rem(shift - steps * member + offset + 4 * panels, panels)
             live = step < steps if had is True else (step < steps) & had
             there = jnp.where(live, step, 0)
-            count = jnp.where(live, counts[there], 0)
+            count = jnp.where(live, meta[2 * cap, there], 0)
             out[slot] = jnp.zeros(out.shape[1:], out.dtype)
             for k in range(cap):
 
                 @pl.when(k < count)
                 def _():
-                    row = lax.rem(rows[k, there], groups) ^ member
-                    col = lax.rem(cols[k, there], groups) ^ member
+                    row = lax.rem(meta[k, there], groups) ^ member
+                    col = lax.rem(meta[cap + k, there], groups) ^ member
                     row = pl.multiple_of(row * size, size)
                     col = pl.multiple_of(col * size, size)
                     out[slot, pl.ds(row, size), pl.ds(col, size)] = tiles[there, k]
 
 
 def place_tiles(plan, slots, own, sib, span):
-    tiles = own[3]
+    tiles = own[1]
     out = like((slots, span, span), tiles.dtype)
     scalars = pl.BlockSpec(memory_space=pltpu.SMEM)
     whole = pl.BlockSpec(memory_space=pltpu.VMEM)
     return pl.pallas_call(
         functools.partial(place_kernel, plan, lax.axis_size("rep"), lax.axis_size("blk")),
-        in_specs=([scalars] * 3 + [whole]) * 2,
+        in_specs=[scalars, whole] * 2,
         out_specs=[whole] * 2,
         out_shape=[out, out],
         compiler_params=pltpu.CompilerParams(vmem_limit_bytes=limit_for(out, tiles)),
@@ -191,11 +266,14 @@
     )(*own, *sib)
 
 
-def gather_kernel(counts, own_a, sib_a, *refs):
+def gather_kernel(slots, counts, began, own_a, sib_a, *refs):
     slabs, (own_out, sib_out) = refs[:-2], refs[-2:]
     own = sib = None
+    if began:
+        (own_in, sib_in), slabs = slabs[:2], slabs[2:]
+        own, sib = own_in[...], sib_in[...]
     start = 0
-    for s, count in enumerate(counts):
+    for s, count in zip(slots, counts):
         panel = [slab[...] for slab in slabs[start : start + count]]
         start += count
         panel = panel[0] if count == 1 else jnp.concatenate(panel, axis=0)
@@ -207,26 +285,31 @@
     sib_out[...] = sib.astype(sib_out.dtype)
 
 
-def forward_product(own_a, sib_a, held):
-    slots, span, _ = own_a.shape
-    slabs = [slab for slot in held for slab in slot]
+def forward_product(own_a, sib_a, held, slots, sums, last):
+    _, span, _ = own_a.shape
+    slabs = [slab for s in slots for slab in held[s]]
     width = slabs[0].shape[1]
     return pl.pallas_call(
-        functools.partial(gather_kernel, [len(slot) for slot in held]),
-        out_shape=[like((span, width), jnp.float32), like((span, width), jnp.bfloat16)],
-        compiler_params=pltpu.CompilerParams(vmem_limit_bytes=limit_for(own_a, sib_a, *slabs)),
-        cost_estimate=pl.CostEstimate(
-            flops=4 * slots * span * span * width,
-            bytes_accessed=4 * slots * span * span,
+        functools.partial(gather_kernel, slots, [len(held[s]) for s in slots], bool(sums)),
+        out_shape=[
+            like((span, width), jnp.float32),
+            like((span, width), jnp.bfloat16 if last else jnp.float32),
+        ],
+        compiler_params=pltpu.CompilerParams(
+            vmem_limit_bytes=limit_for(own_a, sib_a, *slabs, *sums)
+        ),
+        cost_estimate=pl.CostEstimate(
+            flops=4 * len(slots) * span * span * width,
+            bytes_accessed=4 * len(slots) * span * span,
             transcendentals=0,
         ),
         name="forward_product",
-    )(own_a, sib_a, *slabs)
+    )(own_a, sib_a, *sums, *slabs)
 
 
 def layer_kernel(groups, first, second, weight, *refs):
     core = lax.axis_index("blk") % 2
-    cots, (act_out, keep_out, pass_out, back_out, grad) = refs[:groups], refs[groups:]
+    cots, (act_out, keep_out, sent_out, grad) = refs[:groups], refs[groups:]
     size = cots[0].shape[0]
     half = keep_out.shape[0]
     grads = []
@@ -249,12 +332,12 @@
         back = lax.dot_general(
             slope, weight[...], (((1,), (1,)), ((), ())), preferred_element_type=jnp.float32
         )
-        back_out[here, :] = back.astype(back_out.dtype)
+        sent_out[here, :] = back.astype(sent_out.dtype)
     grad[...] = tree_sum(grads)
     keep = pl.multiple_of(core * half, half)
     away = pl.multiple_of((1 - core) * half, half)
-    keep_out[...] = grad[pl.ds(keep, half), :].astype(keep_out.dtype)
-    pass_out[...] = grad[pl.ds(away, half), :].astype(pass_out.dtype)
+    keep_out[...] = grad[pl.ds(keep, half), :]
+    sent_out[groups * size :, :] = grad[pl.ds(away, half), :].astype(sent_out.dtype)
 
 
 def layer(first, second, weight, cots, groups):
@@ -264,9 +347,8 @@
         functools.partial(layer_kernel, groups),
         out_shape=[
             like((size, width), jnp.bfloat16),
-            like((width // 2, width), jnp.bfloat16),
-            like((width // 2, width), jnp.bfloat16),
-            like((span, width), jnp.bfloat16),
+            like((width // 2, width), jnp.float32),
+            like((span + width // 2, width), jnp.bfloat16),
         ],
         scratch_shapes=[pltpu.VMEM((width, width), jnp.float32)],
         compiler_params=pltpu.CompilerParams(vmem_limit_bytes=limit_for(first, second, *cots)),
@@ -279,21 +361,29 @@
     )(first, second, weight, *cots)
 
 
-def scatter_kernel(own_a, sib_a, own_rows, sib_rows, *outs):
+def scatter_kernel(own_a, sib_a, own_sent, sib_sent, grad, *outs):
     turned = (((0,), (0,)), ((), ()))
+    span = own_a.shape[1]
+    *outs, grad_out = outs
     for s, out in enumerate(outs):
         total = lax.dot_general(
-            own_a[s], own_rows[...], turned, preferred_element_type=jnp.float32
-        ) + lax.dot_general(sib_a[s], sib_rows[...], turned, preferred_element_type=jnp.float32)
+            own_a[s], own_sent[:span, :], turned, preferred_element_type=jnp.float32
+        ) + lax.dot_general(
+            sib_a[s], sib_sent[:span, :], turned, preferred_element_type=jnp.float32
+        )
         out[...] = total.astype(out.dtype)
-
-
-def backward_product(own_a, sib_a, own_rows, sib_rows, types):
+    total = grad[...] + sib_sent[span:, :].astype(jnp.float32)
+    grad_out[...] = total.astype(grad_out.dtype)
+
+
+def backward_product(own_a, sib_a, own_sent, sib_sent, grad, types):
     slots, span, _ = own_a.shape
-    width = own_rows.shape[1]
+    rows, width = own_sent.shape
+    outs = [like((span, width), kind) for kind in types]
+    outs.append(like((rows - span, width), jnp.bfloat16))
     return pl.pallas_call(
         scatter_kernel,
-        out_shape=[like((span, width), kind) for kind in types],
+        out_shape=outs,
         compiler_params=pltpu.CompilerParams(
             vmem_limit_bytes=limit_for(own_a, sib_a) + slots * span * width * 8
         ),
@@ -303,7 +393,7 @@
             transcendentals=0,
         ),
         name="backward_product",
-    )(own_a, sib_a, own_rows, sib_rows)
+    )(own_a, sib_a, own_sent, sib_sent, grad)
 
 
 def on_device(features, weight, cotangent, tile_row, tile_col, tile_count, tile_vals):
@@ -316,12 +406,16 @@
     types = plan.part_types()
 
     tiles = (tile_row[0, 0].T, tile_col[0, 0].T, tile_count[0, 0], tile_vals[0, 0])
-    sib_tiles = [along(t, 1) for t in tiles]
-    own_a, sib_a = place_tiles(plan, len(types), tiles, sib_tiles, span)
+    meta = jnp.concatenate([tiles[0], tiles[1], tile_count[0]])
+    sib_tiles = [along(meta, 1), along(tiles[3], 1)]
+    own_a, sib_a = place_tiles(plan, len(types), [meta, tiles[3]], sib_tiles, span)
     cots = [cotangent] + [across(cotangent, i) for i in range(1, groups)]
     held = plan.gather(features, sib_tiles + cots[1:], [own_a])
 
-    own_part, sib_part = forward_product(own_a, sib_a, held)
+    sums = ()
+    for slots in plan.batches:
+        sums = forward_product(own_a, sib_a, held, slots, sums, slots is plan.batches[-1])
+    own_part, sib_part = sums
     total = (own_part + along(sib_part, 1).astype(jnp.float32)).astype(jnp.bfloat16)
     bit = 1
     while 2 * bit < groups:
@@ -331,22 +425,9 @@
         bit *= 2
     other = across(total, bit)
 
-    activations, grad_keep, grad_pass, back_rows = layer(total, other, weight, cots, groups)
-    sib_rows = along(back_rows, 1)
-    parts = backward_product(own_a, sib_a, back_rows, sib_rows, types)
-    feature_grad, came = plan.scatter(parts, size)
-
-    grad_pass = after(grad_pass, parts[0])
-    grad = (grad_keep.astype(jnp.float32) + along(grad_pass, 1).astype(jnp.float32)).astype(
-        jnp.bfloat16
-    )
-    grad = after(grad, came)
-    bit = 2
-    while bit < panels:
-        grad = (grad.astype(jnp.float32) + along(grad, bit).astype(jnp.float32)).astype(
-            jnp.bfloat16
-        )
-        bit *= 2
+    activations, grad, sent = layer(total, other, weight, cots, groups)
+    *parts, grad = backward_product(own_a, sib_a, sent, along(sent, 1), grad, types)
+    feature_grad, grad = plan.scatter(parts, grad, size)
     mate = along(grad, 1)
     weight_grad = jnp.where(
         core == 0, jnp.concatenate([grad, mate]), jnp.concatenate([mate, grad])

time: 59.8 us -> 54.9 us (0.918)
  waiting for transfers between devices: 27 us -> 19.7 us
  starting transfers between devices: 24.9 us -> 27.2 us
  Pallas kernels: 3.19 us -> 4.1 us
  local copies, waits for them, and re-layouts: 2.12 us -> 1.25 us
    ppermute x13 -> x10, waiting for transfers between devices: 17.2 us -> 7.84 us  [along(): return lax.ppermute(array, 'blk', xor_pairs(lax.axis_size('blk'), bit))]
    ppermute x6 -> x7, starting transfers between devices: 9.88 us -> 14.7 us  [move(): return lax.ppermute(array, BOTH, pairs)]
    ppermute x13 -> x10, starting transfers between devices: 8.06 us -> 4.78 us  [along(): return lax.ppermute(array, 'blk', xor_pairs(lax.axis_size('blk'), bit))]
    ppermute x6, waiting for transfers between devices: 5.49 us -> 7.27 us  [across(): return lax.ppermute(array, 'rep', xor_pairs(lax.axis_size('rep'), bit))]
    pallas_call x2 -> x6, Pallas kernels: 1.05 us -> 1.94 us  [the longest x2 0.66 us: forward_product(): pl.pallas_call(functools.partial(gather_kernel, slots, [len(held[s]) for...]
    unnamed x13 -> x8, local copies, waits for them, and re-layouts: 2.1 us -> 1.24 us
    ppermute x6, starting transfers between devices: 6.93 us -> 7.74 us  [across(): return lax.ppermute(array, 'rep', xor_pairs(lax.axis_size('rep'), bit))]
    concatenate x0 -> x1, other arithmetic: none -> 0.72 us  [on_device(): meta = jnp.concatenate([tiles[0], tiles[1], tile_count[0]])]
  transfers between devices with their start and end apart: 25 -> 23, of which waited for: 15 -> 12; matrix products, arithmetic and copies ran while one was open for 3% -> 2% of each run, Pallas kernels for 2% -> 4%
where the time goes in v3:
time: 54.9 us; the launch traced here: 54.6 us
  starting transfers between devices  27.2 us (50%)
  waiting for transfers between devices  19.7 us (36%)
  Pallas kernels  4.1 us (7%)
  other arithmetic  1.6 us (3%)
  local copies, waits for them, and re-layouts  1.25 us (2%)
  between operations  0.85 us (2%)
    ppermute x7, starting transfers between devices, move(): return lax.ppermute(array, BOTH, pairs)  14.7 us
    ppermute x10, waiting for transfers between devices, along(): return lax.ppermute(array, 'blk', xor_pairs(lax.axis_size('blk'), bit))  7.84 us
    ppermute x6, starting transfers between devices, across(): return lax.ppermute(array, 'rep', xor_pairs(lax.axis_size('rep'), bit))  7.74 us
    ppermute x6, waiting for transfers between devices, across(): return lax.ppermute(array, 'rep', xor_pairs(lax.axis_size('rep'), bit))  7.27 us
    ppermute x10, starting transfers between devices, along(): return lax.ppermute(array, 'blk', xor_pairs(lax.axis_size('blk'), bit))  4.78 us
    ppermute x7, waiting for transfers between devices, move(): return lax.ppermute(array, BOTH, pairs)  4.57 us
    pallas_call x1, Pallas kernels, place_tiles(): pl.pallas_call(functools.partial(place_kernel, plan, lax.axis_size('rep')...  1.25 us
    unnamed x8, local copies, waits for them, and re-layouts  1.24 us
  transfers between devices with their start and end apart: 23, of which 12 were waited for; matrix products, arithmetic and copies ran while one was open for 2% of the time, Pallas kernels for 4%

profile of v3, /device:TPU:0, one launch (start us, length us, event | category | flops | bytes accessed | tf_op | source)
XLA Modules:
  0.0 54.6 jit_solution(11437480548746236118)
XLA Ops:
  0.6 0.0 copy-start.1
  0.6 0.5 collective-permute-start.1
  1.2 3.7 %collective-permute-start.5 = (bf16[128,256]{1,0:T(8,128)(2,1)}, bf16[128,256]{1,0:T(8,128)(2,1)S(1)}, u32[]{:S(2)}, u32[]{:S(2)}) collective-permute-start(bf16[128,256]{1,0:T(8,128)(2,1)} %first.1), channel_id=1, source_target_pairs={{0,8},{1,9},{2,10},{3,11},{4,12},{5,13},{6,14},{7,15},{8,0},{9,1},... | collective-permute-start | bytes 196616 | tf_op jit(solution)/shard_map/ppermute | solution.py:56
  4.8 1.5 %collective-permute-start.2 = (bf16[128,256]{1,0:T(8,128)(2,1)}, bf16[128,256]{1,0:T(8,128)(2,1)S(1)}, u32[]{:S(2)}, u32[]{:S(2)}) collective-permute-start(bf16[128,256]{1,0:T(8,128)(2,1)} %first.1), channel_id=1, source_target_pairs={{0,16},{16,0},{1,17},{17,1},{2,18},{18,2},{3,19},{19,3},{4,20},{20... | collective-permute-start | bytes 196616 | tf_op jit(solution)/shard_map/ppermute | solution.py:60
  6.3 0.5 collective-permute-start.6
  6.9 0.7 %pad_add_fusion.refs_0_ = s32[9,8]{1,0:T(8,128)S(1)} fusion(s32[1,8]{1,0:T(1,128)} %bitcast.12, s32[4,8]{1,0:T(4,128)} %bitcast.10, s32[4,8]{1,0:T(4,128)} %bitcast.11), kind=kLoop, calls=%fused_computation.12 | loop fusion | flops 144 | bytes 576 | tf_op jit(solution)/shard_map/concatenate | solution.py:409
  7.6 0.0 collective-permute-start
  7.6 2.1 %collective-permute-done.2.second = bf16[128,256]{1,0:T(8,128)(2,1)S(1)} collective-permute-done((bf16[128,256]{1,0:T(8,128)(2,1)}, bf16[128,256]{1,0:T(8,128)(2,1)S(1)}, u32[]{:S(2)}, u32[]{:S(2)}) %collective-permute-start.2) | collective-permute-done | bytes 65568 | tf_op jit(solution)/shard_map/ppermute | solution.py:60
  9.7 0.0 copy-done.1
  9.7 1.6 %collective-permute-start.3 = (bf16[256,256]{1,0:T(8,128)(2,1)S(1)}, bf16[256,256]{1,0:T(8,128)(2,1)S(1)}, u32[]{:S(2)}, u32[]{:S(2)}) collective-permute-start(bf16[256,256]{1,0:T(8,128)(2,1)S(1)} %stack.1.refs_0_), channel_id=1, source_target_pairs={{0,4},{1,5},{2,6},{3,7},{4,8},{5,9},{6,10},{7,11},{8,12},{9,13},{1... | collective-permute-start | bytes 393224 | tf_op jit(solution)/shard_map/ppermute | solution.py:56
  11.3 0.0 collective-permute-done.refs_2_
  11.3 1.0 %collective-permute-start.4 = (bf16[256,256]{1,0:T(8,128)(2,1)S(1)}, bf16[256,256]{1,0:T(8,128)(2,1)S(1)}, u32[]{:S(2)}, u32[]{:S(2)}) collective-permute-start(bf16[256,256]{1,0:T(8,128)(2,1)S(1)} %stack.1.refs_0_), channel_id=1, source_target_pairs={{0,6},{1,7},{2,4},{3,5},{4,10},{5,11},{6,8},{7,9},{8,14},{9,15},{1... | collective-permute-start | bytes 393224 | tf_op jit(solution)/shard_map/ppermute | solution.py:56
  12.4 0.0 collective-permute-done.6.refs_1_
  12.4 0.0 collective-permute-done.5.refs_2_
  12.4 0.0 collective-permute-done.1.refs_3_
  12.4 0.6 %collective-permute-start.8 = (bf16[128,256]{1,0:T(8,128)(2,1)S(1)}, bf16[128,256]{1,0:T(8,128)(2,1)S(1)}, u32[]{:S(2)}, u32[]{:S(2)}) collective-permute-start(bf16[128,256]{1,0:T(8,128)(2,1)S(1)} %get-tuple-element.48), channel_id=1, source_target_pairs={{0,2},{1,3},{2,0},{3,1},{4,6},{5,7},{6,4},{7,5},{8,10},{9,11},{10,... | collective-permute-start | bytes 196616 | tf_op jit(solution)/shard_map/ppermute | solution.py:64
  13.0 2.8 %collective-permute-start.9 = (bf16[128,256]{1,0:T(8,128)(2,1)S(1)}, bf16[128,256]{1,0:T(8,128)(2,1)S(1)}, u32[]{:S(2)}, u32[]{:S(2)}) collective-permute-start(bf16[128,256]{1,0:T(8,128)(2,1)S(1)} %get-tuple-element.47), channel_id=1, source_target_pairs={{0,18},{1,19},{2,16},{3,17},{4,22},{5,23},{6,20},{7,21},{8,26},{9,... | collective-permute-start | bytes 196616 | tf_op jit(solution)/shard_map/ppermute | solution.py:56
  15.8 0.2 collective-permute-start.7
  16.0 0.0 copy-start
  16.0 1.2 %copy-done = bf16[1,1,8,4,128,128]{5,4,3,2,1,0:T(8,128)(2,1)S(1)} copy-done((bf16[1,1,8,4,128,128]{5,4,3,2,1,0:T(8,128)(2,1)S(1)}, bf16[1,1,8,4,128,128]{5,4,3,2,1,0:T(8,128)(2,1)}, u32[]{:S(2)}) %copy-start) | copy-done | bytes 1048600
  17.2 1.3 %place_tiles.1 = (bf16[5,256,256]{2,1,0:T(8,128)(2,1)S(1)}, bf16[5,256,256]{2,1,0:T(8,128)(2,1)S(1)}) custom-call(s32[9,8]{1,0:T(8,128)S(1)} %pad_add_fusion.refs_0_, bf16[8,4,128,128]{3,2,1,0:T(8,128)(2,1)S(1)} %bitcast.9, s32[9,8]{1,0:T(8,128)S(1)} %collective-permute-done.refs_2_, bf16[8,4,128,128]{3,2,1,0:T(8,128)(2,1)S(1)} %collective-permute-done.1.refs_3_), custom_call_target="tpu_custom_call" | custom-call | bytes 2621440 | tf_op jit(solution)/shard_map/place_tiles/pallas_call | solution.py:256
  18.4 0.0 collective-permute-done.3.refs_1_
  18.4 1.3 %collective-permute-done.4.refs_2_ = bf16[256,256]{1,0:T(8,128)(2,1)S(1)} collective-permute-done((bf16[256,256]{1,0:T(8,128)(2,1)S(1)}, bf16[256,256]{1,0:T(8,128)(2,1)S(1)}, u32[]{:S(2)}, u32[]{:S(2)}) %collective-permute-start.4) | collective-permute-done | bytes 131104 | tf_op jit(solution)/shard_map/ppermute | solution.py:56
  19.7 0.4 forward_product.2
  20.1 0.0 collective-permute-done.8.refs_4_
  20.1 0.0 collective-permute-done.9.refs_5_
  20.1 0.0 collective-permute-done.7.refs_3_
  20.1 0.3 forward_product.3
  20.4 0.1 collective-permute-start.10
  20.5 1.3 %collective-permute-done.10 = bf16[256,256]{1,0:T(8,128)(2,1)S(1)} collective-permute-done((bf16[256,256]{1,0:T(8,128)(2,1)S(1)}, bf16[256,256]{1,0:T(8,128)(2,1)S(1)}, u32[]{:S(2)}, u32[]{:S(2)}) %collective-permute-start.10) | collective-permute-done | bytes 131104 | tf_op jit(solution)/shard_map/ppermute | solution.py:64
  21.8 0.0 copy-start.2
  21.8 0.0 copy-start.3
  21.9 0.7 %collective-permute-start.11 = (bf16[256,256]{1,0:T(8,128)(2,1)S(1)}, bf16[256,256]{1,0:T(8,128)(2,1)S(1)}, u32[]{:S(2)}, u32[]{:S(2)}) collective-permute-start(bf16[256,256]{1,0:T(8,128)(2,1)S(1)} %add_convert_fusion.first), channel_id=1, source_target_pairs={{0,16},{16,0},{1,17},{17,1},{2,18},{18,2},{3,19},{19,3},{4,20},{20... | collective-permute-start | bytes 393224 | tf_op jit(solution)/shard_map/ppermute | solution.py:60
  22.6 4.9 %collective-permute-done.11.second = bf16[256,256]{1,0:T(8,128)(2,1)S(1)} collective-permute-done((bf16[256,256]{1,0:T(8,128)(2,1)S(1)}, bf16[256,256]{1,0:T(8,128)(2,1)S(1)}, u32[]{:S(2)}, u32[]{:S(2)}) %collective-permute-start.11) | collective-permute-done | bytes 131104 | tf_op jit(solution)/shard_map/ppermute | solution.py:60
  27.5 0.0 copy-done.2
  27.5 0.0 copy-done.3
  27.5 0.9 %layer.1 = (bf16[128,256]{1,0:T(8,128)(2,1)}, f32[128,256]{1,0:T(8,128)S(1)}, bf16[384,256]{1,0:T(8,128)(2,1)S(1)}) custom-call(bf16[256,256]{1,0:T(8,128)(2,1)S(1)} %add_convert_fusion.first, bf16[256,256]{1,0:T(8,128)(2,1)S(1)} %collective-permute-done.11.second, bf16[256,256]{1,0:T(8,128)(2,1)S(1)} %copy-done.2, bf16[128,256]{1,0:T(8,128)(2,1)S(1)} %copy-done.3, ...), custom_call_target="tpu_custom_call" | custom-call | flops 100663296 | bytes 524288 | tf_op jit(solution)/shard_map/layer/pallas_call | solution.py:346
  28.4 0.0 collective-permute-start.12
  28.4 1.4 %collective-permute-done.12.sib_sent = bf16[384,256]{1,0:T(8,128)(2,1)S(1)} collective-permute-done((bf16[384,256]{1,0:T(8,128)(2,1)S(1)}, bf16[384,256]{1,0:T(8,128)(2,1)S(1)}, u32[]{:S(2)}, u32[]{:S(2)}) %collective-permute-start.12) | collective-permute-done | bytes 196640 | tf_op jit(solution)/shard_map/ppermute | solution.py:64
  29.8 0.5 %backward_product.1 = (f32[256,256]{1,0:T(8,128)S(1)}, f32[256,256]{1,0:T(8,128)S(1)}, bf16[256,256]{1,0:T(8,128)(2,1)S(1)}, bf16[256,256]{1,0:T(8,128)(2,1)S(1)...) custom-call(bf16[5,256,256]{2,1,0:T(8,128)(2,1)S(1)} %get-tuple-element.25.own_a, ...), custom_call_target="tpu_custom_call" | custom-call | flops 335544320 | bytes 1310720 | tf_op jit(solution)/shard_map/backward_product/pallas_call | solution.py:384
  30.4 1.6 %collective-permute-start.14 = (bf16[256,256]{1,0:T(8,128)(2,1)S(1)}, bf16[256,256]{1,0:T(8,128)(2,1)S(1)}, u32[]{:S(2)}, u32[]{:S(2)}) collective-permute-start(bf16[256,256]{1,0:T(8,128)(2,1)S(1)} %get-tuple-element.36), channel_id=1, source_target_pairs={{0,2},{1,3},{2,0},{3,1},{4,6},{5,7},{6,4},{7,5},{8,10},{9,11},{10,... | collective-permute-start | bytes 393224 | tf_op jit(solution)/shard_map/ppermute | solution.py:64
  32.0 1.8 %collective-permute-start.16 = (bf16[256,256]{1,0:T(8,128)(2,1)S(1)}, bf16[256,256]{1,0:T(8,128)(2,1)S(1)}, u32[]{:S(2)}, u32[]{:S(2)}) collective-permute-start(bf16[256,256]{1,0:T(8,128)(2,1)S(1)} %get-tuple-element.39), channel_id=1, source_target_pairs={{4,0},{5,1},{6,2},{7,3},{8,4},{9,5},{10,6},{11,7},{12,8},{13,9},{1... | collective-permute-start | bytes 393224 | tf_op jit(solution)/shard_map/ppermute | solution.py:56
  33.8 1.3 %collective-permute-start.19 = (bf16[256,256]{1,0:T(8,128)(2,1)S(1)}, bf16[256,256]{1,0:T(8,128)(2,1)S(1)}, u32[]{:S(2)}, u32[]{:S(2)}) collective-permute-start(bf16[256,256]{1,0:T(8,128)(2,1)S(1)} %get-tuple-element.43), channel_id=1, source_target_pairs={{6,0},{7,1},{4,2},{5,3},{10,4},{11,5},{8,6},{9,7},{14,8},{15,9},{1... | collective-permute-start | bytes 393224 | tf_op jit(solution)/shard_map/ppermute | solution.py:56
  35.0 0.7 %collective-permute-start.13 = (bf16[128,256]{1,0:T(8,128)(2,1)S(1)}, bf16[128,256]{1,0:T(8,128)(2,1)S(1)}, u32[]{:S(2)}, u32[]{:S(2)}) collective-permute-start(bf16[128,256]{1,0:T(8,128)(2,1)S(1)} %get-tuple-element.35), channel_id=1, source_target_pairs={{0,2},{1,3},{2,0},{3,1},{4,6},{5,7},{6,4},{7,5},{8,10},{9,11},{10,... | collective-permute-start | bytes 196616 | tf_op jit(solution)/shard_map/ppermute | solution.py:64
  35.7 0.3 collective-permute-done.14.came
  36.0 1.6 %collective-permute-done.16.ahead = bf16[256,256]{1,0:T(8,128)(2,1)S(1)} collective-permute-done((bf16[256,256]{1,0:T(8,128)(2,1)S(1)}, bf16[256,256]{1,0:T(8,128)(2,1)S(1)}, u32[]{:S(2)}, u32[]{:S(2)}) %collective-permute-start.16) | collective-permute-done | bytes 131104 | tf_op jit(solution)/shard_map/ppermute | solution.py:56
  37.7 2.7 %collective-permute-start.17 = (bf16[128,256]{1,0:T(8,128)(2,1)S(1)}, bf16[128,256]{1,0:T(8,128)(2,1)S(1)}, u32[]{:S(2)}, u32[]{:S(2)}) collective-permute-start(bf16[128,256]{1,0:T(8,128)(2,1)S(1)} %slice.15), channel_id=1, source_target_pairs={{0,16},{16,0},{1,17},{17,1},{2,18},{18,2},{3,19},{19,3},{4,20},{20... | collective-permute-start | bytes 196616 | tf_op jit(solution)/shard_map/ppermute | solution.py:60
  40.4 0.0 collective-permute-done.19.cross
  40.4 0.1 add_column.1
  40.5 2.1 %collective-permute-start.20 = (bf16[128,256]{1,0:T(8,128)(2,1)S(1)}, bf16[128,256]{1,0:T(8,128)(2,1)S(1)}, u32[]{:S(2)}, u32[]{:S(2)}) collective-permute-start(bf16[128,256]{1,0:T(8,128)(2,1)S(1)} %get-tuple-element.44), channel_id=1, source_target_pairs={{0,16},{16,0},{1,17},{17,1},{2,18},{18,2},{3,19},{19,3},{4,20},{20... | collective-permute-start | bytes 196616 | tf_op jit(solution)/shard_map/ppermute | solution.py:60
  42.6 0.0 collective-permute-done.13
  42.6 0.1 collective-permute-start.15
  42.7 0.3 collective-permute-done.17
  43.0 2.5 %collective-permute-start.21 = (bf16[128,256]{1,0:T(8,128)(2,1)S(1)}, bf16[128,256]{1,0:T(8,128)(2,1)S(1)}, u32[]{:S(2)}, u32[]{:S(2)}) collective-permute-start(bf16[128,256]{1,0:T(8,128)(2,1)S(1)} %fusion), channel_id=1, source_target_pairs={{8,0},{9,1},{10,2},{11,3},{12,4},{13,5},{14,6},{15,7},{0,8},{1,9},... | collective-permute-start | bytes 196616 | tf_op jit(solution)/shard_map/ppermute | solution.py:56
  45.4 1.5 %collective-permute-done.15 = bf16[128,256]{1,0:T(8,128)(2,1)S(1)} collective-permute-done((bf16[128,256]{1,0:T(8,128)(2,1)S(1)}, bf16[128,256]{1,0:T(8,128)(2,1)S(1)}, u32[]{:S(2)}, u32[]{:S(2)}) %collective-permute-start.15) | collective-permute-done | bytes 65568 | tf_op jit(solution)/shard_map/ppermute | solution.py:64
  46.9 1.2 %collective-permute-start.18 = (bf16[128,256]{1,0:T(8,128)(2,1)S(1)}, bf16[128,256]{1,0:T(8,128)(2,1)S(1)}, u32[]{:S(2)}, u32[]{:S(2)}) collective-permute-start(bf16[128,256]{1,0:T(8,128)(2,1)S(1)} %add_convert_fusion.2), channel_id=1, source_target_pairs={{0,8},{1,9},{2,10},{3,11},{4,12},{5,13},{6,14},{7,15},{8,0},{9,1},... | collective-permute-start | bytes 196616 | tf_op jit(solution)/shard_map/ppermute | solution.py:64
  48.2 0.0 collective-permute-done.20.second
  48.2 1.7 %collective-permute-done.21.third = bf16[128,256]{1,0:T(8,128)(2,1)S(1)} collective-permute-done((bf16[128,256]{1,0:T(8,128)(2,1)S(1)}, bf16[128,256]{1,0:T(8,128)(2,1)S(1)}, u32[]{:S(2)}, u32[]{:S(2)}) %collective-permute-start.21) | collective-permute-done | bytes 65568 | tf_op jit(solution)/shard_map/ppermute | solution.py:56
  49.9 2.7 %collective-permute-done.18 = bf16[128,256]{1,0:T(8,128)(2,1)S(1)} collective-permute-done((bf16[128,256]{1,0:T(8,128)(2,1)S(1)}, bf16[128,256]{1,0:T(8,128)(2,1)S(1)}, u32[]{:S(2)}, u32[]{:S(2)}) %collective-permute-start.18) | collective-permute-done | bytes 65568 | tf_op jit(solution)/shard_map/ppermute | solution.py:64
  52.6 0.1 collective-permute-start.22
  52.7 0.7 %finish.1 = bf16[128,256]{1,0:T(8,128)(2,1)} custom-call(f32[128,256]{1,0:T(8,128)S(1)} %get-tuple-element.46.first, bf16[128,256]{1,0:T(8,128)(2,1)S(1)} %collective-permute-done.20.second, bf16[128,256]{1,0:T(8,128)(2,1)S(1)} %collective-permute-done.21.third), custom_call_target="tpu_custom_call" | custom-call | flops 65536 | bytes 262144 | tf_op jit(solution)/shard_map/finish/pallas_call | solution.py:141
  53.3 0.6 %collective-permute-done.22 = bf16[128,256]{1,0:T(8,128)(2,1)S(1)} collective-permute-done((bf16[128,256]{1,0:T(8,128)(2,1)S(1)}, bf16[128,256]{1,0:T(8,128)(2,1)S(1)}, u32[]{:S(2)}, u32[]{:S(2)}) %collective-permute-start.22) | collective-permute-done | bytes 65568 | tf_op jit(solution)/shard_map/ppermute | solution.py:64
  53.9 0.7 %convert_multiply_fusion = f32[256,256]{1,0:T(8,128)} fusion(bf16[128,256]{1,0:T(8,128)(2,1)S(1)} %collective-permute-done.22, bf16[128,256]{1,0:T(8,128)(2,1)S(1)} %add_convert_fusion.1, pred[]{:T(512)S(6)} %eq.12), kind=kLoop, calls=%fused_computation | loop fusion | flops 720896 | bytes 393217 | tf_op jit(solution)/shard_map/mul | solution.py:432
  (9 shorter events, 0.2 us)
Async XLA Ops:
  0.6 9.1 %copy-start.1 = (bf16[128,256]{1,0:T(8,128)(2,1)S(1)}, bf16[128,256]{1,0:T(8,128)(2,1)}, u32[]{:S(2)}) copy-start(bf16[128,256]{1,0:T(8,128)(2,1)} %first.1) | copy-start | bytes 196612
  0.6 11.7 %collective-permute-start.1 = (bf16[8,4,128,128]{3,2,1,0:T(8,128)(2,1)}, bf16[8,4,128,128]{3,2,1,0:T(8,128)(2,1)S(1)}, u32[]{:S(2)}, u32[]{:S(2)}) collective-permute-start(bf16[8,4,128,128]{3,2,1,0:T(8,128)(2,1)} %bitcast.8), channel_id=1, source_target_pairs={{0,1},{1,0},{2,3},{3,2},{4,5},{5,4},{6,7},{7,6},{8,9},{9,8},{10,11... | collective-permute-start | bytes 3145736 | tf_op jit(solution)/shard_map/ppermute | solution.py:64
  1.2 11.2 %collective-permute-start.5 = (bf16[128,256]{1,0:T(8,128)(2,1)}, bf16[128,256]{1,0:T(8,128)(2,1)S(1)}, u32[]{:S(2)}, u32[]{:S(2)}) collective-permute-start(bf16[128,256]{1,0:T(8,128)(2,1)} %first.1), channel_id=1, source_target_pairs={{0,8},{1,9},{2,10},{3,11},{4,12},{5,13},{6,14},{7,15},{8,0},{9,1},... | collective-permute-start | bytes 196616 | tf_op jit(solution)/shard_map/ppermute | solution.py:56
  4.8 4.9 %collective-permute-start.2 = (bf16[128,256]{1,0:T(8,128)(2,1)}, bf16[128,256]{1,0:T(8,128)(2,1)S(1)}, u32[]{:S(2)}, u32[]{:S(2)}) collective-permute-start(bf16[128,256]{1,0:T(8,128)(2,1)} %first.1), channel_id=1, source_target_pairs={{0,16},{16,0},{1,17},{17,1},{2,18},{18,2},{3,19},{19,3},{4,20},{20... | collective-permute-start | bytes 196616 | tf_op jit(solution)/shard_map/ppermute | solution.py:60
  6.3 6.0 %collective-permute-start.6 = (bf16[128,256]{1,0:T(8,128)(2,1)}, bf16[128,256]{1,0:T(8,128)(2,1)S(1)}, u32[]{:S(2)}, u32[]{:S(2)}) collective-permute-start(bf16[128,256]{1,0:T(8,128)(2,1)} %refs_0_.1), channel_id=1, source_target_pairs={{0,16},{16,0},{1,17},{17,1},{2,18},{18,2},{3,19},{19,3},{4,20},{20... | collective-permute-start | bytes 196616 | tf_op jit(solution)/shard_map/ppermute | solution.py:60
  7.6 3.8 %collective-permute-start = (s32[9,8]{1,0:T(8,128)S(1)}, s32[9,8]{1,0:T(8,128)S(1)}, u32[]{:S(2)}, u32[]{:S(2)}) collective-permute-start(s32[9,8]{1,0:T(8,128)S(1)} %pad_add_fusion.refs_0_), channel_id=1, source_target_pairs={{0,1},{1,0},{2,3},{3,2},{4,5},{5,4},{6,7},{7,6},{8,9},{9,8},{10,11... | collective-permute-start | bytes 872 | tf_op jit(solution)/shard_map/ppermute | solution.py:64
  9.7 8.7 %collective-permute-start.3 = (bf16[256,256]{1,0:T(8,128)(2,1)S(1)}, bf16[256,256]{1,0:T(8,128)(2,1)S(1)}, u32[]{:S(2)}, u32[]{:S(2)}) collective-permute-start(bf16[256,256]{1,0:T(8,128)(2,1)S(1)} %stack.1.refs_0_), channel_id=1, source_target_pairs={{0,4},{1,5},{2,6},{3,7},{4,8},{5,9},{6,10},{7,11},{8,12},{9,13},{1... | collective-permute-start | bytes 393224 | tf_op jit(solution)/shard_map/ppermute | solution.py:56
  11.3 8.4 %collective-permute-start.4 = (bf16[256,256]{1,0:T(8,128)(2,1)S(1)}, bf16[256,256]{1,0:T(8,128)(2,1)S(1)}, u32[]{:S(2)}, u32[]{:S(2)}) collective-permute-start(bf16[256,256]{1,0:T(8,128)(2,1)S(1)} %stack.1.refs_0_), channel_id=1, source_target_pairs={{0,6},{1,7},{2,4},{3,5},{4,10},{5,11},{6,8},{7,9},{8,14},{9,15},{1... | collective-permute-start | bytes 393224 | tf_op jit(solution)/shard_map/ppermute | solution.py:56
  12.4 7.7 %collective-permute-start.8 = (bf16[128,256]{1,0:T(8,128)(2,1)S(1)}, bf16[128,256]{1,0:T(8,128)(2,1)S(1)}, u32[]{:S(2)}, u32[]{:S(2)}) collective-permute-start(bf16[128,256]{1,0:T(8,128)(2,1)S(1)} %get-tuple-element.48), channel_id=1, source_target_pairs={{0,2},{1,3},{2,0},{3,1},{4,6},{5,7},{6,4},{7,5},{8,10},{9,11},{10,... | collective-permute-start | bytes 196616 | tf_op jit(solution)/shard_map/ppermute | solution.py:64
  13.0 7.1 %collective-permute-start.9 = (bf16[128,256]{1,0:T(8,128)(2,1)S(1)}, bf16[128,256]{1,0:T(8,128)(2,1)S(1)}, u32[]{:S(2)}, u32[]{:S(2)}) collective-permute-start(bf16[128,256]{1,0:T(8,128)(2,1)S(1)} %get-tuple-element.47), channel_id=1, source_target_pairs={{0,18},{1,19},{2,16},{3,17},{4,22},{5,23},{6,20},{7,21},{8,26},{9,... | collective-permute-start | bytes 196616 | tf_op jit(solution)/shard_map/ppermute | solution.py:56
  15.8 4.3 %collective-permute-start.7 = (bf16[128,256]{1,0:T(8,128)(2,1)S(1)}, bf16[128,256]{1,0:T(8,128)(2,1)S(1)}, u32[]{:S(2)}, u32[]{:S(2)}) collective-permute-start(bf16[128,256]{1,0:T(8,128)(2,1)S(1)} %collective-permute-done.5.refs_2_), channel_id=1, source_target_pairs={{0,16},{16,0},{1,17},{17,1},{2,18},{18,2},{3,19},{19,3},{4,20},{20... | collective-permute-start | bytes 196616 | tf_op jit(solution)/shard_map/ppermute | solution.py:60
  16.0 1.2 %copy-start = (bf16[1,1,8,4,128,128]{5,4,3,2,1,0:T(8,128)(2,1)S(1)}, bf16[1,1,8,4,128,128]{5,4,3,2,1,0:T(8,128)(2,1)}, u32[]{:S(2)}) copy-start(bf16[1,1,8,4,128,128]{5,4,3,2,1,0:T(8,128)(2,1)} %param.13) | copy-start | bytes 3145732
  20.4 1.4 %collective-permute-start.10 = (bf16[256,256]{1,0:T(8,128)(2,1)S(1)}, bf16[256,256]{1,0:T(8,128)(2,1)S(1)}, u32[]{:S(2)}, u32[]{:S(2)}) collective-permute-start(bf16[256,256]{1,0:T(8,128)(2,1)S(1)} %get-tuple-element.31), channel_id=1, source_target_pairs={{0,1},{1,0},{2,3},{3,2},{4,5},{5,4},{6,7},{7,6},{8,9},{9,8},{10,11... | collective-permute-start | bytes 393224 | tf_op jit(solution)/shard_map/ppermute | solution.py:64
  21.8 5.7 %copy-start.2 = (bf16[256,256]{1,0:T(8,128)(2,1)S(1)}, bf16[256,256]{1,0:T(8,128)(2,1)}, u32[]{:S(2)}) copy-start(bf16[256,256]{1,0:T(8,128)(2,1)} %weight.1) | copy-start | bytes 393220
  21.8 5.7 %copy-start.3 = (bf16[128,256]{1,0:T(8,128)(2,1)S(1)}, bf16[128,256]{1,0:T(8,128)(2,1)}, u32[]{:S(2)}) copy-start(bf16[128,256]{1,0:T(8,128)(2,1)} %refs_0_.1) | copy-start | bytes 196612
  21.9 5.6 %collective-permute-start.11 = (bf16[256,256]{1,0:T(8,128)(2,1)S(1)}, bf16[256,256]{1,0:T(8,128)(2,1)S(1)}, u32[]{:S(2)}, u32[]{:S(2)}) collective-permute-start(bf16[256,256]{1,0:T(8,128)(2,1)S(1)} %add_convert_fusion.first), channel_id=1, source_target_pairs={{0,16},{16,0},{1,17},{17,1},{2,18},{18,2},{3,19},{19,3},{4,20},{20... | collective-permute-start | bytes 393224 | tf_op jit(solution)/shard_map/ppermute | solution.py:60
  28.4 1.4 %collective-permute-start.12 = (bf16[384,256]{1,0:T(8,128)(2,1)S(1)}, bf16[384,256]{1,0:T(8,128)(2,1)S(1)}, u32[]{:S(2)}, u32[]{:S(2)}) collective-permute-start(bf16[384,256]{1,0:T(8,128)(2,1)S(1)} %get-tuple-element.33.own_sent), channel_id=1, source_target_pairs={{0,1},{1,0},{2,3},{3,2},{4,5},{5,4},{6,7},{7,6},{8,9},{9,8},{10,11... | collective-permute-start | bytes 589832 | tf_op jit(solution)/shard_map/ppermute | solution.py:64
  30.4 5.6 %collective-permute-start.14 = (bf16[256,256]{1,0:T(8,128)(2,1)S(1)}, bf16[256,256]{1,0:T(8,128)(2,1)S(1)}, u32[]{:S(2)}, u32[]{:S(2)}) collective-permute-start(bf16[256,256]{1,0:T(8,128)(2,1)S(1)} %get-tuple-element.36), channel_id=1, source_target_pairs={{0,2},{1,3},{2,0},{3,1},{4,6},{5,7},{6,4},{7,5},{8,10},{9,11},{10,... | collective-permute-start | bytes 393224 | tf_op jit(solution)/shard_map/ppermute | solution.py:64
  32.0 5.7 %collective-permute-start.16 = (bf16[256,256]{1,0:T(8,128)(2,1)S(1)}, bf16[256,256]{1,0:T(8,128)(2,1)S(1)}, u32[]{:S(2)}, u32[]{:S(2)}) collective-permute-start(bf16[256,256]{1,0:T(8,128)(2,1)S(1)} %get-tuple-element.39), channel_id=1, source_target_pairs={{4,0},{5,1},{6,2},{7,3},{8,4},{9,5},{10,6},{11,7},{12,8},{13,9},{1... | collective-permute-start | bytes 393224 | tf_op jit(solution)/shard_map/ppermute | solution.py:56
  33.8 6.6 %collective-permute-start.19 = (bf16[256,256]{1,0:T(8,128)(2,1)S(1)}, bf16[256,256]{1,0:T(8,128)(2,1)S(1)}, u32[]{:S(2)}, u32[]{:S(2)}) collective-permute-start(bf16[256,256]{1,0:T(8,128)(2,1)S(1)} %get-tuple-element.43), channel_id=1, source_target_pairs={{6,0},{7,1},{4,2},{5,3},{10,4},{11,5},{8,6},{9,7},{14,8},{15,9},{1... | collective-permute-start | bytes 393224 | tf_op jit(solution)/shard_map/ppermute | solution.py:56
  35.0 7.6 %collective-permute-start.13 = (bf16[128,256]{1,0:T(8,128)(2,1)S(1)}, bf16[128,256]{1,0:T(8,128)(2,1)S(1)}, u32[]{:S(2)}, u32[]{:S(2)}) collective-permute-start(bf16[128,256]{1,0:T(8,128)(2,1)S(1)} %get-tuple-element.35), channel_id=1, source_target_pairs={{0,2},{1,3},{2,0},{3,1},{4,6},{5,7},{6,4},{7,5},{8,10},{9,11},{10,... | collective-permute-start | bytes 196616 | tf_op jit(solution)/shard_map/ppermute | solution.py:64
  37.7 5.3 %collective-permute-start.17 = (bf16[128,256]{1,0:T(8,128)(2,1)S(1)}, bf16[128,256]{1,0:T(8,128)(2,1)S(1)}, u32[]{:S(2)}, u32[]{:S(2)}) collective-permute-start(bf16[128,256]{1,0:T(8,128)(2,1)S(1)} %slice.15), channel_id=1, source_target_pairs={{0,16},{16,0},{1,17},{17,1},{2,18},{18,2},{3,19},{19,3},{4,20},{20... | collective-permute-start | bytes 196616 | tf_op jit(solution)/shard_map/ppermute | solution.py:60
  40.5 7.7 %collective-permute-start.20 = (bf16[128,256]{1,0:T(8,128)(2,1)S(1)}, bf16[128,256]{1,0:T(8,128)(2,1)S(1)}, u32[]{:S(2)}, u32[]{:S(2)}) collective-permute-start(bf16[128,256]{1,0:T(8,128)(2,1)S(1)} %get-tuple-element.44), channel_id=1, source_target_pairs={{0,16},{16,0},{1,17},{17,1},{2,18},{18,2},{3,19},{19,3},{4,20},{20... | collective-permute-start | bytes 196616 | tf_op jit(solution)/shard_map/ppermute | solution.py:60
  42.6 4.3 %collective-permute-start.15 = (bf16[128,256]{1,0:T(8,128)(2,1)S(1)}, bf16[128,256]{1,0:T(8,128)(2,1)S(1)}, u32[]{:S(2)}, u32[]{:S(2)}) collective-permute-start(bf16[128,256]{1,0:T(8,128)(2,1)S(1)} %add_convert_fusion.3), channel_id=1, source_target_pairs={{0,4},{1,5},{2,6},{3,7},{4,0},{5,1},{6,2},{7,3},{8,12},{9,13},{10,... | collective-permute-start | bytes 196616 | tf_op jit(solution)/shard_map/ppermute | solution.py:64
  43.0 6.9 %collective-permute-start.21 = (bf16[128,256]{1,0:T(8,128)(2,1)S(1)}, bf16[128,256]{1,0:T(8,128)(2,1)S(1)}, u32[]{:S(2)}, u32[]{:S(2)}) collective-permute-start(bf16[128,256]{1,0:T(8,128)(2,1)S(1)} %fusion), channel_id=1, source_target_pairs={{8,0},{9,1},{10,2},{11,3},{12,4},{13,5},{14,6},{15,7},{0,8},{1,9},... | collective-permute-start | bytes 196616 | tf_op jit(solution)/shard_map/ppermute | solution.py:56
  46.9 5.6 %collective-permute-start.18 = (bf16[128,256]{1,0:T(8,128)(2,1)S(1)}, bf16[128,256]{1,0:T(8,128)(2,1)S(1)}, u32[]{:S(2)}, u32[]{:S(2)}) collective-permute-start(bf16[128,256]{1,0:T(8,128)(2,1)S(1)} %add_convert_fusion.2), channel_id=1, source_target_pairs={{0,8},{1,9},{2,10},{3,11},{4,12},{5,13},{6,14},{7,15},{8,0},{9,1},... | collective-permute-start | bytes 196616 | tf_op jit(solution)/shard_map/ppermute | solution.py:64
  52.6 1.3 %collective-permute-start.22 = (bf16[128,256]{1,0:T(8,128)(2,1)S(1)}, bf16[128,256]{1,0:T(8,128)(2,1)S(1)}, u32[]{:S(2)}, u32[]{:S(2)}) collective-permute-start(bf16[128,256]{1,0:T(8,128)(2,1)S(1)} %add_convert_fusion.1), channel_id=1, source_target_pairs={{0,1},{1,0},{2,3},{3,2},{4,5},{5,4},{6,7},{7,6},{8,9},{9,8},{10,11... | collective-permute-start | bytes 196616 | tf_op jit(solution)/shard_map/ppermute | solution.py:64

commit v4 on v3

--- a/solution.py
+++ b/solution.py
@@ -87,16 +87,18 @@
             (steps * (member + 1), member <= groups - 2),
         ] + [(steps * member + 2 * k, True) for k in range(1, steps // 2)]
 
-    def gather(self, slab, early, placed):
+    def gather(self, slab, cots, early):
         slabs = [slab] + [across(slab, i) for i in range(1, self.groups)]
-        return [slabs] + [[move(part, pairs) for part in slabs] for pairs in self.moves]
-
-    def part_types(self):
-        return [jnp.float32] + [jnp.bfloat16] * len(self.moves)
-
-    def scatter(self, parts, grad, size):
-        column = parts[0]
-        for pairs, part in zip(self.moves, parts[1:]):
+        cots = [cots] + [across(cots, i) for i in range(1, self.groups)]
+        return cots, [slabs] + [[move(part, pairs) for part in slabs] for pairs in self.moves]
+
+    def pieces(self, size, span):
+        moved = [(s, 0, span, jnp.bfloat16, False) for s in range(1, 1 + len(self.moves))]
+        return [(0, 0, span, jnp.float32, False)] + moved + [(0, 0, 0, jnp.bfloat16, True)]
+
+    def scatter(self, parts, size):
+        column, grad = parts[0], parts[-1]
+        for pairs, part in zip(self.moves, parts[1:-1]):
             column = column + move(part, back(pairs)).astype(jnp.float32)
         total = column[:size]
         for i in range(1, self.groups):
@@ -109,27 +111,47 @@
         return total, grad
 
 
-def column_kernel(own, came, ahead, cross, keep_out, pass_out):
+def sends_own():
+    return (lax.axis_index("blk") // 2) % 2 == lax.axis_index("rep")
+
+
+def far_kernel(far, far_mate, came, corner, side, far_out, grad_out):
+    size = far_out.shape[0]
+    slant = jnp.where(sends_own(), corner[...], came[:size, :]).astype(jnp.float32)
+    total = far[...] + far_mate[...].astype(jnp.float32) + slant
+    far_out[...] = total.astype(far_out.dtype)
+    grad = side[size:, :].astype(jnp.float32) + came[size:, :].astype(jnp.float32)
+    grad_out[...] = grad.astype(grad_out.dtype)
+
+
+def column_kernel(own, came, corner, ahead, cross, keep_out, pass_out):
     size = keep_out.shape[0]
-    kept = (lax.axis_index("blk") // 2) % 2 == lax.axis_index("rep")
-    mine = jnp.where(kept, 1.0, 0.0)
-    total = own[...] + mine * came[...].astype(jnp.float32)
-    total = total + (ahead[...].astype(jnp.float32) + cross[...].astype(jnp.float32))
-    keep_out[...] = total[:size]
+    slant = jnp.where(sends_own(), came[:size, :], corner[...]).astype(jnp.float32)
+    total = own[...] + (ahead[...].astype(jnp.float32) + cross[...].astype(jnp.float32))
+    keep_out[...] = total[:size] + slant
     pass_out[...] = total[size:].astype(pass_out.dtype)
 
 
-def add_column(own, came, ahead, cross, size):
-    span, width = own.shape
-    return pl.pallas_call(
-        column_kernel,
-        out_shape=[like((size, width), jnp.float32), like((span - size, width), jnp.bfloat16)],
-        compiler_params=pltpu.CompilerParams(vmem_limit_bytes=limit_for(own, came, ahead, cross)),
-        cost_estimate=pl.CostEstimate(
-            flops=3 * span * width, bytes_accessed=8 * span * width, transcendentals=0
-        ),
-        name="add_column",
-    )(own, came, ahead, cross)
+def local_call(kernel, name, outs, *arrays):
+    moved = sum(a.size * a.dtype.itemsize for a in arrays)
+    return pl.pallas_call(
+        kernel,
+        out_shape=outs,
+        compiler_params=pltpu.CompilerParams(vmem_limit_bytes=limit_for(*arrays)),
+        cost_estimate=pl.CostEstimate(flops=moved, bytes_accessed=moved, transcendentals=0),
+        name=name,
+    )(*arrays)
+
+
+def sort_far(far, far_mate, came, corner, side):
+    rows, width = came.shape
+    outs = [like(far.shape, came.dtype), like((rows - far.shape[0], width), came.dtype)]
+    return local_call(far_kernel, "sort_far", outs, far, far_mate, came, corner, side)
+
+
+def add_column(own, came, corner, ahead, cross):
+    outs = [like(corner.shape, jnp.float32), like(corner.shape, corner.dtype)]
+    return local_call(column_kernel, "add_column", outs, own, came, corner, ahead, cross)
 
 
 def finish_kernel(first, second, third, out):
@@ -192,37 +214,44 @@
     def sends_own(self):
         return (lax.axis_index("blk") // 2) % 2 == lax.axis_index("rep")
 
-    def gather(self, slab, early, placed):
+    def gather(self, slab, cots, early):
         mate = across(slab, 1)
-        far = after(move(slab, self.half), *early)
+        cots = [cots, across(cots, 1)]
+        far = after(move(slab, self.half), cots[1], *early)
         both = stack(slab, mate)
         ahead = move(both, self.ahead)
         cross = move(both, self.cross)
         own = self.sends_own()
         last = along(jnp.where(own, slab, far), 2)
         last_mate = move(jnp.where(own, far, slab), self.corner)
-        return [[both], [far, across(far, 1)], [ahead], [cross], [last, last_mate]]
-
-    def part_types(self):
-        return [jnp.float32, jnp.float32, jnp.bfloat16, jnp.bfloat16, jnp.bfloat16]
-
-    def scatter(self, parts, grad, size):
-        own, far, ahead, cross, last = parts
+        return cots, [[both], [far, across(far, 1)], [ahead], [cross], [last, last_mate]]
+
+    def pieces(self, size, span):
+        half = jnp.bfloat16
+        return [
+            (0, 0, span, jnp.float32, False),
+            (1, 0, size, jnp.float32, False),
+            (1, size, span, half, False),
+            (2, 0, span, half, False),
+            (3, 0, span, half, False),
+            (4, 0, size, half, True),
+            (4, size, span, half, False),
+        ]
+
+    def scatter(self, parts, size):
+        own, far, far_pass, ahead, cross, side, corner = parts
         ahead = move(ahead, back(self.ahead))
-        came = along(last, 2)
-        grad = add_rounded(grad, after(along(grad, 2), came))
-        kept = self.sends_own()
-        far = far + jnp.where(kept, 0.0, came.astype(jnp.float32))
-        far_pass = far[size:].astype(jnp.bfloat16)
-        far_mate = across(after(far_pass, ahead), 1)
         cross = move(cross, back(self.cross))
-        grad = add_rounded(grad, after(along(grad, 4), far_mate))
-        far_sum = (far[:size] + far_mate.astype(jnp.float32)).astype(jnp.bfloat16)
+        came = along(side, 2)
+        corner = move(corner, back(self.corner))
+        far_mate = across(far_pass, 1)
+        far_sum, grad = sort_far(far, far_mate, came, corner, side)
+        column, column_pass = add_column(own, came, corner, ahead, cross)
+        grad = add_rounded(grad, along(grad, 4))
         far_back = move(far_sum, back(self.half))
-        column, column_pass = add_column(own, came, ahead, cross, size)
         mate = across(column_pass, 1)
-        grad = add_rounded(grad, after(along(grad, 8), mate, far_back))
-        return finish(column, mate, far_back), grad
+        result = finish(column, mate, far_back)
+        return result, add_rounded(grad, after(along(grad, 8), result))
 
 
 def place_kernel(plan, groups, panels, *refs):
@@ -361,29 +390,33 @@
     )(first, second, weight, *cots)
 
 
-def scatter_kernel(own_a, sib_a, own_sent, sib_sent, grad, *outs):
+def scatter_kernel(pieces, own_a, sib_a, own_sent, sib_sent, grad, *outs):
     turned = (((0,), (0,)), ((), ()))
-    span = own_a.shape[1]
-    *outs, grad_out = outs
-    for s, out in enumerate(outs):
+    slots, span, _ = own_a.shape
+    for s in range(slots):
         total = lax.dot_general(
             own_a[s], own_sent[:span, :], turned, preferred_element_type=jnp.float32
         ) + lax.dot_general(
             sib_a[s], sib_sent[:span, :], turned, preferred_element_type=jnp.float32
         )
-        out[...] = total.astype(out.dtype)
+        for (slot, low, high, _, _), out in zip(pieces, outs):
+            if slot == s and high > low:
+                out[: high - low, :] = total[low:high].astype(out.dtype)
     total = grad[...] + sib_sent[span:, :].astype(jnp.float32)
-    grad_out[...] = total.astype(grad_out.dtype)
-
-
-def backward_product(own_a, sib_a, own_sent, sib_sent, grad, types):
+    for (_, low, high, _, follows), out in zip(pieces, outs):
+        if follows:
+            out[high - low :, :] = total.astype(out.dtype)
+
+
+def backward_product(own_a, sib_a, own_sent, sib_sent, grad, pieces):
     slots, span, _ = own_a.shape
-    rows, width = own_sent.shape
-    outs = [like((span, width), kind) for kind in types]
-    outs.append(like((rows - span, width), jnp.bfloat16))
-    return pl.pallas_call(
-        scatter_kernel,
-        out_shape=outs,
+    half, width = grad.shape
+    return pl.pallas_call(
+        functools.partial(scatter_kernel, pieces),
+        out_shape=[
+            like((high - low + half * follows, width), kind)
+            for _, low, high, kind, follows in pieces
+        ],
         compiler_params=pltpu.CompilerParams(
             vmem_limit_bytes=limit_for(own_a, sib_a) + slots * span * width * 8
         ),
@@ -403,18 +436,17 @@
     span = groups * size
     core = lax.axis_index("blk") % 2
     plan = (Halves if Halves.fits(groups, panels) else Direct)(groups, panels)
-    types = plan.part_types()
+    slots = sum(len(batch) for batch in plan.batches)
 
     tiles = (tile_row[0, 0].T, tile_col[0, 0].T, tile_count[0, 0], tile_vals[0, 0])
     meta = jnp.concatenate([tiles[0], tiles[1], tile_count[0]])
     sib_tiles = [along(meta, 1), along(tiles[3], 1)]
-    own_a, sib_a = place_tiles(plan, len(types), [meta, tiles[3]], sib_tiles, span)
-    cots = [cotangent] + [across(cotangent, i) for i in range(1, groups)]
-    held = plan.gather(features, sib_tiles + cots[1:], [own_a])
+    own_a, sib_a = place_tiles(plan, slots, [meta, tiles[3]], sib_tiles, span)
+    cots, held = plan.gather(features, cotangent, sib_tiles)
 
     sums = ()
-    for slots in plan.batches:
-        sums = forward_product(own_a, sib_a, held, slots, sums, slots is plan.batches[-1])
+    for batch in plan.batches:
+        sums = forward_product(own_a, sib_a, held, batch, sums, batch is plan.batches[-1])
     own_part, sib_part = sums
     total = (own_part + along(sib_part, 1).astype(jnp.float32)).astype(jnp.bfloat16)
     bit = 1
@@ -426,8 +458,9 @@
     other = across(total, bit)
 
     activations, grad, sent = layer(total, other, weight, cots, groups)
-    *parts, grad = backward_product(own_a, sib_a, sent, along(sent, 1), grad, types)
-    feature_grad, grad = plan.scatter(parts, grad, size)
+    pieces = plan.pieces(size, span)
+    parts = backward_product(own_a, sib_a, sent, along(sent, 1), grad, pieces)
+    feature_grad, grad = plan.scatter(parts, size)
     mate = along(grad, 1)
     weight_grad = jnp.where(
         core == 0, jnp.concatenate([grad, mate]), jnp.concatenate([mate, grad])

time: 54.9 us -> 53.2 us (0.969)
  starting transfers between devices: 27.2 us -> 24.8 us
  waiting for transfers between devices: 19.7 us -> 20.5 us
    ppermute x7 -> x8, waiting for transfers between devices: 4.57 us -> 7.07 us  [move(): return lax.ppermute(array, BOTH, pairs)]
    ppermute x6, starting transfers between devices: 7.74 us -> 5.53 us  [across(): return lax.ppermute(array, 'rep', xor_pairs(lax.axis_size('rep'), bit))]
    ppermute x10 -> x9, waiting for transfers between devices: 7.84 us -> 6.34 us  [along(): return lax.ppermute(array, 'blk', xor_pairs(lax.axis_size('blk'), bit))]
    ppermute x7 -> x8, starting transfers between devices: 14.7 us -> 13.6 us  [move(): return lax.ppermute(array, BOTH, pairs)]
    ppermute x10 -> x9, starting transfers between devices: 4.78 us -> 5.6 us  [along(): return lax.ppermute(array, 'blk', xor_pairs(lax.axis_size('blk'), bit))]
  transfers between devices with their start and end apart: 23 -> 23, of which waited for: 12 -> 11; matrix products, arithmetic and copies ran while one was open for 2% -> 1% of each run, Pallas kernels for 4% -> 4%
where the time goes in v4:
time: 53.2 us; the launch traced here: 53 us
  starting transfers between devices  24.8 us (47%)
  waiting for transfers between devices  20.5 us (39%)
  Pallas kernels  4.12 us (8%)
  other arithmetic  1.54 us (3%)
  local copies, waits for them, and re-layouts  1.24 us (2%)
  between operations  0.83 us (2%)
    ppermute x8, starting transfers between devices, move(): return lax.ppermute(array, BOTH, pairs)  13.6 us
    ppermute x6, waiting for transfers between devices, across(): return lax.ppermute(array, 'rep', xor_pairs(lax.axis_size('rep'), bit))  7.13 us
    ppermute x8, waiting for transfers between devices, move(): return lax.ppermute(array, BOTH, pairs)  7.07 us
    ppermute x9, waiting for transfers between devices, along(): return lax.ppermute(array, 'blk', xor_pairs(lax.axis_size('blk'), bit))  6.34 us
    ppermute x9, starting transfers between devices, along(): return lax.ppermute(array, 'blk', xor_pairs(lax.axis_size('blk'), bit))  5.6 us
    ppermute x6, starting transfers between devices, across(): return lax.ppermute(array, 'rep', xor_pairs(lax.axis_size('rep'), bit))  5.53 us
    pallas_call x1, Pallas kernels, place_tiles(): pl.pallas_call(functools.partial(place_kernel, plan, lax.axis_size('rep')...  1.25 us
    unnamed x8, local copies, waits for them, and re-layouts  1.24 us
  transfers between devices with their start and end apart: 23, of which 11 were waited for; matrix products, arithmetic and copies ran while one was open for 1% of the time, Pallas kernels for 4%

profile of v4, /device:TPU:0, one launch (start us, length us, event | category | flops | bytes accessed | tf_op | source)
XLA Modules:
  0.0 53.0 jit_solution(14669953883779018741)
XLA Ops:
  0.6 0.0 copy-start.1
  0.6 0.5 collective-permute-start.1
  1.2 3.7 %collective-permute-start.5 = (bf16[128,256]{1,0:T(8,128)(2,1)}, bf16[128,256]{1,0:T(8,128)(2,1)S(1)}, u32[]{:S(2)}, u32[]{:S(2)}) collective-permute-start(bf16[128,256]{1,0:T(8,128)(2,1)} %first.1), channel_id=1, source_target_pairs={{0,8},{1,9},{2,10},{3,11},{4,12},{5,13},{6,14},{7,15},{8,0},{9,1},... | collective-permute-start | bytes 196616 | tf_op jit(solution)/shard_map/ppermute | solution.py:56
  4.8 1.5 %collective-permute-start.2 = (bf16[128,256]{1,0:T(8,128)(2,1)}, bf16[128,256]{1,0:T(8,128)(2,1)S(1)}, u32[]{:S(2)}, u32[]{:S(2)}) collective-permute-start(bf16[128,256]{1,0:T(8,128)(2,1)} %first.1), channel_id=1, source_target_pairs={{0,16},{16,0},{1,17},{17,1},{2,18},{18,2},{3,19},{19,3},{4,20},{20... | collective-permute-start | bytes 196616 | tf_op jit(solution)/shard_map/ppermute | solution.py:60
  6.3 0.5 %collective-permute-start.6 = (bf16[128,256]{1,0:T(8,128)(2,1)}, bf16[128,256]{1,0:T(8,128)(2,1)S(1)}, u32[]{:S(2)}, u32[]{:S(2)}) collective-permute-start(bf16[128,256]{1,0:T(8,128)(2,1)} %refs_0_.1), channel_id=1, source_target_pairs={{0,16},{16,0},{1,17},{17,1},{2,18},{18,2},{3,19},{19,3},{4,20},{20... | collective-permute-start | bytes 196616 | tf_op jit(solution)/shard_map/ppermute | solution.py:60
  6.9 0.7 %pad_add_fusion.refs_0_ = s32[9,8]{1,0:T(8,128)S(1)} fusion(s32[1,8]{1,0:T(1,128)} %bitcast.12, s32[4,8]{1,0:T(4,128)} %bitcast.10, s32[4,8]{1,0:T(4,128)} %bitcast.11), kind=kLoop, calls=%fused_computation.7 | loop fusion | flops 144 | bytes 576 | tf_op jit(solution)/shard_map/concatenate | solution.py:442
  7.6 0.0 collective-permute-start
  7.6 2.1 %collective-permute-done.2.second = bf16[128,256]{1,0:T(8,128)(2,1)S(1)} collective-permute-done((bf16[128,256]{1,0:T(8,128)(2,1)}, bf16[128,256]{1,0:T(8,128)(2,1)S(1)}, u32[]{:S(2)}, u32[]{:S(2)}) %collective-permute-start.2) | collective-permute-done | bytes 65568 | tf_op jit(solution)/shard_map/ppermute | solution.py:60
  9.7 0.0 copy-done.1
  9.7 1.6 %collective-permute-start.3 = (bf16[256,256]{1,0:T(8,128)(2,1)S(1)}, bf16[256,256]{1,0:T(8,128)(2,1)S(1)}, u32[]{:S(2)}, u32[]{:S(2)}) collective-permute-start(bf16[256,256]{1,0:T(8,128)(2,1)S(1)} %stack.1.refs_0_), channel_id=1, source_target_pairs={{0,4},{1,5},{2,6},{3,7},{4,8},{5,9},{6,10},{7,11},{8,12},{9,13},{1... | collective-permute-start | bytes 393224 | tf_op jit(solution)/shard_map/ppermute | solution.py:56
  11.3 0.0 collective-permute-done.refs_2_
  11.3 1.0 %collective-permute-start.4 = (bf16[256,256]{1,0:T(8,128)(2,1)S(1)}, bf16[256,256]{1,0:T(8,128)(2,1)S(1)}, u32[]{:S(2)}, u32[]{:S(2)}) collective-permute-start(bf16[256,256]{1,0:T(8,128)(2,1)S(1)} %stack.1.refs_0_), channel_id=1, source_target_pairs={{0,6},{1,7},{2,4},{3,5},{4,10},{5,11},{6,8},{7,9},{8,14},{9,15},{1... | collective-permute-start | bytes 393224 | tf_op jit(solution)/shard_map/ppermute | solution.py:56
  12.4 0.0 collective-permute-done.6.refs_1_
  12.4 0.0 collective-permute-done.5.refs_2_
  12.4 0.0 collective-permute-done.1.refs_3_
  12.4 0.6 %collective-permute-start.8 = (bf16[128,256]{1,0:T(8,128)(2,1)S(1)}, bf16[128,256]{1,0:T(8,128)(2,1)S(1)}, u32[]{:S(2)}, u32[]{:S(2)}) collective-permute-start(bf16[128,256]{1,0:T(8,128)(2,1)S(1)} %get-tuple-element.48), channel_id=1, source_target_pairs={{0,2},{1,3},{2,0},{3,1},{4,6},{5,7},{6,4},{7,5},{8,10},{9,11},{10,... | collective-permute-start | bytes 196616 | tf_op jit(solution)/shard_map/ppermute | solution.py:64
  13.0 2.8 %collective-permute-start.9 = (bf16[128,256]{1,0:T(8,128)(2,1)S(1)}, bf16[128,256]{1,0:T(8,128)(2,1)S(1)}, u32[]{:S(2)}, u32[]{:S(2)}) collective-permute-start(bf16[128,256]{1,0:T(8,128)(2,1)S(1)} %get-tuple-element.47), channel_id=1, source_target_pairs={{0,18},{1,19},{2,16},{3,17},{4,22},{5,23},{6,20},{7,21},{8,26},{9,... | collective-permute-start | bytes 196616 | tf_op jit(solution)/shard_map/ppermute | solution.py:56
  15.8 0.2 collective-permute-start.7
  16.0 0.0 copy-start
  16.0 1.2 %copy-done = bf16[1,1,8,4,128,128]{5,4,3,2,1,0:T(8,128)(2,1)S(1)} copy-done((bf16[1,1,8,4,128,128]{5,4,3,2,1,0:T(8,128)(2,1)S(1)}, bf16[1,1,8,4,128,128]{5,4,3,2,1,0:T(8,128)(2,1)}, u32[]{:S(2)}) %copy-start) | copy-done | bytes 1048600
  17.2 1.3 %place_tiles.1 = (bf16[5,256,256]{2,1,0:T(8,128)(2,1)S(1)}, bf16[5,256,256]{2,1,0:T(8,128)(2,1)S(1)}) custom-call(s32[9,8]{1,0:T(8,128)S(1)} %pad_add_fusion.refs_0_, bf16[8,4,128,128]{3,2,1,0:T(8,128)(2,1)S(1)} %bitcast.9, s32[9,8]{1,0:T(8,128)S(1)} %collective-permute-done.refs_2_, bf16[8,4,128,128]{3,2,1,0:T(8,128)(2,1)S(1)} %collective-permute-done.1.refs_3_), custom_call_target="tpu_custom_call" | custom-call | bytes 2621440 | tf_op jit(solution)/shard_map/place_tiles/pallas_call | solution.py:285
  18.4 0.0 collective-permute-done.3.refs_1_
  18.5 1.2 %collective-permute-done.4.refs_2_ = bf16[256,256]{1,0:T(8,128)(2,1)S(1)} collective-permute-done((bf16[256,256]{1,0:T(8,128)(2,1)S(1)}, bf16[256,256]{1,0:T(8,128)(2,1)S(1)}, u32[]{:S(2)}, u32[]{:S(2)}) %collective-permute-start.4) | collective-permute-done | bytes 131104 | tf_op jit(solution)/shard_map/ppermute | solution.py:56
  19.7 0.4 forward_product.2
  20.1 0.0 collective-permute-done.8.refs_4_
  20.1 0.0 collective-permute-done.9.refs_5_
  20.1 0.0 collective-permute-done.7.refs_3_
  20.1 0.3 forward_product.3
  20.4 0.1 collective-permute-start.10
  20.5 1.3 %collective-permute-done.10 = bf16[256,256]{1,0:T(8,128)(2,1)S(1)} collective-permute-done((bf16[256,256]{1,0:T(8,128)(2,1)S(1)}, bf16[256,256]{1,0:T(8,128)(2,1)S(1)}, u32[]{:S(2)}, u32[]{:S(2)}) %collective-permute-start.10) | collective-permute-done | bytes 131104 | tf_op jit(solution)/shard_map/ppermute | solution.py:64
  21.8 0.0 copy-start.2
  21.8 0.0 copy-start.3
  21.9 0.7 %collective-permute-start.11 = (bf16[256,256]{1,0:T(8,128)(2,1)S(1)}, bf16[256,256]{1,0:T(8,128)(2,1)S(1)}, u32[]{:S(2)}, u32[]{:S(2)}) collective-permute-start(bf16[256,256]{1,0:T(8,128)(2,1)S(1)} %add_convert_fusion.first), channel_id=1, source_target_pairs={{0,16},{16,0},{1,17},{17,1},{2,18},{18,2},{3,19},{19,3},{4,20},{20... | collective-permute-start | bytes 393224 | tf_op jit(solution)/shard_map/ppermute | solution.py:60
  22.6 4.9 %collective-permute-done.11.second = bf16[256,256]{1,0:T(8,128)(2,1)S(1)} collective-permute-done((bf16[256,256]{1,0:T(8,128)(2,1)S(1)}, bf16[256,256]{1,0:T(8,128)(2,1)S(1)}, u32[]{:S(2)}, u32[]{:S(2)}) %collective-permute-start.11) | collective-permute-done | bytes 131104 | tf_op jit(solution)/shard_map/ppermute | solution.py:60
  27.5 0.0 copy-done.2
  27.5 0.0 copy-done.3
  27.5 0.9 %layer.1 = (bf16[128,256]{1,0:T(8,128)(2,1)}, f32[128,256]{1,0:T(8,128)S(1)}, bf16[384,256]{1,0:T(8,128)(2,1)S(1)}) custom-call(bf16[256,256]{1,0:T(8,128)(2,1)S(1)} %add_convert_fusion.first, bf16[256,256]{1,0:T(8,128)(2,1)S(1)} %collective-permute-done.11.second, bf16[256,256]{1,0:T(8,128)(2,1)S(1)} %copy-done.2, bf16[128,256]{1,0:T(8,128)(2,1)S(1)} %copy-done.3, ...), custom_call_target="tpu_custom_call" | custom-call | flops 100663296 | bytes 524288 | tf_op jit(solution)/shard_map/layer/pallas_call | solution.py:375
  28.4 0.0 collective-permute-start.12
  28.4 1.4 %collective-permute-done.12.sib_sent = bf16[384,256]{1,0:T(8,128)(2,1)S(1)} collective-permute-done((bf16[384,256]{1,0:T(8,128)(2,1)S(1)}, bf16[384,256]{1,0:T(8,128)(2,1)S(1)}, u32[]{:S(2)}, u32[]{:S(2)}) %collective-permute-start.12) | collective-permute-done | bytes 196640 | tf_op jit(solution)/shard_map/ppermute | solution.py:64
  29.8 0.6 %backward_product.1 = (f32[256,256]{1,0:T(8,128)S(1)}, f32[128,256]{1,0:T(8,128)S(1)}, bf16[128,256]{1,0:T(8,128)(2,1)S(1)}, bf16[256,256]{1,0:T(8,128)(2,1)S(1)...) custom-call(bf16[5,256,256]{2,1,0:T(8,128)(2,1)S(1)} %get-tuple-element.25.own_a, ...), custom_call_target="tpu_custom_call" | custom-call | flops 335544320 | bytes 1310720 | tf_op jit(solution)/shard_map/backward_product/pallas_call | solution.py:414
  30.4 1.6 %collective-permute-start.14 = (bf16[256,256]{1,0:T(8,128)(2,1)S(1)}, bf16[256,256]{1,0:T(8,128)(2,1)S(1)}, u32[]{:S(2)}, u32[]{:S(2)}) collective-permute-start(bf16[256,256]{1,0:T(8,128)(2,1)S(1)} %get-tuple-element.37.side), channel_id=1, source_target_pairs={{0,2},{1,3},{2,0},{3,1},{4,6},{5,7},{6,4},{7,5},{8,10},{9,11},{10,... | collective-permute-start | bytes 393224 | tf_op jit(solution)/shard_map/ppermute | solution.py:64
  32.0 1.8 %collective-permute-start.18 = (bf16[256,256]{1,0:T(8,128)(2,1)S(1)}, bf16[256,256]{1,0:T(8,128)(2,1)S(1)}, u32[]{:S(2)}, u32[]{:S(2)}) collective-permute-start(bf16[256,256]{1,0:T(8,128)(2,1)S(1)} %get-tuple-element.41), channel_id=1, source_target_pairs={{4,0},{5,1},{6,2},{7,3},{8,4},{9,5},{10,6},{11,7},{12,8},{13,9},{1... | collective-permute-start | bytes 393224 | tf_op jit(solution)/shard_map/ppermute | solution.py:56
  33.8 1.3 %collective-permute-start.19 = (bf16[256,256]{1,0:T(8,128)(2,1)S(1)}, bf16[256,256]{1,0:T(8,128)(2,1)S(1)}, u32[]{:S(2)}, u32[]{:S(2)}) collective-permute-start(bf16[256,256]{1,0:T(8,128)(2,1)S(1)} %get-tuple-element.42), channel_id=1, source_target_pairs={{6,0},{7,1},{4,2},{5,3},{10,4},{11,5},{8,6},{9,7},{14,8},{15,9},{1... | collective-permute-start | bytes 393224 | tf_op jit(solution)/shard_map/ppermute | solution.py:56
  35.0 0.3 collective-permute-start.15
  35.3 1.9 %collective-permute-start.13 = (bf16[128,256]{1,0:T(8,128)(2,1)S(1)}, bf16[128,256]{1,0:T(8,128)(2,1)S(1)}, u32[]{:S(2)}, u32[]{:S(2)}) collective-permute-start(bf16[128,256]{1,0:T(8,128)(2,1)S(1)} %get-tuple-element.36), channel_id=1, source_target_pairs={{0,16},{16,0},{1,17},{17,1},{2,18},{18,2},{3,19},{19,3},{4,20},{20... | collective-permute-start | bytes 196616 | tf_op jit(solution)/shard_map/ppermute | solution.py:60
  37.1 3.8 %collective-permute-done.15.corner = bf16[128,256]{1,0:T(8,128)(2,1)S(1)} collective-permute-done((bf16[128,256]{1,0:T(8,128)(2,1)S(1)}, bf16[128,256]{1,0:T(8,128)(2,1)S(1)}, u32[]{:S(2)}, u32[]{:S(2)}) %collective-permute-start.15) | collective-permute-done | bytes 65568 | tf_op jit(solution)/shard_map/ppermute | solution.py:56
  40.9 0.0 collective-permute-done.13.far_mate
  40.9 0.0 collective-permute-done.14.came
  41.0 1.6 %collective-permute-start.16 = (bf16[128,256]{1,0:T(8,128)(2,1)S(1)}, bf16[128,256]{1,0:T(8,128)(2,1)S(1)}, u32[]{:S(2)}, u32[]{:S(2)}) collective-permute-start(bf16[128,256]{1,0:T(8,128)(2,1)S(1)} %get-tuple-element.39), channel_id=1, source_target_pairs={{0,4},{1,5},{2,6},{3,7},{4,0},{5,1},{6,2},{7,3},{8,12},{9,13},{10,... | collective-permute-start | bytes 196616 | tf_op jit(solution)/shard_map/ppermute | solution.py:64
  42.6 0.0 collective-permute-done.18.ahead
  42.6 0.0 collective-permute-done.19.cross
  42.6 0.1 add_column.1
  42.7 0.8 %collective-permute-start.20 = (bf16[128,256]{1,0:T(8,128)(2,1)S(1)}, bf16[128,256]{1,0:T(8,128)(2,1)S(1)}, u32[]{:S(2)}, u32[]{:S(2)}) collective-permute-start(bf16[128,256]{1,0:T(8,128)(2,1)S(1)} %get-tuple-element.44), channel_id=1, source_target_pairs={{0,16},{16,0},{1,17},{17,1},{2,18},{18,2},{3,19},{19,3},{4,20},{20... | collective-permute-start | bytes 196616 | tf_op jit(solution)/shard_map/ppermute | solution.py:60
  43.5 1.2 %collective-permute-start.21 = (bf16[128,256]{1,0:T(8,128)(2,1)S(1)}, bf16[128,256]{1,0:T(8,128)(2,1)S(1)}, u32[]{:S(2)}, u32[]{:S(2)}) collective-permute-start(bf16[128,256]{1,0:T(8,128)(2,1)S(1)} %get-tuple-element.45), channel_id=1, source_target_pairs={{8,0},{9,1},{10,2},{11,3},{12,4},{13,5},{14,6},{15,7},{0,8},{1,9},... | collective-permute-start | bytes 196616 | tf_op jit(solution)/shard_map/ppermute | solution.py:56
  44.6 1.1 %collective-permute-done.16 = bf16[128,256]{1,0:T(8,128)(2,1)S(1)} collective-permute-done((bf16[128,256]{1,0:T(8,128)(2,1)S(1)}, bf16[128,256]{1,0:T(8,128)(2,1)S(1)}, u32[]{:S(2)}, u32[]{:S(2)}) %collective-permute-start.16) | collective-permute-done | bytes 65568 | tf_op jit(solution)/shard_map/ppermute | solution.py:64
  45.7 1.1 %collective-permute-start.17 = (bf16[128,256]{1,0:T(8,128)(2,1)S(1)}, bf16[128,256]{1,0:T(8,128)(2,1)S(1)}, u32[]{:S(2)}, u32[]{:S(2)}) collective-permute-start(bf16[128,256]{1,0:T(8,128)(2,1)S(1)} %add_convert_fusion.2), channel_id=1, source_target_pairs={{0,8},{1,9},{2,10},{3,11},{4,12},{5,13},{6,14},{7,15},{8,0},{9,1},... | collective-permute-start | bytes 196616 | tf_op jit(solution)/shard_map/ppermute | solution.py:64
  46.9 0.1 collective-permute-done.20.second
  47.0 2.0 %collective-permute-done.21.third = bf16[128,256]{1,0:T(8,128)(2,1)S(1)} collective-permute-done((bf16[128,256]{1,0:T(8,128)(2,1)S(1)}, bf16[128,256]{1,0:T(8,128)(2,1)S(1)}, u32[]{:S(2)}, u32[]{:S(2)}) %collective-permute-start.21) | collective-permute-done | bytes 65568 | tf_op jit(solution)/shard_map/ppermute | solution.py:56
  49.0 0.7 %finish.1 = bf16[128,256]{1,0:T(8,128)(2,1)} custom-call(f32[128,256]{1,0:T(8,128)S(1)} %get-tuple-element.43.first, bf16[128,256]{1,0:T(8,128)(2,1)S(1)} %collective-permute-done.20.second, bf16[128,256]{1,0:T(8,128)(2,1)S(1)} %collective-permute-done.21.third), custom_call_target="tpu_custom_call" | custom-call | flops 65536 | bytes 262144 | tf_op jit(solution)/shard_map/finish/pallas_call | solution.py:163
  49.7 1.3 %collective-permute-done.17 = bf16[128,256]{1,0:T(8,128)(2,1)S(1)} collective-permute-done((bf16[128,256]{1,0:T(8,128)(2,1)S(1)}, bf16[128,256]{1,0:T(8,128)(2,1)S(1)}, u32[]{:S(2)}, u32[]{:S(2)}) %collective-permute-start.17) | collective-permute-done | bytes 65568 | tf_op jit(solution)/shard_map/ppermute | solution.py:64
  51.0 0.1 collective-permute-start.22
  51.1 1.2 %collective-permute-done.22 = bf16[128,256]{1,0:T(8,128)(2,1)S(1)} collective-permute-done((bf16[128,256]{1,0:T(8,128)(2,1)S(1)}, bf16[128,256]{1,0:T(8,128)(2,1)S(1)}, u32[]{:S(2)}, u32[]{:S(2)}) %collective-permute-start.22) | collective-permute-done | bytes 65568 | tf_op jit(solution)/shard_map/ppermute | solution.py:64
  52.3 0.7 %convert_multiply_fusion = f32[256,256]{1,0:T(8,128)} fusion(bf16[128,256]{1,0:T(8,128)(2,1)S(1)} %collective-permute-done.22, bf16[128,256]{1,0:T(8,128)(2,1)S(1)} %add_convert_fusion.1, pred[]{:T(512)S(6)} %eq.10), kind=kLoop, calls=%fused_computation | loop fusion | flops 720896 | bytes 393217 | tf_op jit(solution)/shard_map/mul | solution.py:465
  (6 shorter events, 0.1 us)
Async XLA Ops:
  0.6 9.1 %copy-start.1 = (bf16[128,256]{1,0:T(8,128)(2,1)S(1)}, bf16[128,256]{1,0:T(8,128)(2,1)}, u32[]{:S(2)}) copy-start(bf16[128,256]{1,0:T(8,128)(2,1)} %first.1) | copy-start | bytes 196612
  0.6 11.7 %collective-permute-start.1 = (bf16[8,4,128,128]{3,2,1,0:T(8,128)(2,1)}, bf16[8,4,128,128]{3,2,1,0:T(8,128)(2,1)S(1)}, u32[]{:S(2)}, u32[]{:S(2)}) collective-permute-start(bf16[8,4,128,128]{3,2,1,0:T(8,128)(2,1)} %bitcast.8), channel_id=1, source_target_pairs={{0,1},{1,0},{2,3},{3,2},{4,5},{5,4},{6,7},{7,6},{8,9},{9,8},{10,11... | collective-permute-start | bytes 3145736 | tf_op jit(solution)/shard_map/ppermute | solution.py:64
  1.2 11.2 %collective-permute-start.5 = (bf16[128,256]{1,0:T(8,128)(2,1)}, bf16[128,256]{1,0:T(8,128)(2,1)S(1)}, u32[]{:S(2)}, u32[]{:S(2)}) collective-permute-start(bf16[128,256]{1,0:T(8,128)(2,1)} %first.1), channel_id=1, source_target_pairs={{0,8},{1,9},{2,10},{3,11},{4,12},{5,13},{6,14},{7,15},{8,0},{9,1},... | collective-permute-start | bytes 196616 | tf_op jit(solution)/shard_map/ppermute | solution.py:56
  4.8 4.9 %collective-permute-start.2 = (bf16[128,256]{1,0:T(8,128)(2,1)}, bf16[128,256]{1,0:T(8,128)(2,1)S(1)}, u32[]{:S(2)}, u32[]{:S(2)}) collective-permute-start(bf16[128,256]{1,0:T(8,128)(2,1)} %first.1), channel_id=1, source_target_pairs={{0,16},{16,0},{1,17},{17,1},{2,18},{18,2},{3,19},{19,3},{4,20},{20... | collective-permute-start | bytes 196616 | tf_op jit(solution)/shard_map/ppermute | solution.py:60
  6.3 6.0 %collective-permute-start.6 = (bf16[128,256]{1,0:T(8,128)(2,1)}, bf16[128,256]{1,0:T(8,128)(2,1)S(1)}, u32[]{:S(2)}, u32[]{:S(2)}) collective-permute-start(bf16[128,256]{1,0:T(8,128)(2,1)} %refs_0_.1), channel_id=1, source_target_pairs={{0,16},{16,0},{1,17},{17,1},{2,18},{18,2},{3,19},{19,3},{4,20},{20... | collective-permute-start | bytes 196616 | tf_op jit(solution)/shard_map/ppermute | solution.py:60
  7.6 3.8 %collective-permute-start = (s32[9,8]{1,0:T(8,128)S(1)}, s32[9,8]{1,0:T(8,128)S(1)}, u32[]{:S(2)}, u32[]{:S(2)}) collective-permute-start(s32[9,8]{1,0:T(8,128)S(1)} %pad_add_fusion.refs_0_), channel_id=1, source_target_pairs={{0,1},{1,0},{2,3},{3,2},{4,5},{5,4},{6,7},{7,6},{8,9},{9,8},{10,11... | collective-permute-start | bytes 872 | tf_op jit(solution)/shard_map/ppermute | solution.py:64
  9.7 8.7 %collective-permute-start.3 = (bf16[256,256]{1,0:T(8,128)(2,1)S(1)}, bf16[256,256]{1,0:T(8,128)(2,1)S(1)}, u32[]{:S(2)}, u32[]{:S(2)}) collective-permute-start(bf16[256,256]{1,0:T(8,128)(2,1)S(1)} %stack.1.refs_0_), channel_id=1, source_target_pairs={{0,4},{1,5},{2,6},{3,7},{4,8},{5,9},{6,10},{7,11},{8,12},{9,13},{1... | collective-permute-start | bytes 393224 | tf_op jit(solution)/shard_map/ppermute | solution.py:56
  11.3 8.4 %collective-permute-start.4 = (bf16[256,256]{1,0:T(8,128)(2,1)S(1)}, bf16[256,256]{1,0:T(8,128)(2,1)S(1)}, u32[]{:S(2)}, u32[]{:S(2)}) collective-permute-start(bf16[256,256]{1,0:T(8,128)(2,1)S(1)} %stack.1.refs_0_), channel_id=1, source_target_pairs={{0,6},{1,7},{2,4},{3,5},{4,10},{5,11},{6,8},{7,9},{8,14},{9,15},{1... | collective-permute-start | bytes 393224 | tf_op jit(solution)/shard_map/ppermute | solution.py:56
  12.4 7.7 %collective-permute-start.8 = (bf16[128,256]{1,0:T(8,128)(2,1)S(1)}, bf16[128,256]{1,0:T(8,128)(2,1)S(1)}, u32[]{:S(2)}, u32[]{:S(2)}) collective-permute-start(bf16[128,256]{1,0:T(8,128)(2,1)S(1)} %get-tuple-element.48), channel_id=1, source_target_pairs={{0,2},{1,3},{2,0},{3,1},{4,6},{5,7},{6,4},{7,5},{8,10},{9,11},{10,... | collective-permute-start | bytes 196616 | tf_op jit(solution)/shard_map/ppermute | solution.py:64
  13.0 7.1 %collective-permute-start.9 = (bf16[128,256]{1,0:T(8,128)(2,1)S(1)}, bf16[128,256]{1,0:T(8,128)(2,1)S(1)}, u32[]{:S(2)}, u32[]{:S(2)}) collective-permute-start(bf16[128,256]{1,0:T(8,128)(2,1)S(1)} %get-tuple-element.47), channel_id=1, source_target_pairs={{0,18},{1,19},{2,16},{3,17},{4,22},{5,23},{6,20},{7,21},{8,26},{9,... | collective-permute-start | bytes 196616 | tf_op jit(solution)/shard_map/ppermute | solution.py:56
  15.8 4.3 %collective-permute-start.7 = (bf16[128,256]{1,0:T(8,128)(2,1)S(1)}, bf16[128,256]{1,0:T(8,128)(2,1)S(1)}, u32[]{:S(2)}, u32[]{:S(2)}) collective-permute-start(bf16[128,256]{1,0:T(8,128)(2,1)S(1)} %collective-permute-done.5.refs_2_), channel_id=1, source_target_pairs={{0,16},{16,0},{1,17},{17,1},{2,18},{18,2},{3,19},{19,3},{4,20},{20... | collective-permute-start | bytes 196616 | tf_op jit(solution)/shard_map/ppermute | solution.py:60
  16.0 1.2 %copy-start = (bf16[1,1,8,4,128,128]{5,4,3,2,1,0:T(8,128)(2,1)S(1)}, bf16[1,1,8,4,128,128]{5,4,3,2,1,0:T(8,128)(2,1)}, u32[]{:S(2)}) copy-start(bf16[1,1,8,4,128,128]{5,4,3,2,1,0:T(8,128)(2,1)} %param.13) | copy-start | bytes 3145732
  20.4 1.4 %collective-permute-start.10 = (bf16[256,256]{1,0:T(8,128)(2,1)S(1)}, bf16[256,256]{1,0:T(8,128)(2,1)S(1)}, u32[]{:S(2)}, u32[]{:S(2)}) collective-permute-start(bf16[256,256]{1,0:T(8,128)(2,1)S(1)} %get-tuple-element.31), channel_id=1, source_target_pairs={{0,1},{1,0},{2,3},{3,2},{4,5},{5,4},{6,7},{7,6},{8,9},{9,8},{10,11... | collective-permute-start | bytes 393224 | tf_op jit(solution)/shard_map/ppermute | solution.py:64
  21.8 5.7 %copy-start.2 = (bf16[256,256]{1,0:T(8,128)(2,1)S(1)}, bf16[256,256]{1,0:T(8,128)(2,1)}, u32[]{:S(2)}) copy-start(bf16[256,256]{1,0:T(8,128)(2,1)} %weight.1) | copy-start | bytes 393220
  21.8 5.7 %copy-start.3 = (bf16[128,256]{1,0:T(8,128)(2,1)S(1)}, bf16[128,256]{1,0:T(8,128)(2,1)}, u32[]{:S(2)}) copy-start(bf16[128,256]{1,0:T(8,128)(2,1)} %refs_0_.1) | copy-start | bytes 196612
  21.9 5.6 %collective-permute-start.11 = (bf16[256,256]{1,0:T(8,128)(2,1)S(1)}, bf16[256,256]{1,0:T(8,128)(2,1)S(1)}, u32[]{:S(2)}, u32[]{:S(2)}) collective-permute-start(bf16[256,256]{1,0:T(8,128)(2,1)S(1)} %add_convert_fusion.first), channel_id=1, source_target_pairs={{0,16},{16,0},{1,17},{17,1},{2,18},{18,2},{3,19},{19,3},{4,20},{20... | collective-permute-start | bytes 393224 | tf_op jit(solution)/shard_map/ppermute | solution.py:60
  28.4 1.4 %collective-permute-start.12 = (bf16[384,256]{1,0:T(8,128)(2,1)S(1)}, bf16[384,256]{1,0:T(8,128)(2,1)S(1)}, u32[]{:S(2)}, u32[]{:S(2)}) collective-permute-start(bf16[384,256]{1,0:T(8,128)(2,1)S(1)} %get-tuple-element.33.own_sent), channel_id=1, source_target_pairs={{0,1},{1,0},{2,3},{3,2},{4,5},{5,4},{6,7},{7,6},{8,9},{9,8},{10,11... | collective-permute-start | bytes 589832 | tf_op jit(solution)/shard_map/ppermute | solution.py:64
  30.4 10.6 %collective-permute-start.14 = (bf16[256,256]{1,0:T(8,128)(2,1)S(1)}, bf16[256,256]{1,0:T(8,128)(2,1)S(1)}, u32[]{:S(2)}, u32[]{:S(2)}) collective-permute-start(bf16[256,256]{1,0:T(8,128)(2,1)S(1)} %get-tuple-element.37.side), channel_id=1, source_target_pairs={{0,2},{1,3},{2,0},{3,1},{4,6},{5,7},{6,4},{7,5},{8,10},{9,11},{10,... | collective-permute-start | bytes 393224 | tf_op jit(solution)/shard_map/ppermute | solution.py:64
  32.0 10.7 %collective-permute-start.18 = (bf16[256,256]{1,0:T(8,128)(2,1)S(1)}, bf16[256,256]{1,0:T(8,128)(2,1)S(1)}, u32[]{:S(2)}, u32[]{:S(2)}) collective-permute-start(bf16[256,256]{1,0:T(8,128)(2,1)S(1)} %get-tuple-element.41), channel_id=1, source_target_pairs={{4,0},{5,1},{6,2},{7,3},{8,4},{9,5},{10,6},{11,7},{12,8},{13,9},{1... | collective-permute-start | bytes 393224 | tf_op jit(solution)/shard_map/ppermute | solution.py:56
  33.8 8.9 %collective-permute-start.19 = (bf16[256,256]{1,0:T(8,128)(2,1)S(1)}, bf16[256,256]{1,0:T(8,128)(2,1)S(1)}, u32[]{:S(2)}, u32[]{:S(2)}) collective-permute-start(bf16[256,256]{1,0:T(8,128)(2,1)S(1)} %get-tuple-element.42), channel_id=1, source_target_pairs={{6,0},{7,1},{4,2},{5,3},{10,4},{11,5},{8,6},{9,7},{14,8},{15,9},{1... | collective-permute-start | bytes 393224 | tf_op jit(solution)/shard_map/ppermute | solution.py:56
  35.0 5.9 %collective-permute-start.15 = (bf16[128,256]{1,0:T(8,128)(2,1)S(1)}, bf16[128,256]{1,0:T(8,128)(2,1)S(1)}, u32[]{:S(2)}, u32[]{:S(2)}) collective-permute-start(bf16[128,256]{1,0:T(8,128)(2,1)S(1)} %get-tuple-element.38), channel_id=1, source_target_pairs={{18,0},{19,1},{16,2},{17,3},{22,4},{23,5},{20,6},{21,7},{26,8},{27... | collective-permute-start | bytes 196616 | tf_op jit(solution)/shard_map/ppermute | solution.py:56
  35.3 5.7 %collective-permute-start.13 = (bf16[128,256]{1,0:T(8,128)(2,1)S(1)}, bf16[128,256]{1,0:T(8,128)(2,1)S(1)}, u32[]{:S(2)}, u32[]{:S(2)}) collective-permute-start(bf16[128,256]{1,0:T(8,128)(2,1)S(1)} %get-tuple-element.36), channel_id=1, source_target_pairs={{0,16},{16,0},{1,17},{17,1},{2,18},{18,2},{3,19},{19,3},{4,20},{20... | collective-permute-start | bytes 196616 | tf_op jit(solution)/shard_map/ppermute | solution.py:60
  41.0 4.7 %collective-permute-start.16 = (bf16[128,256]{1,0:T(8,128)(2,1)S(1)}, bf16[128,256]{1,0:T(8,128)(2,1)S(1)}, u32[]{:S(2)}, u32[]{:S(2)}) collective-permute-start(bf16[128,256]{1,0:T(8,128)(2,1)S(1)} %get-tuple-element.39), channel_id=1, source_target_pairs={{0,4},{1,5},{2,6},{3,7},{4,0},{5,1},{6,2},{7,3},{8,12},{9,13},{10,... | collective-permute-start | bytes 196616 | tf_op jit(solution)/shard_map/ppermute | solution.py:64
  42.7 4.3 %collective-permute-start.20 = (bf16[128,256]{1,0:T(8,128)(2,1)S(1)}, bf16[128,256]{1,0:T(8,128)(2,1)S(1)}, u32[]{:S(2)}, u32[]{:S(2)}) collective-permute-start(bf16[128,256]{1,0:T(8,128)(2,1)S(1)} %get-tuple-element.44), channel_id=1, source_target_pairs={{0,16},{16,0},{1,17},{17,1},{2,18},{18,2},{3,19},{19,3},{4,20},{20... | collective-permute-start | bytes 196616 | tf_op jit(solution)/shard_map/ppermute | solution.py:60
  43.5 5.6 %collective-permute-start.21 = (bf16[128,256]{1,0:T(8,128)(2,1)S(1)}, bf16[128,256]{1,0:T(8,128)(2,1)S(1)}, u32[]{:S(2)}, u32[]{:S(2)}) collective-permute-start(bf16[128,256]{1,0:T(8,128)(2,1)S(1)} %get-tuple-element.45), channel_id=1, source_target_pairs={{8,0},{9,1},{10,2},{11,3},{12,4},{13,5},{14,6},{15,7},{0,8},{1,9},... | collective-permute-start | bytes 196616 | tf_op jit(solution)/shard_map/ppermute | solution.py:56
  45.7 5.2 %collective-permute-start.17 = (bf16[128,256]{1,0:T(8,128)(2,1)S(1)}, bf16[128,256]{1,0:T(8,128)(2,1)S(1)}, u32[]{:S(2)}, u32[]{:S(2)}) collective-permute-start(bf16[128,256]{1,0:T(8,128)(2,1)S(1)} %add_convert_fusion.2), channel_id=1, source_target_pairs={{0,8},{1,9},{2,10},{3,11},{4,12},{5,13},{6,14},{7,15},{8,0},{9,1},... | collective-permute-start | bytes 196616 | tf_op jit(solution)/shard_map/ppermute | solution.py:64
  51.0 1.3 %collective-permute-start.22 = (bf16[128,256]{1,0:T(8,128)(2,1)S(1)}, bf16[128,256]{1,0:T(8,128)(2,1)S(1)}, u32[]{:S(2)}, u32[]{:S(2)}) collective-permute-start(bf16[128,256]{1,0:T(8,128)(2,1)S(1)} %add_convert_fusion.1), channel_id=1, source_target_pairs={{0,1},{1,0},{2,3},{3,2},{4,5},{5,4},{6,7},{7,6},{8,9},{9,8},{10,11... | collective-permute-start | bytes 196616 | tf_op jit(solution)/shard_map/ppermute | solution.py:64

commit v5 on v4

--- a/solution.py
+++ b/solution.py
@@ -115,13 +115,10 @@
     return (lax.axis_index("blk") // 2) % 2 == lax.axis_index("rep")
 
 
-def far_kernel(far, far_mate, came, corner, side, far_out, grad_out):
-    size = far_out.shape[0]
-    slant = jnp.where(sends_own(), corner[...], came[:size, :]).astype(jnp.float32)
-    total = far[...] + far_mate[...].astype(jnp.float32) + slant
-    far_out[...] = total.astype(far_out.dtype)
-    grad = side[size:, :].astype(jnp.float32) + came[size:, :].astype(jnp.float32)
-    grad_out[...] = grad.astype(grad_out.dtype)
+def far_kernel(far, far_mate, came, corner, out):
+    size = out.shape[0]
+    late = jnp.where(sends_own(), corner[...], came[:size, :]).astype(jnp.float32)
+    out[...] = (far[...] + far_mate[...].astype(jnp.float32) + late).astype(out.dtype)
 
 
 def column_kernel(own, came, corner, ahead, cross, keep_out, pass_out):
@@ -143,10 +140,22 @@
     )(*arrays)
 
 
-def sort_far(far, far_mate, came, corner, side):
-    rows, width = came.shape
-    outs = [like(far.shape, came.dtype), like((rows - far.shape[0], width), came.dtype)]
-    return local_call(far_kernel, "sort_far", outs, far, far_mate, came, corner, side)
+def tails_kernel(first, second, out):
+    size = first.shape[0] - out.shape[0]
+    total = first[size:, :].astype(jnp.float32) + second[size:, :].astype(jnp.float32)
+    out[...] = total.astype(out.dtype)
+
+
+def add_tails(first, second, size):
+    rows, width = first.shape
+    return local_call(
+        tails_kernel, "add_tails", like((rows - size, width), first.dtype), first, second
+    )
+
+
+def sort_far(far, far_mate, came, corner):
+    out = like(far.shape, came.dtype)
+    return local_call(far_kernel, "sort_far", out, far, far_mate, came, corner)
 
 
 def add_column(own, came, corner, ahead, cross):
@@ -245,7 +254,8 @@
         came = along(side, 2)
         corner = move(corner, back(self.corner))
         far_mate = across(far_pass, 1)
-        far_sum, grad = sort_far(far, far_mate, came, corner, side)
+        grad = add_tails(side, came, size)
+        far_sum = sort_far(far, far_mate, came, corner)
         column, column_pass = add_column(own, came, corner, ahead, cross)
         grad = add_rounded(grad, along(grad, 4))
         far_back = move(far_sum, back(self.half))

time: 53.2 us -> 51.2 us (0.962)
  waiting for transfers between devices: 20.5 us -> 17.6 us
    ppermute x9, waiting for transfers between devices: 6.34 us -> 4.27 us  [along(): return lax.ppermute(array, 'blk', xor_pairs(lax.axis_size('blk'), bit))]
    ppermute x8, waiting for transfers between devices: 7.07 us -> 6.34 us  [move(): return lax.ppermute(array, BOTH, pairs)]
    ppermute x6, starting transfers between devices: 5.53 us -> 6.11 us  [across(): return lax.ppermute(array, 'rep', xor_pairs(lax.axis_size('rep'), bit))]
  transfers between devices with their start and end apart: 23 -> 23, of which waited for: 11 -> 9; matrix products, arithmetic and copies ran while one was open for 1% -> 2% of each run, Pallas kernels for 4% -> 5%
where the time goes in v5:
time: 51.2 us; the launch traced here: 50.6 us
  starting transfers between devices  25.3 us (49%)
  waiting for transfers between devices  17.6 us (34%)
  Pallas kernels  4.15 us (8%)
  other arithmetic  1.54 us (3%)
  local copies, waits for them, and re-layouts  1.24 us (2%)
  between operations  0.83 us (2%)
    ppermute x8, starting transfers between devices, move(): return lax.ppermute(array, BOTH, pairs)  13.4 us
    ppermute x6, waiting for transfers between devices, across(): return lax.ppermute(array, 'rep', xor_pairs(lax.axis_size('rep'), bit))  6.98 us
    ppermute x8, waiting for transfers between devices, move(): return lax.ppermute(array, BOTH, pairs)  6.34 us
    ppermute x6, starting transfers between devices, across(): return lax.ppermute(array, 'rep', xor_pairs(lax.axis_size('rep'), bit))  6.11 us
    ppermute x9, starting transfers between devices, along(): return lax.ppermute(array, 'blk', xor_pairs(lax.axis_size('blk'), bit))  5.78 us
    ppermute x9, waiting for transfers between devices, along(): return lax.ppermute(array, 'blk', xor_pairs(lax.axis_size('blk'), bit))  4.27 us
    pallas_call x1, Pallas kernels, place_tiles(): pl.pallas_call(functools.partial(place_kernel, plan, lax.axis_size('rep')...  1.27 us
    unnamed x8, local copies, waits for them, and re-layouts  1.24 us
  transfers between devices with their start and end apart: 23, of which 9 were waited for; matrix products, arithmetic and copies ran while one was open for 2% of the time, Pallas kernels for 5%

profile of v5, /device:TPU:0, one launch (start us, length us, event | category | flops | bytes accessed | tf_op | source)
XLA Modules:
  0.0 50.6 jit_solution(11658468064353994344)
XLA Ops:
  0.6 0.0 copy-start.1
  0.6 0.5 %collective-permute-start.1 = (bf16[8,4,128,128]{3,2,1,0:T(8,128)(2,1)}, bf16[8,4,128,128]{3,2,1,0:T(8,128)(2,1)S(1)}, u32[]{:S(2)}, u32[]{:S(2)}) collective-permute-start(bf16[8,4,128,128]{3,2,1,0:T(8,128)(2,1)} %bitcast.8), channel_id=1, source_target_pairs={{0,1},{1,0},{2,3},{3,2},{4,5},{5,4},{6,7},{7,6},{8,9},{9,8},{10,11... | collective-permute-start | bytes 3145736 | tf_op jit(solution)/shard_map/ppermute | solution.py:64
  1.2 3.7 %collective-permute-start.5 = (bf16[128,256]{1,0:T(8,128)(2,1)}, bf16[128,256]{1,0:T(8,128)(2,1)S(1)}, u32[]{:S(2)}, u32[]{:S(2)}) collective-permute-start(bf16[128,256]{1,0:T(8,128)(2,1)} %first.1), channel_id=1, source_target_pairs={{0,8},{1,9},{2,10},{3,11},{4,12},{5,13},{6,14},{7,15},{8,0},{9,1},... | collective-permute-start | bytes 196616 | tf_op jit(solution)/shard_map/ppermute | solution.py:56
  4.8 1.5 %collective-permute-start.2 = (bf16[128,256]{1,0:T(8,128)(2,1)}, bf16[128,256]{1,0:T(8,128)(2,1)S(1)}, u32[]{:S(2)}, u32[]{:S(2)}) collective-permute-start(bf16[128,256]{1,0:T(8,128)(2,1)} %first.1), channel_id=1, source_target_pairs={{0,16},{16,0},{1,17},{17,1},{2,18},{18,2},{3,19},{19,3},{4,20},{20... | collective-permute-start | bytes 196616 | tf_op jit(solution)/shard_map/ppermute | solution.py:60
  6.3 0.5 %collective-permute-start.6 = (bf16[128,256]{1,0:T(8,128)(2,1)}, bf16[128,256]{1,0:T(8,128)(2,1)S(1)}, u32[]{:S(2)}, u32[]{:S(2)}) collective-permute-start(bf16[128,256]{1,0:T(8,128)(2,1)} %refs_0_.1), channel_id=1, source_target_pairs={{0,16},{16,0},{1,17},{17,1},{2,18},{18,2},{3,19},{19,3},{4,20},{20... | collective-permute-start | bytes 196616 | tf_op jit(solution)/shard_map/ppermute | solution.py:60
  6.9 0.7 %pad_add_fusion.refs_0_ = s32[9,8]{1,0:T(8,128)S(1)} fusion(s32[1,8]{1,0:T(1,128)} %bitcast.12, s32[4,8]{1,0:T(4,128)} %bitcast.10, s32[4,8]{1,0:T(4,128)} %bitcast.11), kind=kLoop, calls=%fused_computation.7 | loop fusion | flops 144 | bytes 576 | tf_op jit(solution)/shard_map/concatenate | solution.py:452
  7.6 0.0 collective-permute-start
  7.6 2.1 %collective-permute-done.2.second = bf16[128,256]{1,0:T(8,128)(2,1)S(1)} collective-permute-done((bf16[128,256]{1,0:T(8,128)(2,1)}, bf16[128,256]{1,0:T(8,128)(2,1)S(1)}, u32[]{:S(2)}, u32[]{:S(2)}) %collective-permute-start.2) | collective-permute-done | bytes 65568 | tf_op jit(solution)/shard_map/ppermute | solution.py:60
  9.7 0.0 copy-done.1
  9.7 1.6 %collective-permute-start.3 = (bf16[256,256]{1,0:T(8,128)(2,1)S(1)}, bf16[256,256]{1,0:T(8,128)(2,1)S(1)}, u32[]{:S(2)}, u32[]{:S(2)}) collective-permute-start(bf16[256,256]{1,0:T(8,128)(2,1)S(1)} %stack.1.refs_0_), channel_id=1, source_target_pairs={{0,4},{1,5},{2,6},{3,7},{4,8},{5,9},{6,10},{7,11},{8,12},{9,13},{1... | collective-permute-start | bytes 393224 | tf_op jit(solution)/shard_map/ppermute | solution.py:56
  11.3 0.0 collective-permute-done.refs_2_
  11.3 1.0 %collective-permute-start.4 = (bf16[256,256]{1,0:T(8,128)(2,1)S(1)}, bf16[256,256]{1,0:T(8,128)(2,1)S(1)}, u32[]{:S(2)}, u32[]{:S(2)}) collective-permute-start(bf16[256,256]{1,0:T(8,128)(2,1)S(1)} %stack.1.refs_0_), channel_id=1, source_target_pairs={{0,6},{1,7},{2,4},{3,5},{4,10},{5,11},{6,8},{7,9},{8,14},{9,15},{1... | collective-permute-start | bytes 393224 | tf_op jit(solution)/shard_map/ppermute | solution.py:56
  12.4 0.0 collective-permute-done.6.refs_1_
  12.4 0.0 collective-permute-done.5.refs_2_
  12.4 0.0 collective-permute-done.1.refs_3_
  12.4 0.6 %collective-permute-start.8 = (bf16[128,256]{1,0:T(8,128)(2,1)S(1)}, bf16[128,256]{1,0:T(8,128)(2,1)S(1)}, u32[]{:S(2)}, u32[]{:S(2)}) collective-permute-start(bf16[128,256]{1,0:T(8,128)(2,1)S(1)} %get-tuple-element.44), channel_id=1, source_target_pairs={{0,2},{1,3},{2,0},{3,1},{4,6},{5,7},{6,4},{7,5},{8,10},{9,11},{10,... | collective-permute-start | bytes 196616 | tf_op jit(solution)/shard_map/ppermute | solution.py:64
  13.0 2.8 %collective-permute-start.9 = (bf16[128,256]{1,0:T(8,128)(2,1)S(1)}, bf16[128,256]{1,0:T(8,128)(2,1)S(1)}, u32[]{:S(2)}, u32[]{:S(2)}) collective-permute-start(bf16[128,256]{1,0:T(8,128)(2,1)S(1)} %get-tuple-element.43), channel_id=1, source_target_pairs={{0,18},{1,19},{2,16},{3,17},{4,22},{5,23},{6,20},{7,21},{8,26},{9,... | collective-permute-start | bytes 196616 | tf_op jit(solution)/shard_map/ppermute | solution.py:56
  15.8 0.2 collective-permute-start.7
  16.0 0.0 copy-start
  16.0 1.2 %copy-done = bf16[1,1,8,4,128,128]{5,4,3,2,1,0:T(8,128)(2,1)S(1)} copy-done((bf16[1,1,8,4,128,128]{5,4,3,2,1,0:T(8,128)(2,1)S(1)}, bf16[1,1,8,4,128,128]{5,4,3,2,1,0:T(8,128)(2,1)}, u32[]{:S(2)}) %copy-start) | copy-done | bytes 1048600
  17.2 1.3 %place_tiles.1 = (bf16[5,256,256]{2,1,0:T(8,128)(2,1)S(1)}, bf16[5,256,256]{2,1,0:T(8,128)(2,1)S(1)}) custom-call(s32[9,8]{1,0:T(8,128)S(1)} %pad_add_fusion.refs_0_, bf16[8,4,128,128]{3,2,1,0:T(8,128)(2,1)S(1)} %bitcast.9, s32[9,8]{1,0:T(8,128)S(1)} %collective-permute-done.refs_2_, bf16[8,4,128,128]{3,2,1,0:T(8,128)(2,1)S(1)} %collective-permute-done.1.refs_3_), custom_call_target="tpu_custom_call" | custom-call | bytes 2621440 | tf_op jit(solution)/shard_map/place_tiles/pallas_call | solution.py:295
  18.5 0.0 collective-permute-done.3.refs_1_
  18.5 1.2 %collective-permute-done.4.refs_2_ = bf16[256,256]{1,0:T(8,128)(2,1)S(1)} collective-permute-done((bf16[256,256]{1,0:T(8,128)(2,1)S(1)}, bf16[256,256]{1,0:T(8,128)(2,1)S(1)}, u32[]{:S(2)}, u32[]{:S(2)}) %collective-permute-start.4) | collective-permute-done | bytes 131104 | tf_op jit(solution)/shard_map/ppermute | solution.py:56
  19.7 0.4 forward_product.2
  20.1 0.0 collective-permute-done.8.refs_4_
  20.1 0.0 collective-permute-done.9.refs_5_
  20.1 0.0 collective-permute-done.7.refs_3_
  20.1 0.3 forward_product.3
  20.4 0.1 collective-permute-start.10
  20.5 1.3 %collective-permute-done.10 = bf16[256,256]{1,0:T(8,128)(2,1)S(1)} collective-permute-done((bf16[256,256]{1,0:T(8,128)(2,1)S(1)}, bf16[256,256]{1,0:T(8,128)(2,1)S(1)}, u32[]{:S(2)}, u32[]{:S(2)}) %collective-permute-start.10) | collective-permute-done | bytes 131104 | tf_op jit(solution)/shard_map/ppermute | solution.py:64
  21.8 0.0 copy-start.2
  21.8 0.0 copy-start.3
  21.9 0.7 %collective-permute-start.11 = (bf16[256,256]{1,0:T(8,128)(2,1)S(1)}, bf16[256,256]{1,0:T(8,128)(2,1)S(1)}, u32[]{:S(2)}, u32[]{:S(2)}) collective-permute-start(bf16[256,256]{1,0:T(8,128)(2,1)S(1)} %add_convert_fusion.first), channel_id=1, source_target_pairs={{0,16},{16,0},{1,17},{17,1},{2,18},{18,2},{3,19},{19,3},{4,20},{20... | collective-permute-start | bytes 393224 | tf_op jit(solution)/shard_map/ppermute | solution.py:60
  22.6 4.9 %collective-permute-done.11.second = bf16[256,256]{1,0:T(8,128)(2,1)S(1)} collective-permute-done((bf16[256,256]{1,0:T(8,128)(2,1)S(1)}, bf16[256,256]{1,0:T(8,128)(2,1)S(1)}, u32[]{:S(2)}, u32[]{:S(2)}) %collective-permute-start.11) | collective-permute-done | bytes 131104 | tf_op jit(solution)/shard_map/ppermute | solution.py:60
  27.5 0.0 copy-done.2
  27.5 0.0 copy-done.3
  27.5 0.9 %layer.1 = (bf16[128,256]{1,0:T(8,128)(2,1)}, f32[128,256]{1,0:T(8,128)S(1)}, bf16[384,256]{1,0:T(8,128)(2,1)S(1)}) custom-call(bf16[256,256]{1,0:T(8,128)(2,1)S(1)} %add_convert_fusion.first, bf16[256,256]{1,0:T(8,128)(2,1)S(1)} %collective-permute-done.11.second, bf16[256,256]{1,0:T(8,128)(2,1)S(1)} %copy-done.2, bf16[128,256]{1,0:T(8,128)(2,1)S(1)} %copy-done.3, ...), custom_call_target="tpu_custom_call" | custom-call | flops 100663296 | bytes 524288 | tf_op jit(solution)/shard_map/layer/pallas_call | solution.py:385
  28.4 0.0 collective-permute-start.12
  28.4 1.4 %collective-permute-done.12.sib_sent = bf16[384,256]{1,0:T(8,128)(2,1)S(1)} collective-permute-done((bf16[384,256]{1,0:T(8,128)(2,1)S(1)}, bf16[384,256]{1,0:T(8,128)(2,1)S(1)}, u32[]{:S(2)}, u32[]{:S(2)}) %collective-permute-start.12) | collective-permute-done | bytes 196640 | tf_op jit(solution)/shard_map/ppermute | solution.py:64
  29.8 0.6 %backward_product.1 = (f32[256,256]{1,0:T(8,128)S(1)}, f32[128,256]{1,0:T(8,128)S(1)}, bf16[128,256]{1,0:T(8,128)(2,1)S(1)}, bf16[256,256]{1,0:T(8,128)(2,1)S(1)...) custom-call(bf16[5,256,256]{2,1,0:T(8,128)(2,1)S(1)} %get-tuple-element.23.own_a, ...), custom_call_target="tpu_custom_call" | custom-call | flops 335544320 | bytes 1310720 | tf_op jit(solution)/shard_map/backward_product/pallas_call | solution.py:424
  30.4 1.6 %collective-permute-start.13 = (bf16[256,256]{1,0:T(8,128)(2,1)S(1)}, bf16[256,256]{1,0:T(8,128)(2,1)S(1)}, u32[]{:S(2)}, u32[]{:S(2)}) collective-permute-start(bf16[256,256]{1,0:T(8,128)(2,1)S(1)} %get-tuple-element.33.first), channel_id=1, source_target_pairs={{0,2},{1,3},{2,0},{3,1},{4,6},{5,7},{6,4},{7,5},{8,10},{9,11},{10,... | collective-permute-start | bytes 393224 | tf_op jit(solution)/shard_map/ppermute | solution.py:64
  32.0 1.8 %collective-permute-start.17 = (bf16[256,256]{1,0:T(8,128)(2,1)S(1)}, bf16[256,256]{1,0:T(8,128)(2,1)S(1)}, u32[]{:S(2)}, u32[]{:S(2)}) collective-permute-start(bf16[256,256]{1,0:T(8,128)(2,1)S(1)} %get-tuple-element.36), channel_id=1, source_target_pairs={{4,0},{5,1},{6,2},{7,3},{8,4},{9,5},{10,6},{11,7},{12,8},{13,9},{1... | collective-permute-start | bytes 393224 | tf_op jit(solution)/shard_map/ppermute | solution.py:56
  33.8 1.3 %collective-permute-start.18 = (bf16[256,256]{1,0:T(8,128)(2,1)S(1)}, bf16[256,256]{1,0:T(8,128)(2,1)S(1)}, u32[]{:S(2)}, u32[]{:S(2)}) collective-permute-start(bf16[256,256]{1,0:T(8,128)(2,1)S(1)} %get-tuple-element.37), channel_id=1, source_target_pairs={{6,0},{7,1},{4,2},{5,3},{10,4},{11,5},{8,6},{9,7},{14,8},{15,9},{1... | collective-permute-start | bytes 393224 | tf_op jit(solution)/shard_map/ppermute | solution.py:56
  35.0 0.3 collective-permute-start.16
  35.3 1.9 %collective-permute-start.20 = (bf16[128,256]{1,0:T(8,128)(2,1)S(1)}, bf16[128,256]{1,0:T(8,128)(2,1)S(1)}, u32[]{:S(2)}, u32[]{:S(2)}) collective-permute-start(bf16[128,256]{1,0:T(8,128)(2,1)S(1)} %get-tuple-element.41), channel_id=1, source_target_pairs={{0,16},{16,0},{1,17},{17,1},{2,18},{18,2},{3,19},{19,3},{4,20},{20... | collective-permute-start | bytes 196616 | tf_op jit(solution)/shard_map/ppermute | solution.py:60
  37.1 0.0 collective-permute-done.13.second.came
  37.2 1.6 %collective-permute-start.14 = (bf16[128,256]{1,0:T(8,128)(2,1)S(1)}, bf16[128,256]{1,0:T(8,128)(2,1)S(1)}, u32[]{:S(2)}, u32[]{:S(2)}) collective-permute-start(bf16[128,256]{1,0:T(8,128)(2,1)S(1)} %add_tails.1), channel_id=1, source_target_pairs={{0,4},{1,5},{2,6},{3,7},{4,0},{5,1},{6,2},{7,3},{8,12},{9,13},{10,... | collective-permute-start | bytes 196616 | tf_op jit(solution)/shard_map/ppermute | solution.py:64
  38.8 2.1 %collective-permute-done.16.corner = bf16[128,256]{1,0:T(8,128)(2,1)S(1)} collective-permute-done((bf16[128,256]{1,0:T(8,128)(2,1)S(1)}, bf16[128,256]{1,0:T(8,128)(2,1)S(1)}, u32[]{:S(2)}, u32[]{:S(2)}) %collective-permute-start.16) | collective-permute-done | bytes 65568 | tf_op jit(solution)/shard_map/ppermute | solution.py:56
  40.9 0.0 collective-permute-done.20.far_mate
  40.9 1.0 %collective-permute-start.21 = (bf16[128,256]{1,0:T(8,128)(2,1)S(1)}, bf16[128,256]{1,0:T(8,128)(2,1)S(1)}, u32[]{:S(2)}, u32[]{:S(2)}) collective-permute-start(bf16[128,256]{1,0:T(8,128)(2,1)S(1)} %sort_far.1), channel_id=1, source_target_pairs={{8,0},{9,1},{10,2},{11,3},{12,4},{13,5},{14,6},{15,7},{0,8},{1,9},... | collective-permute-start | bytes 196616 | tf_op jit(solution)/shard_map/ppermute | solution.py:56
  41.9 0.0 collective-permute-done.17.ahead
  41.9 0.0 collective-permute-done.18.cross
  41.9 0.1 add_column.1
  42.0 1.3 %collective-permute-start.19 = (bf16[128,256]{1,0:T(8,128)(2,1)S(1)}, bf16[128,256]{1,0:T(8,128)(2,1)S(1)}, u32[]{:S(2)}, u32[]{:S(2)}) collective-permute-start(bf16[128,256]{1,0:T(8,128)(2,1)S(1)} %get-tuple-element.39), channel_id=1, source_target_pairs={{0,16},{16,0},{1,17},{17,1},{2,18},{18,2},{3,19},{19,3},{4,20},{20... | collective-permute-start | bytes 196616 | tf_op jit(solution)/shard_map/ppermute | solution.py:60
  43.3 0.0 collective-permute-done.14
  43.3 1.3 %collective-permute-start.15 = (bf16[128,256]{1,0:T(8,128)(2,1)S(1)}, bf16[128,256]{1,0:T(8,128)(2,1)S(1)}, u32[]{:S(2)}, u32[]{:S(2)}) collective-permute-start(bf16[128,256]{1,0:T(8,128)(2,1)S(1)} %add_convert_fusion.2), channel_id=1, source_target_pairs={{0,8},{1,9},{2,10},{3,11},{4,12},{5,13},{6,14},{7,15},{8,0},{9,1},... | collective-permute-start | bytes 196616 | tf_op jit(solution)/shard_map/ppermute | solution.py:64
  44.7 3.0 %collective-permute-done.21.third = bf16[128,256]{1,0:T(8,128)(2,1)S(1)} collective-permute-done((bf16[128,256]{1,0:T(8,128)(2,1)S(1)}, bf16[128,256]{1,0:T(8,128)(2,1)S(1)}, u32[]{:S(2)}, u32[]{:S(2)}) %collective-permute-start.21) | collective-permute-done | bytes 65568 | tf_op jit(solution)/shard_map/ppermute | solution.py:56
  47.7 0.0 collective-permute-done.19.second
  47.7 0.7 %finish.1 = bf16[128,256]{1,0:T(8,128)(2,1)} custom-call(f32[128,256]{1,0:T(8,128)S(1)} %get-tuple-element.38.first, bf16[128,256]{1,0:T(8,128)(2,1)S(1)} %collective-permute-done.19.second, bf16[128,256]{1,0:T(8,128)(2,1)S(1)} %collective-permute-done.21.third), custom_call_target="tpu_custom_call" | custom-call | flops 65536 | bytes 262144 | tf_op jit(solution)/shard_map/finish/pallas_call | solution.py:172
  48.3 0.3 collective-permute-done.15
  48.6 0.1 collective-permute-start.22
  48.7 1.2 %collective-permute-done.22 = bf16[128,256]{1,0:T(8,128)(2,1)S(1)} collective-permute-done((bf16[128,256]{1,0:T(8,128)(2,1)S(1)}, bf16[128,256]{1,0:T(8,128)(2,1)S(1)}, u32[]{:S(2)}, u32[]{:S(2)}) %collective-permute-start.22) | collective-permute-done | bytes 65568 | tf_op jit(solution)/shard_map/ppermute | solution.py:64
  49.9 0.7 %convert_multiply_fusion = f32[256,256]{1,0:T(8,128)} fusion(bf16[128,256]{1,0:T(8,128)(2,1)S(1)} %collective-permute-done.22, bf16[128,256]{1,0:T(8,128)(2,1)S(1)} %add_convert_fusion.1, pred[]{:T(512)S(6)} %eq.10), kind=kLoop, calls=%fused_computation | loop fusion | flops 720896 | bytes 393217 | tf_op jit(solution)/shard_map/mul | solution.py:475
  (7 shorter events, 0.1 us)
Async XLA Ops:
  0.6 9.1 %copy-start.1 = (bf16[128,256]{1,0:T(8,128)(2,1)S(1)}, bf16[128,256]{1,0:T(8,128)(2,1)}, u32[]{:S(2)}) copy-start(bf16[128,256]{1,0:T(8,128)(2,1)} %first.1) | copy-start | bytes 196612
  0.6 11.7 %collective-permute-start.1 = (bf16[8,4,128,128]{3,2,1,0:T(8,128)(2,1)}, bf16[8,4,128,128]{3,2,1,0:T(8,128)(2,1)S(1)}, u32[]{:S(2)}, u32[]{:S(2)}) collective-permute-start(bf16[8,4,128,128]{3,2,1,0:T(8,128)(2,1)} %bitcast.8), channel_id=1, source_target_pairs={{0,1},{1,0},{2,3},{3,2},{4,5},{5,4},{6,7},{7,6},{8,9},{9,8},{10,11... | collective-permute-start | bytes 3145736 | tf_op jit(solution)/shard_map/ppermute | solution.py:64
  1.2 11.2 %collective-permute-start.5 = (bf16[128,256]{1,0:T(8,128)(2,1)}, bf16[128,256]{1,0:T(8,128)(2,1)S(1)}, u32[]{:S(2)}, u32[]{:S(2)}) collective-permute-start(bf16[128,256]{1,0:T(8,128)(2,1)} %first.1), channel_id=1, source_target_pairs={{0,8},{1,9},{2,10},{3,11},{4,12},{5,13},{6,14},{7,15},{8,0},{9,1},... | collective-permute-start | bytes 196616 | tf_op jit(solution)/shard_map/ppermute | solution.py:56
  4.8 4.9 %collective-permute-start.2 = (bf16[128,256]{1,0:T(8,128)(2,1)}, bf16[128,256]{1,0:T(8,128)(2,1)S(1)}, u32[]{:S(2)}, u32[]{:S(2)}) collective-permute-start(bf16[128,256]{1,0:T(8,128)(2,1)} %first.1), channel_id=1, source_target_pairs={{0,16},{16,0},{1,17},{17,1},{2,18},{18,2},{3,19},{19,3},{4,20},{20... | collective-permute-start | bytes 196616 | tf_op jit(solution)/shard_map/ppermute | solution.py:60
  6.3 6.0 %collective-permute-start.6 = (bf16[128,256]{1,0:T(8,128)(2,1)}, bf16[128,256]{1,0:T(8,128)(2,1)S(1)}, u32[]{:S(2)}, u32[]{:S(2)}) collective-permute-start(bf16[128,256]{1,0:T(8,128)(2,1)} %refs_0_.1), channel_id=1, source_target_pairs={{0,16},{16,0},{1,17},{17,1},{2,18},{18,2},{3,19},{19,3},{4,20},{20... | collective-permute-start | bytes 196616 | tf_op jit(solution)/shard_map/ppermute | solution.py:60
  7.6 3.8 %collective-permute-start = (s32[9,8]{1,0:T(8,128)S(1)}, s32[9,8]{1,0:T(8,128)S(1)}, u32[]{:S(2)}, u32[]{:S(2)}) collective-permute-start(s32[9,8]{1,0:T(8,128)S(1)} %pad_add_fusion.refs_0_), channel_id=1, source_target_pairs={{0,1},{1,0},{2,3},{3,2},{4,5},{5,4},{6,7},{7,6},{8,9},{9,8},{10,11... | collective-permute-start | bytes 872 | tf_op jit(solution)/shard_map/ppermute | solution.py:64
  9.7 8.8 %collective-permute-start.3 = (bf16[256,256]{1,0:T(8,128)(2,1)S(1)}, bf16[256,256]{1,0:T(8,128)(2,1)S(1)}, u32[]{:S(2)}, u32[]{:S(2)}) collective-permute-start(bf16[256,256]{1,0:T(8,128)(2,1)S(1)} %stack.1.refs_0_), channel_id=1, source_target_pairs={{0,4},{1,5},{2,6},{3,7},{4,8},{5,9},{6,10},{7,11},{8,12},{9,13},{1... | collective-permute-start | bytes 393224 | tf_op jit(solution)/shard_map/ppermute | solution.py:56
  11.3 8.4 %collective-permute-start.4 = (bf16[256,256]{1,0:T(8,128)(2,1)S(1)}, bf16[256,256]{1,0:T(8,128)(2,1)S(1)}, u32[]{:S(2)}, u32[]{:S(2)}) collective-permute-start(bf16[256,256]{1,0:T(8,128)(2,1)S(1)} %stack.1.refs_0_), channel_id=1, source_target_pairs={{0,6},{1,7},{2,4},{3,5},{4,10},{5,11},{6,8},{7,9},{8,14},{9,15},{1... | collective-permute-start | bytes 393224 | tf_op jit(solution)/shard_map/ppermute | solution.py:56
  12.4 7.7 %collective-permute-start.8 = (bf16[128,256]{1,0:T(8,128)(2,1)S(1)}, bf16[128,256]{1,0:T(8,128)(2,1)S(1)}, u32[]{:S(2)}, u32[]{:S(2)}) collective-permute-start(bf16[128,256]{1,0:T(8,128)(2,1)S(1)} %get-tuple-element.44), channel_id=1, source_target_pairs={{0,2},{1,3},{2,0},{3,1},{4,6},{5,7},{6,4},{7,5},{8,10},{9,11},{10,... | collective-permute-start | bytes 196616 | tf_op jit(solution)/shard_map/ppermute | solution.py:64
  13.0 7.1 %collective-permute-start.9 = (bf16[128,256]{1,0:T(8,128)(2,1)S(1)}, bf16[128,256]{1,0:T(8,128)(2,1)S(1)}, u32[]{:S(2)}, u32[]{:S(2)}) collective-permute-start(bf16[128,256]{1,0:T(8,128)(2,1)S(1)} %get-tuple-element.43), channel_id=1, source_target_pairs={{0,18},{1,19},{2,16},{3,17},{4,22},{5,23},{6,20},{7,21},{8,26},{9,... | collective-permute-start | bytes 196616 | tf_op jit(solution)/shard_map/ppermute | solution.py:56
  15.8 4.3 %collective-permute-start.7 = (bf16[128,256]{1,0:T(8,128)(2,1)S(1)}, bf16[128,256]{1,0:T(8,128)(2,1)S(1)}, u32[]{:S(2)}, u32[]{:S(2)}) collective-permute-start(bf16[128,256]{1,0:T(8,128)(2,1)S(1)} %collective-permute-done.5.refs_2_), channel_id=1, source_target_pairs={{0,16},{16,0},{1,17},{17,1},{2,18},{18,2},{3,19},{19,3},{4,20},{20... | collective-permute-start | bytes 196616 | tf_op jit(solution)/shard_map/ppermute | solution.py:60
  16.0 1.2 %copy-start = (bf16[1,1,8,4,128,128]{5,4,3,2,1,0:T(8,128)(2,1)S(1)}, bf16[1,1,8,4,128,128]{5,4,3,2,1,0:T(8,128)(2,1)}, u32[]{:S(2)}) copy-start(bf16[1,1,8,4,128,128]{5,4,3,2,1,0:T(8,128)(2,1)} %param.13) | copy-start | bytes 3145732
  20.4 1.4 %collective-permute-start.10 = (bf16[256,256]{1,0:T(8,128)(2,1)S(1)}, bf16[256,256]{1,0:T(8,128)(2,1)S(1)}, u32[]{:S(2)}, u32[]{:S(2)}) collective-permute-start(bf16[256,256]{1,0:T(8,128)(2,1)S(1)} %get-tuple-element.29), channel_id=1, source_target_pairs={{0,1},{1,0},{2,3},{3,2},{4,5},{5,4},{6,7},{7,6},{8,9},{9,8},{10,11... | collective-permute-start | bytes 393224 | tf_op jit(solution)/shard_map/ppermute | solution.py:64
  21.8 5.7 %copy-start.2 = (bf16[256,256]{1,0:T(8,128)(2,1)S(1)}, bf16[256,256]{1,0:T(8,128)(2,1)}, u32[]{:S(2)}) copy-start(bf16[256,256]{1,0:T(8,128)(2,1)} %weight.1) | copy-start | bytes 393220
  21.8 5.7 %copy-start.3 = (bf16[128,256]{1,0:T(8,128)(2,1)S(1)}, bf16[128,256]{1,0:T(8,128)(2,1)}, u32[]{:S(2)}) copy-start(bf16[128,256]{1,0:T(8,128)(2,1)} %refs_0_.1) | copy-start | bytes 196612
  21.9 5.6 %collective-permute-start.11 = (bf16[256,256]{1,0:T(8,128)(2,1)S(1)}, bf16[256,256]{1,0:T(8,128)(2,1)S(1)}, u32[]{:S(2)}, u32[]{:S(2)}) collective-permute-start(bf16[256,256]{1,0:T(8,128)(2,1)S(1)} %add_convert_fusion.first), channel_id=1, source_target_pairs={{0,16},{16,0},{1,17},{17,1},{2,18},{18,2},{3,19},{19,3},{4,20},{20... | collective-permute-start | bytes 393224 | tf_op jit(solution)/shard_map/ppermute | solution.py:60
  28.4 1.4 %collective-permute-start.12 = (bf16[384,256]{1,0:T(8,128)(2,1)S(1)}, bf16[384,256]{1,0:T(8,128)(2,1)S(1)}, u32[]{:S(2)}, u32[]{:S(2)}) collective-permute-start(bf16[384,256]{1,0:T(8,128)(2,1)S(1)} %get-tuple-element.31.own_sent), channel_id=1, source_target_pairs={{0,1},{1,0},{2,3},{3,2},{4,5},{5,4},{6,7},{7,6},{8,9},{9,8},{10,11... | collective-permute-start | bytes 589832 | tf_op jit(solution)/shard_map/ppermute | solution.py:64
  30.4 6.8 %collective-permute-start.13 = (bf16[256,256]{1,0:T(8,128)(2,1)S(1)}, bf16[256,256]{1,0:T(8,128)(2,1)S(1)}, u32[]{:S(2)}, u32[]{:S(2)}) collective-permute-start(bf16[256,256]{1,0:T(8,128)(2,1)S(1)} %get-tuple-element.33.first), channel_id=1, source_target_pairs={{0,2},{1,3},{2,0},{3,1},{4,6},{5,7},{6,4},{7,5},{8,10},{9,11},{10,... | collective-permute-start | bytes 393224 | tf_op jit(solution)/shard_map/ppermute | solution.py:64
  32.0 9.9 %collective-permute-start.17 = (bf16[256,256]{1,0:T(8,128)(2,1)S(1)}, bf16[256,256]{1,0:T(8,128)(2,1)S(1)}, u32[]{:S(2)}, u32[]{:S(2)}) collective-permute-start(bf16[256,256]{1,0:T(8,128)(2,1)S(1)} %get-tuple-element.36), channel_id=1, source_target_pairs={{4,0},{5,1},{6,2},{7,3},{8,4},{9,5},{10,6},{11,7},{12,8},{13,9},{1... | collective-permute-start | bytes 393224 | tf_op jit(solution)/shard_map/ppermute | solution.py:56
  33.8 8.1 %collective-permute-start.18 = (bf16[256,256]{1,0:T(8,128)(2,1)S(1)}, bf16[256,256]{1,0:T(8,128)(2,1)S(1)}, u32[]{:S(2)}, u32[]{:S(2)}) collective-permute-start(bf16[256,256]{1,0:T(8,128)(2,1)S(1)} %get-tuple-element.37), channel_id=1, source_target_pairs={{6,0},{7,1},{4,2},{5,3},{10,4},{11,5},{8,6},{9,7},{14,8},{15,9},{1... | collective-permute-start | bytes 393224 | tf_op jit(solution)/shard_map/ppermute | solution.py:56
  35.0 5.9 %collective-permute-start.16 = (bf16[128,256]{1,0:T(8,128)(2,1)S(1)}, bf16[128,256]{1,0:T(8,128)(2,1)S(1)}, u32[]{:S(2)}, u32[]{:S(2)}) collective-permute-start(bf16[128,256]{1,0:T(8,128)(2,1)S(1)} %get-tuple-element.35), channel_id=1, source_target_pairs={{18,0},{19,1},{16,2},{17,3},{22,4},{23,5},{20,6},{21,7},{26,8},{27... | collective-permute-start | bytes 196616 | tf_op jit(solution)/shard_map/ppermute | solution.py:56
  35.3 5.6 %collective-permute-start.20 = (bf16[128,256]{1,0:T(8,128)(2,1)S(1)}, bf16[128,256]{1,0:T(8,128)(2,1)S(1)}, u32[]{:S(2)}, u32[]{:S(2)}) collective-permute-start(bf16[128,256]{1,0:T(8,128)(2,1)S(1)} %get-tuple-element.41), channel_id=1, source_target_pairs={{0,16},{16,0},{1,17},{17,1},{2,18},{18,2},{3,19},{19,3},{4,20},{20... | collective-permute-start | bytes 196616 | tf_op jit(solution)/shard_map/ppermute | solution.py:60
  37.2 6.1 %collective-permute-start.14 = (bf16[128,256]{1,0:T(8,128)(2,1)S(1)}, bf16[128,256]{1,0:T(8,128)(2,1)S(1)}, u32[]{:S(2)}, u32[]{:S(2)}) collective-permute-start(bf16[128,256]{1,0:T(8,128)(2,1)S(1)} %add_tails.1), channel_id=1, source_target_pairs={{0,4},{1,5},{2,6},{3,7},{4,0},{5,1},{6,2},{7,3},{8,12},{9,13},{10,... | collective-permute-start | bytes 196616 | tf_op jit(solution)/shard_map/ppermute | solution.py:64
  40.9 6.7 %collective-permute-start.21 = (bf16[128,256]{1,0:T(8,128)(2,1)S(1)}, bf16[128,256]{1,0:T(8,128)(2,1)S(1)}, u32[]{:S(2)}, u32[]{:S(2)}) collective-permute-start(bf16[128,256]{1,0:T(8,128)(2,1)S(1)} %sort_far.1), channel_id=1, source_target_pairs={{8,0},{9,1},{10,2},{11,3},{12,4},{13,5},{14,6},{15,7},{0,8},{1,9},... | collective-permute-start | bytes 196616 | tf_op jit(solution)/shard_map/ppermute | solution.py:56
  42.0 5.7 %collective-permute-start.19 = (bf16[128,256]{1,0:T(8,128)(2,1)S(1)}, bf16[128,256]{1,0:T(8,128)(2,1)S(1)}, u32[]{:S(2)}, u32[]{:S(2)}) collective-permute-start(bf16[128,256]{1,0:T(8,128)(2,1)S(1)} %get-tuple-element.39), channel_id=1, source_target_pairs={{0,16},{16,0},{1,17},{17,1},{2,18},{18,2},{3,19},{19,3},{4,20},{20... | collective-permute-start | bytes 196616 | tf_op jit(solution)/shard_map/ppermute | solution.py:60
  43.3 5.2 %collective-permute-start.15 = (bf16[128,256]{1,0:T(8,128)(2,1)S(1)}, bf16[128,256]{1,0:T(8,128)(2,1)S(1)}, u32[]{:S(2)}, u32[]{:S(2)}) collective-permute-start(bf16[128,256]{1,0:T(8,128)(2,1)S(1)} %add_convert_fusion.2), channel_id=1, source_target_pairs={{0,8},{1,9},{2,10},{3,11},{4,12},{5,13},{6,14},{7,15},{8,0},{9,1},... | collective-permute-start | bytes 196616 | tf_op jit(solution)/shard_map/ppermute | solution.py:64
  48.6 1.3 %collective-permute-start.22 = (bf16[128,256]{1,0:T(8,128)(2,1)S(1)}, bf16[128,256]{1,0:T(8,128)(2,1)S(1)}, u32[]{:S(2)}, u32[]{:S(2)}) collective-permute-start(bf16[128,256]{1,0:T(8,128)(2,1)S(1)} %add_convert_fusion.1), channel_id=1, source_target_pairs={{0,1},{1,0},{2,3},{3,2},{4,5},{5,4},{6,7},{7,6},{8,9},{9,8},{10,11... | collective-permute-start | bytes 196616 | tf_op jit(solution)/shard_map/ppermute | solution.py:64

commit v6 on v5

--- a/solution.py
+++ b/solution.py
@@ -351,27 +351,28 @@
     cots, (act_out, keep_out, sent_out, grad) = refs[:groups], refs[groups:]
     size = cots[0].shape[0]
     half = keep_out.shape[0]
-    grads = []
-    for i in range(groups):
-        here = pl.ds(i * size, size)
-        there = pl.ds((i ^ (groups // 2)) * size, size)
-        total = first[here, :].astype(jnp.float32) + second[there, :].astype(jnp.float32)
-        aggregated = total.astype(jnp.bfloat16)
-        preact = jnp.dot(aggregated, weight[...], preferred_element_type=jnp.float32)
-        s = 1.0 / (1.0 + jnp.exp(-preact))
-        if i == 0:
-            act_out[...] = (preact * s).astype(act_out.dtype)
-        slope = cots[i][...].astype(jnp.float32) * s * (1.0 + preact * (1.0 - s))
-        slope = slope.astype(jnp.bfloat16)
-        grads.append(
-            lax.dot_general(
-                aggregated, slope, (((0,), (0,)), ((), ())), preferred_element_type=jnp.float32
-            )
+    theirs = [i ^ (groups // 2) for i in range(groups)]
+    other = jnp.concatenate([second[i * size : (i + 1) * size, :] for i in theirs], axis=0)
+    total = first[...].astype(jnp.float32) + other.astype(jnp.float32)
+    aggregated = total.astype(jnp.bfloat16)
+    preact = jnp.dot(aggregated, weight[...], preferred_element_type=jnp.float32)
+    s = 1.0 / (1.0 + jnp.exp(-preact))
+    act_out[...] = (preact[:size] * s[:size]).astype(act_out.dtype)
+    cot = jnp.concatenate([c[...] for c in cots], axis=0).astype(jnp.float32)
+    slope = (cot * s * (1.0 + preact * (1.0 - s))).astype(jnp.bfloat16)
+    rows = slope.shape[0]
+    sent_out[:rows, :] = lax.dot_general(
+        slope, weight[...], (((1,), (1,)), ((), ())), preferred_element_type=jnp.float32
+    ).astype(sent_out.dtype)
+    grads = [
+        lax.dot_general(
+            aggregated[i * size : (i + 1) * size],
+            slope[i * size : (i + 1) * size],
+            (((0,), (0,)), ((), ())),
+            preferred_element_type=jnp.float32,
         )
-        back = lax.dot_general(
-            slope, weight[...], (((1,), (1,)), ((), ())), preferred_element_type=jnp.float32
-        )
-        sent_out[here, :] = back.astype(sent_out.dtype)
+        for i in range(groups)
+    ]
     grad[...] = tree_sum(grads)
     keep = pl.multiple_of(core * half, half)
     away = pl.multiple_of((1 - core) * half, half)

time: 51.2 us -> 51.5 us (level)
  waiting for transfers between devices: 17.6 us -> 18.3 us
    ppermute x9, waiting for transfers between devices: 4.27 us -> 4.96 us  [along(): return lax.ppermute(array, 'blk', xor_pairs(lax.axis_size('blk'), bit))]
  transfers between devices with their start and end apart: 23 -> 23, of which waited for: 9 -> 9; matrix products, arithmetic and copies ran while one was open for 2% -> 1% of each run, Pallas kernels for 5% -> 5%
where the time goes in v6:
time: 51.5 us; the launch traced here: 51.3 us
  starting transfers between devices  25.3 us (49%)
  waiting for transfers between devices  18.3 us (36%)
  Pallas kernels  4.05 us (8%)
  other arithmetic  1.54 us (3%)
  local copies, waits for them, and re-layouts  1.24 us (2%)
  between operations  0.83 us (2%)
    ppermute x8, starting transfers between devices, move(): return lax.ppermute(array, BOTH, pairs)  13.4 us
    ppermute x6, waiting for transfers between devices, across(): return lax.ppermute(array, 'rep', xor_pairs(lax.axis_size('rep'), bit))  6.98 us
    ppermute x8, waiting for transfers between devices, move(): return lax.ppermute(array, BOTH, pairs)  6.38 us
    ppermute x6, starting transfers between devices, across(): return lax.ppermute(array, 'rep', xor_pairs(lax.axis_size('rep'), bit))  6.1 us
    ppermute x9, starting transfers between devices, along(): return lax.ppermute(array, 'blk', xor_pairs(lax.axis_size('blk'), bit))  5.79 us
    ppermute x9, waiting for transfers between devices, along(): return lax.ppermute(array, 'blk', xor_pairs(lax.axis_size('blk'), bit))  4.96 us
    unnamed x8, local copies, waits for them, and re-layouts  1.24 us
    pallas_call x1, Pallas kernels, place_tiles(): pl.pallas_call(functools.partial(place_kernel, plan, lax.axis_size('rep')...  1.23 us
  transfers between devices with their start and end apart: 23, of which 9 were waited for; matrix products, arithmetic and copies ran while one was open for 1% of the time, Pallas kernels for 5%

profile of v6, /device:TPU:0, one launch (start us, length us, event | category | flops | bytes accessed | tf_op | source)
XLA Modules:
  0.0 51.3 jit_solution(244989054884753417)
XLA Ops:
  0.6 0.0 copy-start.1
  0.6 0.5 %collective-permute-start.1 = (bf16[8,4,128,128]{3,2,1,0:T(8,128)(2,1)}, bf16[8,4,128,128]{3,2,1,0:T(8,128)(2,1)S(1)}, u32[]{:S(2)}, u32[]{:S(2)}) collective-permute-start(bf16[8,4,128,128]{3,2,1,0:T(8,128)(2,1)} %bitcast.8), channel_id=1, source_target_pairs={{0,1},{1,0},{2,3},{3,2},{4,5},{5,4},{6,7},{7,6},{8,9},{9,8},{10,11... | collective-permute-start | bytes 3145736 | tf_op jit(solution)/shard_map/ppermute | solution.py:64
  1.2 3.7 %collective-permute-start.5 = (bf16[128,256]{1,0:T(8,128)(2,1)}, bf16[128,256]{1,0:T(8,128)(2,1)S(1)}, u32[]{:S(2)}, u32[]{:S(2)}) collective-permute-start(bf16[128,256]{1,0:T(8,128)(2,1)} %first.1), channel_id=1, source_target_pairs={{0,8},{1,9},{2,10},{3,11},{4,12},{5,13},{6,14},{7,15},{8,0},{9,1},... | collective-permute-start | bytes 196616 | tf_op jit(solution)/shard_map/ppermute | solution.py:56
  4.8 1.5 %collective-permute-start.2 = (bf16[128,256]{1,0:T(8,128)(2,1)}, bf16[128,256]{1,0:T(8,128)(2,1)S(1)}, u32[]{:S(2)}, u32[]{:S(2)}) collective-permute-start(bf16[128,256]{1,0:T(8,128)(2,1)} %first.1), channel_id=1, source_target_pairs={{0,16},{16,0},{1,17},{17,1},{2,18},{18,2},{3,19},{19,3},{4,20},{20... | collective-permute-start | bytes 196616 | tf_op jit(solution)/shard_map/ppermute | solution.py:60
  6.3 0.5 %collective-permute-start.6 = (bf16[128,256]{1,0:T(8,128)(2,1)}, bf16[128,256]{1,0:T(8,128)(2,1)S(1)}, u32[]{:S(2)}, u32[]{:S(2)}) collective-permute-start(bf16[128,256]{1,0:T(8,128)(2,1)} %refs_0_.1), channel_id=1, source_target_pairs={{0,16},{16,0},{1,17},{17,1},{2,18},{18,2},{3,19},{19,3},{4,20},{20... | collective-permute-start | bytes 196616 | tf_op jit(solution)/shard_map/ppermute | solution.py:60
  6.9 0.7 %pad_add_fusion.refs_0_ = s32[9,8]{1,0:T(8,128)S(1)} fusion(s32[1,8]{1,0:T(1,128)} %bitcast.12, s32[4,8]{1,0:T(4,128)} %bitcast.10, s32[4,8]{1,0:T(4,128)} %bitcast.11), kind=kLoop, calls=%fused_computation.7 | loop fusion | flops 144 | bytes 576 | tf_op jit(solution)/shard_map/concatenate | solution.py:453
  7.6 0.0 collective-permute-start
  7.6 2.1 %collective-permute-done.2.second = bf16[128,256]{1,0:T(8,128)(2,1)S(1)} collective-permute-done((bf16[128,256]{1,0:T(8,128)(2,1)}, bf16[128,256]{1,0:T(8,128)(2,1)S(1)}, u32[]{:S(2)}, u32[]{:S(2)}) %collective-permute-start.2) | collective-permute-done | bytes 65568 | tf_op jit(solution)/shard_map/ppermute | solution.py:60
  9.7 0.0 copy-done.1
  9.7 1.6 %collective-permute-start.3 = (bf16[256,256]{1,0:T(8,128)(2,1)S(1)}, bf16[256,256]{1,0:T(8,128)(2,1)S(1)}, u32[]{:S(2)}, u32[]{:S(2)}) collective-permute-start(bf16[256,256]{1,0:T(8,128)(2,1)S(1)} %stack.1.refs_0_), channel_id=1, source_target_pairs={{0,4},{1,5},{2,6},{3,7},{4,8},{5,9},{6,10},{7,11},{8,12},{9,13},{1... | collective-permute-start | bytes 393224 | tf_op jit(solution)/shard_map/ppermute | solution.py:56
  11.3 0.0 collective-permute-done.refs_2_
  11.3 1.0 %collective-permute-start.4 = (bf16[256,256]{1,0:T(8,128)(2,1)S(1)}, bf16[256,256]{1,0:T(8,128)(2,1)S(1)}, u32[]{:S(2)}, u32[]{:S(2)}) collective-permute-start(bf16[256,256]{1,0:T(8,128)(2,1)S(1)} %stack.1.refs_0_), channel_id=1, source_target_pairs={{0,6},{1,7},{2,4},{3,5},{4,10},{5,11},{6,8},{7,9},{8,14},{9,15},{1... | collective-permute-start | bytes 393224 | tf_op jit(solution)/shard_map/ppermute | solution.py:56
  12.4 0.0 collective-permute-done.6.refs_1_
  12.4 0.0 collective-permute-done.5.refs_2_
  12.4 0.0 collective-permute-done.1.refs_3_
  12.4 0.6 %collective-permute-start.8 = (bf16[128,256]{1,0:T(8,128)(2,1)S(1)}, bf16[128,256]{1,0:T(8,128)(2,1)S(1)}, u32[]{:S(2)}, u32[]{:S(2)}) collective-permute-start(bf16[128,256]{1,0:T(8,128)(2,1)S(1)} %get-tuple-element.44), channel_id=1, source_target_pairs={{0,2},{1,3},{2,0},{3,1},{4,6},{5,7},{6,4},{7,5},{8,10},{9,11},{10,... | collective-permute-start | bytes 196616 | tf_op jit(solution)/shard_map/ppermute | solution.py:64
  13.0 2.8 %collective-permute-start.9 = (bf16[128,256]{1,0:T(8,128)(2,1)S(1)}, bf16[128,256]{1,0:T(8,128)(2,1)S(1)}, u32[]{:S(2)}, u32[]{:S(2)}) collective-permute-start(bf16[128,256]{1,0:T(8,128)(2,1)S(1)} %get-tuple-element.43), channel_id=1, source_target_pairs={{0,18},{1,19},{2,16},{3,17},{4,22},{5,23},{6,20},{7,21},{8,26},{9,... | collective-permute-start | bytes 196616 | tf_op jit(solution)/shard_map/ppermute | solution.py:56
  15.8 0.2 collective-permute-start.7
  16.0 0.0 copy-start
  16.0 1.2 %copy-done = bf16[1,1,8,4,128,128]{5,4,3,2,1,0:T(8,128)(2,1)S(1)} copy-done((bf16[1,1,8,4,128,128]{5,4,3,2,1,0:T(8,128)(2,1)S(1)}, bf16[1,1,8,4,128,128]{5,4,3,2,1,0:T(8,128)(2,1)}, u32[]{:S(2)}) %copy-start) | copy-done | bytes 1048600
  17.2 1.2 %place_tiles.1 = (bf16[5,256,256]{2,1,0:T(8,128)(2,1)S(1)}, bf16[5,256,256]{2,1,0:T(8,128)(2,1)S(1)}) custom-call(s32[9,8]{1,0:T(8,128)S(1)} %pad_add_fusion.refs_0_, bf16[8,4,128,128]{3,2,1,0:T(8,128)(2,1)S(1)} %bitcast.9, s32[9,8]{1,0:T(8,128)S(1)} %collective-permute-done.refs_2_, bf16[8,4,128,128]{3,2,1,0:T(8,128)(2,1)S(1)} %collective-permute-done.1.refs_3_), custom_call_target="tpu_custom_call" | custom-call | bytes 2621440 | tf_op jit(solution)/shard_map/place_tiles/pallas_call | solution.py:295
  18.4 0.0 collective-permute-done.3.refs_1_
  18.4 1.3 %collective-permute-done.4.refs_2_ = bf16[256,256]{1,0:T(8,128)(2,1)S(1)} collective-permute-done((bf16[256,256]{1,0:T(8,128)(2,1)S(1)}, bf16[256,256]{1,0:T(8,128)(2,1)S(1)}, u32[]{:S(2)}, u32[]{:S(2)}) %collective-permute-start.4) | collective-permute-done | bytes 131104 | tf_op jit(solution)/shard_map/ppermute | solution.py:56
  19.7 0.4 forward_product.2
  20.1 0.0 collective-permute-done.8.refs_4_
  20.1 0.0 collective-permute-done.9.refs_5_
  20.1 0.0 collective-permute-done.7.refs_3_
  20.1 0.3 forward_product.3
  20.4 0.1 collective-permute-start.10
  20.5 1.3 %collective-permute-done.10 = bf16[256,256]{1,0:T(8,128)(2,1)S(1)} collective-permute-done((bf16[256,256]{1,0:T(8,128)(2,1)S(1)}, bf16[256,256]{1,0:T(8,128)(2,1)S(1)}, u32[]{:S(2)}, u32[]{:S(2)}) %collective-permute-start.10) | collective-permute-done | bytes 131104 | tf_op jit(solution)/shard_map/ppermute | solution.py:64
  21.8 0.0 copy-start.2
  21.8 0.0 copy-start.3
  21.9 0.7 %collective-permute-start.11 = (bf16[256,256]{1,0:T(8,128)(2,1)S(1)}, bf16[256,256]{1,0:T(8,128)(2,1)S(1)}, u32[]{:S(2)}, u32[]{:S(2)}) collective-permute-start(bf16[256,256]{1,0:T(8,128)(2,1)S(1)} %add_convert_fusion.first), channel_id=1, source_target_pairs={{0,16},{16,0},{1,17},{17,1},{2,18},{18,2},{3,19},{19,3},{4,20},{20... | collective-permute-start | bytes 393224 | tf_op jit(solution)/shard_map/ppermute | solution.py:60
  22.6 4.9 %collective-permute-done.11.second = bf16[256,256]{1,0:T(8,128)(2,1)S(1)} collective-permute-done((bf16[256,256]{1,0:T(8,128)(2,1)S(1)}, bf16[256,256]{1,0:T(8,128)(2,1)S(1)}, u32[]{:S(2)}, u32[]{:S(2)}) %collective-permute-start.11) | collective-permute-done | bytes 131104 | tf_op jit(solution)/shard_map/ppermute | solution.py:60
  27.5 0.0 copy-done.2
  27.5 0.0 copy-done.3
  27.5 0.8 %layer.1 = (bf16[128,256]{1,0:T(8,128)(2,1)}, f32[128,256]{1,0:T(8,128)S(1)}, bf16[384,256]{1,0:T(8,128)(2,1)S(1)}) custom-call(bf16[256,256]{1,0:T(8,128)(2,1)S(1)} %add_convert_fusion.first, bf16[256,256]{1,0:T(8,128)(2,1)S(1)} %collective-permute-done.11.second, bf16[256,256]{1,0:T(8,128)(2,1)S(1)} %copy-done.2, bf16[128,256]{1,0:T(8,128)(2,1)S(1)} %copy-done.3, ...), custom_call_target="tpu_custom_call" | custom-call | flops 100663296 | bytes 524288 | tf_op jit(solution)/shard_map/layer/pallas_call | solution.py:386
  28.3 0.0 collective-permute-start.12
  28.3 1.4 %collective-permute-done.12.sib_sent = bf16[384,256]{1,0:T(8,128)(2,1)S(1)} collective-permute-done((bf16[384,256]{1,0:T(8,128)(2,1)S(1)}, bf16[384,256]{1,0:T(8,128)(2,1)S(1)}, u32[]{:S(2)}, u32[]{:S(2)}) %collective-permute-start.12) | collective-permute-done | bytes 196640 | tf_op jit(solution)/shard_map/ppermute | solution.py:64
  29.8 0.5 %backward_product.1 = (f32[256,256]{1,0:T(8,128)S(1)}, f32[128,256]{1,0:T(8,128)S(1)}, bf16[128,256]{1,0:T(8,128)(2,1)S(1)}, bf16[256,256]{1,0:T(8,128)(2,1)S(1)...) custom-call(bf16[5,256,256]{2,1,0:T(8,128)(2,1)S(1)} %get-tuple-element.23.own_a, ...), custom_call_target="tpu_custom_call" | custom-call | flops 335544320 | bytes 1310720 | tf_op jit(solution)/shard_map/backward_product/pallas_call | solution.py:425
  30.3 1.6 %collective-permute-start.13 = (bf16[256,256]{1,0:T(8,128)(2,1)S(1)}, bf16[256,256]{1,0:T(8,128)(2,1)S(1)}, u32[]{:S(2)}, u32[]{:S(2)}) collective-permute-start(bf16[256,256]{1,0:T(8,128)(2,1)S(1)} %get-tuple-element.33.first), channel_id=1, source_target_pairs={{0,2},{1,3},{2,0},{3,1},{4,6},{5,7},{6,4},{7,5},{8,10},{9,11},{10,... | collective-permute-start | bytes 393224 | tf_op jit(solution)/shard_map/ppermute | solution.py:64
  31.9 1.8 %collective-permute-start.17 = (bf16[256,256]{1,0:T(8,128)(2,1)S(1)}, bf16[256,256]{1,0:T(8,128)(2,1)S(1)}, u32[]{:S(2)}, u32[]{:S(2)}) collective-permute-start(bf16[256,256]{1,0:T(8,128)(2,1)S(1)} %get-tuple-element.36), channel_id=1, source_target_pairs={{4,0},{5,1},{6,2},{7,3},{8,4},{9,5},{10,6},{11,7},{12,8},{13,9},{1... | collective-permute-start | bytes 393224 | tf_op jit(solution)/shard_map/ppermute | solution.py:56
  33.7 1.3 %collective-permute-start.18 = (bf16[256,256]{1,0:T(8,128)(2,1)S(1)}, bf16[256,256]{1,0:T(8,128)(2,1)S(1)}, u32[]{:S(2)}, u32[]{:S(2)}) collective-permute-start(bf16[256,256]{1,0:T(8,128)(2,1)S(1)} %get-tuple-element.37), channel_id=1, source_target_pairs={{6,0},{7,1},{4,2},{5,3},{10,4},{11,5},{8,6},{9,7},{14,8},{15,9},{1... | collective-permute-start | bytes 393224 | tf_op jit(solution)/shard_map/ppermute | solution.py:56
  35.0 0.3 collective-permute-start.16
  35.2 1.9 %collective-permute-start.20 = (bf16[128,256]{1,0:T(8,128)(2,1)S(1)}, bf16[128,256]{1,0:T(8,128)(2,1)S(1)}, u32[]{:S(2)}, u32[]{:S(2)}) collective-permute-start(bf16[128,256]{1,0:T(8,128)(2,1)S(1)} %get-tuple-element.41), channel_id=1, source_target_pairs={{0,16},{16,0},{1,17},{17,1},{2,18},{18,2},{3,19},{19,3},{4,20},{20... | collective-permute-start | bytes 196616 | tf_op jit(solution)/shard_map/ppermute | solution.py:60
  37.1 0.0 collective-permute-done.13.second.came
  37.1 1.6 %collective-permute-start.14 = (bf16[128,256]{1,0:T(8,128)(2,1)S(1)}, bf16[128,256]{1,0:T(8,128)(2,1)S(1)}, u32[]{:S(2)}, u32[]{:S(2)}) collective-permute-start(bf16[128,256]{1,0:T(8,128)(2,1)S(1)} %add_tails.1), channel_id=1, source_target_pairs={{0,4},{1,5},{2,6},{3,7},{4,0},{5,1},{6,2},{7,3},{8,12},{9,13},{10,... | collective-permute-start | bytes 196616 | tf_op jit(solution)/shard_map/ppermute | solution.py:64
  38.7 2.1 %collective-permute-done.16.corner = bf16[128,256]{1,0:T(8,128)(2,1)S(1)} collective-permute-done((bf16[128,256]{1,0:T(8,128)(2,1)S(1)}, bf16[128,256]{1,0:T(8,128)(2,1)S(1)}, u32[]{:S(2)}, u32[]{:S(2)}) %collective-permute-start.16) | collective-permute-done | bytes 65568 | tf_op jit(solution)/shard_map/ppermute | solution.py:56
  40.8 0.0 collective-permute-done.20.far_mate
  40.9 1.0 %collective-permute-start.21 = (bf16[128,256]{1,0:T(8,128)(2,1)S(1)}, bf16[128,256]{1,0:T(8,128)(2,1)S(1)}, u32[]{:S(2)}, u32[]{:S(2)}) collective-permute-start(bf16[128,256]{1,0:T(8,128)(2,1)S(1)} %sort_far.1), channel_id=1, source_target_pairs={{8,0},{9,1},{10,2},{11,3},{12,4},{13,5},{14,6},{15,7},{0,8},{1,9},... | collective-permute-start | bytes 196616 | tf_op jit(solution)/shard_map/ppermute | solution.py:56
  41.8 0.0 collective-permute-done.17.ahead
  41.8 0.0 collective-permute-done.18.cross
  41.9 0.1 add_column.1
  41.9 1.3 %collective-permute-start.19 = (bf16[128,256]{1,0:T(8,128)(2,1)S(1)}, bf16[128,256]{1,0:T(8,128)(2,1)S(1)}, u32[]{:S(2)}, u32[]{:S(2)}) collective-permute-start(bf16[128,256]{1,0:T(8,128)(2,1)S(1)} %get-tuple-element.39), channel_id=1, source_target_pairs={{0,16},{16,0},{1,17},{17,1},{2,18},{18,2},{3,19},{19,3},{4,20},{20... | collective-permute-start | bytes 196616 | tf_op jit(solution)/shard_map/ppermute | solution.py:60
  43.2 0.0 collective-permute-done.14
  43.3 1.3 %collective-permute-start.15 = (bf16[128,256]{1,0:T(8,128)(2,1)S(1)}, bf16[128,256]{1,0:T(8,128)(2,1)S(1)}, u32[]{:S(2)}, u32[]{:S(2)}) collective-permute-start(bf16[128,256]{1,0:T(8,128)(2,1)S(1)} %add_convert_fusion.2), channel_id=1, source_target_pairs={{0,8},{1,9},{2,10},{3,11},{4,12},{5,13},{6,14},{7,15},{8,0},{9,1},... | collective-permute-start | bytes 196616 | tf_op jit(solution)/shard_map/ppermute | solution.py:64
  44.6 3.0 %collective-permute-done.21.third = bf16[128,256]{1,0:T(8,128)(2,1)S(1)} collective-permute-done((bf16[128,256]{1,0:T(8,128)(2,1)S(1)}, bf16[128,256]{1,0:T(8,128)(2,1)S(1)}, u32[]{:S(2)}, u32[]{:S(2)}) %collective-permute-start.21) | collective-permute-done | bytes 65568 | tf_op jit(solution)/shard_map/ppermute | solution.py:56
  47.6 0.0 collective-permute-done.19.second
  47.6 0.7 %finish.1 = bf16[128,256]{1,0:T(8,128)(2,1)} custom-call(f32[128,256]{1,0:T(8,128)S(1)} %get-tuple-element.38.first, bf16[128,256]{1,0:T(8,128)(2,1)S(1)} %collective-permute-done.19.second, bf16[128,256]{1,0:T(8,128)(2,1)S(1)} %collective-permute-done.21.third), custom_call_target="tpu_custom_call" | custom-call | flops 65536 | bytes 262144 | tf_op jit(solution)/shard_map/finish/pallas_call | solution.py:172
  48.3 0.9 %collective-permute-done.15 = bf16[128,256]{1,0:T(8,128)(2,1)S(1)} collective-permute-done((bf16[128,256]{1,0:T(8,128)(2,1)S(1)}, bf16[128,256]{1,0:T(8,128)(2,1)S(1)}, u32[]{:S(2)}, u32[]{:S(2)}) %collective-permute-start.15) | collective-permute-done | bytes 65568 | tf_op jit(solution)/shard_map/ppermute | solution.py:64
  49.2 0.1 collective-permute-start.22
  49.3 1.2 %collective-permute-done.22 = bf16[128,256]{1,0:T(8,128)(2,1)S(1)} collective-permute-done((bf16[128,256]{1,0:T(8,128)(2,1)S(1)}, bf16[128,256]{1,0:T(8,128)(2,1)S(1)}, u32[]{:S(2)}, u32[]{:S(2)}) %collective-permute-start.22) | collective-permute-done | bytes 65568 | tf_op jit(solution)/shard_map/ppermute | solution.py:64
  50.5 0.7 %convert_multiply_fusion = f32[256,256]{1,0:T(8,128)} fusion(bf16[128,256]{1,0:T(8,128)(2,1)S(1)} %collective-permute-done.22, bf16[128,256]{1,0:T(8,128)(2,1)S(1)} %add_convert_fusion.1, pred[]{:T(512)S(6)} %eq.10), kind=kLoop, calls=%fused_computation | loop fusion | flops 720896 | bytes 393217 | tf_op jit(solution)/shard_map/mul | solution.py:476
  (7 shorter events, 0.1 us)
Async XLA Ops:
  0.6 9.1 %copy-start.1 = (bf16[128,256]{1,0:T(8,128)(2,1)S(1)}, bf16[128,256]{1,0:T(8,128)(2,1)}, u32[]{:S(2)}) copy-start(bf16[128,256]{1,0:T(8,128)(2,1)} %first.1) | copy-start | bytes 196612
  0.6 11.7 %collective-permute-start.1 = (bf16[8,4,128,128]{3,2,1,0:T(8,128)(2,1)}, bf16[8,4,128,128]{3,2,1,0:T(8,128)(2,1)S(1)}, u32[]{:S(2)}, u32[]{:S(2)}) collective-permute-start(bf16[8,4,128,128]{3,2,1,0:T(8,128)(2,1)} %bitcast.8), channel_id=1, source_target_pairs={{0,1},{1,0},{2,3},{3,2},{4,5},{5,4},{6,7},{7,6},{8,9},{9,8},{10,11... | collective-permute-start | bytes 3145736 | tf_op jit(solution)/shard_map/ppermute | solution.py:64
  1.2 11.2 %collective-permute-start.5 = (bf16[128,256]{1,0:T(8,128)(2,1)}, bf16[128,256]{1,0:T(8,128)(2,1)S(1)}, u32[]{:S(2)}, u32[]{:S(2)}) collective-permute-start(bf16[128,256]{1,0:T(8,128)(2,1)} %first.1), channel_id=1, source_target_pairs={{0,8},{1,9},{2,10},{3,11},{4,12},{5,13},{6,14},{7,15},{8,0},{9,1},... | collective-permute-start | bytes 196616 | tf_op jit(solution)/shard_map/ppermute | solution.py:56
  4.8 4.9 %collective-permute-start.2 = (bf16[128,256]{1,0:T(8,128)(2,1)}, bf16[128,256]{1,0:T(8,128)(2,1)S(1)}, u32[]{:S(2)}, u32[]{:S(2)}) collective-permute-start(bf16[128,256]{1,0:T(8,128)(2,1)} %first.1), channel_id=1, source_target_pairs={{0,16},{16,0},{1,17},{17,1},{2,18},{18,2},{3,19},{19,3},{4,20},{20... | collective-permute-start | bytes 196616 | tf_op jit(solution)/shard_map/ppermute | solution.py:60
  6.3 6.0 %collective-permute-start.6 = (bf16[128,256]{1,0:T(8,128)(2,1)}, bf16[128,256]{1,0:T(8,128)(2,1)S(1)}, u32[]{:S(2)}, u32[]{:S(2)}) collective-permute-start(bf16[128,256]{1,0:T(8,128)(2,1)} %refs_0_.1), channel_id=1, source_target_pairs={{0,16},{16,0},{1,17},{17,1},{2,18},{18,2},{3,19},{19,3},{4,20},{20... | collective-permute-start | bytes 196616 | tf_op jit(solution)/shard_map/ppermute | solution.py:60
  7.6 3.8 %collective-permute-start = (s32[9,8]{1,0:T(8,128)S(1)}, s32[9,8]{1,0:T(8,128)S(1)}, u32[]{:S(2)}, u32[]{:S(2)}) collective-permute-start(s32[9,8]{1,0:T(8,128)S(1)} %pad_add_fusion.refs_0_), channel_id=1, source_target_pairs={{0,1},{1,0},{2,3},{3,2},{4,5},{5,4},{6,7},{7,6},{8,9},{9,8},{10,11... | collective-permute-start | bytes 872 | tf_op jit(solution)/shard_map/ppermute | solution.py:64
  9.7 8.7 %collective-permute-start.3 = (bf16[256,256]{1,0:T(8,128)(2,1)S(1)}, bf16[256,256]{1,0:T(8,128)(2,1)S(1)}, u32[]{:S(2)}, u32[]{:S(2)}) collective-permute-start(bf16[256,256]{1,0:T(8,128)(2,1)S(1)} %stack.1.refs_0_), channel_id=1, source_target_pairs={{0,4},{1,5},{2,6},{3,7},{4,8},{5,9},{6,10},{7,11},{8,12},{9,13},{1... | collective-permute-start | bytes 393224 | tf_op jit(solution)/shard_map/ppermute | solution.py:56
  11.3 8.4 %collective-permute-start.4 = (bf16[256,256]{1,0:T(8,128)(2,1)S(1)}, bf16[256,256]{1,0:T(8,128)(2,1)S(1)}, u32[]{:S(2)}, u32[]{:S(2)}) collective-permute-start(bf16[256,256]{1,0:T(8,128)(2,1)S(1)} %stack.1.refs_0_), channel_id=1, source_target_pairs={{0,6},{1,7},{2,4},{3,5},{4,10},{5,11},{6,8},{7,9},{8,14},{9,15},{1... | collective-permute-start | bytes 393224 | tf_op jit(solution)/shard_map/ppermute | solution.py:56
  12.4 7.7 %collective-permute-start.8 = (bf16[128,256]{1,0:T(8,128)(2,1)S(1)}, bf16[128,256]{1,0:T(8,128)(2,1)S(1)}, u32[]{:S(2)}, u32[]{:S(2)}) collective-permute-start(bf16[128,256]{1,0:T(8,128)(2,1)S(1)} %get-tuple-element.44), channel_id=1, source_target_pairs={{0,2},{1,3},{2,0},{3,1},{4,6},{5,7},{6,4},{7,5},{8,10},{9,11},{10,... | collective-permute-start | bytes 196616 | tf_op jit(solution)/shard_map/ppermute | solution.py:64
  13.0 7.1 %collective-permute-start.9 = (bf16[128,256]{1,0:T(8,128)(2,1)S(1)}, bf16[128,256]{1,0:T(8,128)(2,1)S(1)}, u32[]{:S(2)}, u32[]{:S(2)}) collective-permute-start(bf16[128,256]{1,0:T(8,128)(2,1)S(1)} %get-tuple-element.43), channel_id=1, source_target_pairs={{0,18},{1,19},{2,16},{3,17},{4,22},{5,23},{6,20},{7,21},{8,26},{9,... | collective-permute-start | bytes 196616 | tf_op jit(solution)/shard_map/ppermute | solution.py:56
  15.8 4.3 %collective-permute-start.7 = (bf16[128,256]{1,0:T(8,128)(2,1)S(1)}, bf16[128,256]{1,0:T(8,128)(2,1)S(1)}, u32[]{:S(2)}, u32[]{:S(2)}) collective-permute-start(bf16[128,256]{1,0:T(8,128)(2,1)S(1)} %collective-permute-done.5.refs_2_), channel_id=1, source_target_pairs={{0,16},{16,0},{1,17},{17,1},{2,18},{18,2},{3,19},{19,3},{4,20},{20... | collective-permute-start | bytes 196616 | tf_op jit(solution)/shard_map/ppermute | solution.py:60
  16.0 1.2 %copy-start = (bf16[1,1,8,4,128,128]{5,4,3,2,1,0:T(8,128)(2,1)S(1)}, bf16[1,1,8,4,128,128]{5,4,3,2,1,0:T(8,128)(2,1)}, u32[]{:S(2)}) copy-start(bf16[1,1,8,4,128,128]{5,4,3,2,1,0:T(8,128)(2,1)} %param.13) | copy-start | bytes 3145732
  20.4 1.4 %collective-permute-start.10 = (bf16[256,256]{1,0:T(8,128)(2,1)S(1)}, bf16[256,256]{1,0:T(8,128)(2,1)S(1)}, u32[]{:S(2)}, u32[]{:S(2)}) collective-permute-start(bf16[256,256]{1,0:T(8,128)(2,1)S(1)} %get-tuple-element.29), channel_id=1, source_target_pairs={{0,1},{1,0},{2,3},{3,2},{4,5},{5,4},{6,7},{7,6},{8,9},{9,8},{10,11... | collective-permute-start | bytes 393224 | tf_op jit(solution)/shard_map/ppermute | solution.py:64
  21.8 5.7 %copy-start.2 = (bf16[256,256]{1,0:T(8,128)(2,1)S(1)}, bf16[256,256]{1,0:T(8,128)(2,1)}, u32[]{:S(2)}) copy-start(bf16[256,256]{1,0:T(8,128)(2,1)} %weight.1) | copy-start | bytes 393220
  21.8 5.7 %copy-start.3 = (bf16[128,256]{1,0:T(8,128)(2,1)S(1)}, bf16[128,256]{1,0:T(8,128)(2,1)}, u32[]{:S(2)}) copy-start(bf16[128,256]{1,0:T(8,128)(2,1)} %refs_0_.1) | copy-start | bytes 196612
  21.9 5.6 %collective-permute-start.11 = (bf16[256,256]{1,0:T(8,128)(2,1)S(1)}, bf16[256,256]{1,0:T(8,128)(2,1)S(1)}, u32[]{:S(2)}, u32[]{:S(2)}) collective-permute-start(bf16[256,256]{1,0:T(8,128)(2,1)S(1)} %add_convert_fusion.first), channel_id=1, source_target_pairs={{0,16},{16,0},{1,17},{17,1},{2,18},{18,2},{3,19},{19,3},{4,20},{20... | collective-permute-start | bytes 393224 | tf_op jit(solution)/shard_map/ppermute | solution.py:60
  28.3 1.4 %collective-permute-start.12 = (bf16[384,256]{1,0:T(8,128)(2,1)S(1)}, bf16[384,256]{1,0:T(8,128)(2,1)S(1)}, u32[]{:S(2)}, u32[]{:S(2)}) collective-permute-start(bf16[384,256]{1,0:T(8,128)(2,1)S(1)} %get-tuple-element.31.own_sent), channel_id=1, source_target_pairs={{0,1},{1,0},{2,3},{3,2},{4,5},{5,4},{6,7},{7,6},{8,9},{9,8},{10,11... | collective-permute-start | bytes 589832 | tf_op jit(solution)/shard_map/ppermute | solution.py:64
  30.3 6.8 %collective-permute-start.13 = (bf16[256,256]{1,0:T(8,128)(2,1)S(1)}, bf16[256,256]{1,0:T(8,128)(2,1)S(1)}, u32[]{:S(2)}, u32[]{:S(2)}) collective-permute-start(bf16[256,256]{1,0:T(8,128)(2,1)S(1)} %get-tuple-element.33.first), channel_id=1, source_target_pairs={{0,2},{1,3},{2,0},{3,1},{4,6},{5,7},{6,4},{7,5},{8,10},{9,11},{10,... | collective-permute-start | bytes 393224 | tf_op jit(solution)/shard_map/ppermute | solution.py:64
  31.9 9.9 %collective-permute-start.17 = (bf16[256,256]{1,0:T(8,128)(2,1)S(1)}, bf16[256,256]{1,0:T(8,128)(2,1)S(1)}, u32[]{:S(2)}, u32[]{:S(2)}) collective-permute-start(bf16[256,256]{1,0:T(8,128)(2,1)S(1)} %get-tuple-element.36), channel_id=1, source_target_pairs={{4,0},{5,1},{6,2},{7,3},{8,4},{9,5},{10,6},{11,7},{12,8},{13,9},{1... | collective-permute-start | bytes 393224 | tf_op jit(solution)/shard_map/ppermute | solution.py:56
  33.7 8.1 %collective-permute-start.18 = (bf16[256,256]{1,0:T(8,128)(2,1)S(1)}, bf16[256,256]{1,0:T(8,128)(2,1)S(1)}, u32[]{:S(2)}, u32[]{:S(2)}) collective-permute-start(bf16[256,256]{1,0:T(8,128)(2,1)S(1)} %get-tuple-element.37), channel_id=1, source_target_pairs={{6,0},{7,1},{4,2},{5,3},{10,4},{11,5},{8,6},{9,7},{14,8},{15,9},{1... | collective-permute-start | bytes 393224 | tf_op jit(solution)/shard_map/ppermute | solution.py:56
  35.0 5.9 %collective-permute-start.16 = (bf16[128,256]{1,0:T(8,128)(2,1)S(1)}, bf16[128,256]{1,0:T(8,128)(2,1)S(1)}, u32[]{:S(2)}, u32[]{:S(2)}) collective-permute-start(bf16[128,256]{1,0:T(8,128)(2,1)S(1)} %get-tuple-element.35), channel_id=1, source_target_pairs={{18,0},{19,1},{16,2},{17,3},{22,4},{23,5},{20,6},{21,7},{26,8},{27... | collective-permute-start | bytes 196616 | tf_op jit(solution)/shard_map/ppermute | solution.py:56
  35.2 5.6 %collective-permute-start.20 = (bf16[128,256]{1,0:T(8,128)(2,1)S(1)}, bf16[128,256]{1,0:T(8,128)(2,1)S(1)}, u32[]{:S(2)}, u32[]{:S(2)}) collective-permute-start(bf16[128,256]{1,0:T(8,128)(2,1)S(1)} %get-tuple-element.41), channel_id=1, source_target_pairs={{0,16},{16,0},{1,17},{17,1},{2,18},{18,2},{3,19},{19,3},{4,20},{20... | collective-permute-start | bytes 196616 | tf_op jit(solution)/shard_map/ppermute | solution.py:60
  37.1 6.1 %collective-permute-start.14 = (bf16[128,256]{1,0:T(8,128)(2,1)S(1)}, bf16[128,256]{1,0:T(8,128)(2,1)S(1)}, u32[]{:S(2)}, u32[]{:S(2)}) collective-permute-start(bf16[128,256]{1,0:T(8,128)(2,1)S(1)} %add_tails.1), channel_id=1, source_target_pairs={{0,4},{1,5},{2,6},{3,7},{4,0},{5,1},{6,2},{7,3},{8,12},{9,13},{10,... | collective-permute-start | bytes 196616 | tf_op jit(solution)/shard_map/ppermute | solution.py:64
  40.9 6.7 %collective-permute-start.21 = (bf16[128,256]{1,0:T(8,128)(2,1)S(1)}, bf16[128,256]{1,0:T(8,128)(2,1)S(1)}, u32[]{:S(2)}, u32[]{:S(2)}) collective-permute-start(bf16[128,256]{1,0:T(8,128)(2,1)S(1)} %sort_far.1), channel_id=1, source_target_pairs={{8,0},{9,1},{10,2},{11,3},{12,4},{13,5},{14,6},{15,7},{0,8},{1,9},... | collective-permute-start | bytes 196616 | tf_op jit(solution)/shard_map/ppermute | solution.py:56
  41.9 5.7 %collective-permute-start.19 = (bf16[128,256]{1,0:T(8,128)(2,1)S(1)}, bf16[128,256]{1,0:T(8,128)(2,1)S(1)}, u32[]{:S(2)}, u32[]{:S(2)}) collective-permute-start(bf16[128,256]{1,0:T(8,128)(2,1)S(1)} %get-tuple-element.39), channel_id=1, source_target_pairs={{0,16},{16,0},{1,17},{17,1},{2,18},{18,2},{3,19},{19,3},{4,20},{20... | collective-permute-start | bytes 196616 | tf_op jit(solution)/shard_map/ppermute | solution.py:60
  43.3 5.9 %collective-permute-start.15 = (bf16[128,256]{1,0:T(8,128)(2,1)S(1)}, bf16[128,256]{1,0:T(8,128)(2,1)S(1)}, u32[]{:S(2)}, u32[]{:S(2)}) collective-permute-start(bf16[128,256]{1,0:T(8,128)(2,1)S(1)} %add_convert_fusion.2), channel_id=1, source_target_pairs={{0,8},{1,9},{2,10},{3,11},{4,12},{5,13},{6,14},{7,15},{8,0},{9,1},... | collective-permute-start | bytes 196616 | tf_op jit(solution)/shard_map/ppermute | solution.py:64
  49.2 1.3 %collective-permute-start.22 = (bf16[128,256]{1,0:T(8,128)(2,1)S(1)}, bf16[128,256]{1,0:T(8,128)(2,1)S(1)}, u32[]{:S(2)}, u32[]{:S(2)}) collective-permute-start(bf16[128,256]{1,0:T(8,128)(2,1)S(1)} %add_convert_fusion.1), channel_id=1, source_target_pairs={{0,1},{1,0},{2,3},{3,2},{4,5},{5,4},{6,7},{7,6},{8,9},{9,8},{10,11... | collective-permute-start | bytes 196616 | tf_op jit(solution)/shard_map/ppermute | solution.py:64

commit v7 on v6

--- a/solution.py
+++ b/solution.py
@@ -440,12 +440,26 @@
     )(own_a, sib_a, own_sent, sib_sent, grad)
 
 
+def whole_kernel(scale, mine, theirs, out):
+    half = mine.shape[0]
+    core = lax.axis_index("blk") % 2
+    here = pl.multiple_of(core * half, half)
+    there = pl.multiple_of((1 - core) * half, half)
+    out[pl.ds(here, half), :] = mine[...].astype(jnp.float32) * scale
+    out[pl.ds(there, half), :] = theirs[...].astype(jnp.float32) * scale
+
+
+def whole_grad(mine, theirs, scale):
+    half, width = mine.shape
+    out = like((2 * half, width), jnp.float32)
+    return local_call(functools.partial(whole_kernel, scale), "whole_grad", out, mine, theirs)
+
+
 def on_device(features, weight, cotangent, tile_row, tile_col, tile_count, tile_vals):
     size, width = features.shape
     groups = lax.axis_size("rep")
     panels = lax.axis_size("blk")
     span = groups * size
-    core = lax.axis_index("blk") % 2
     plan = (Halves if Halves.fits(groups, panels) else Direct)(groups, panels)
     slots = sum(len(batch) for batch in plan.batches)
 
@@ -473,9 +487,8 @@
     parts = backward_product(own_a, sib_a, sent, along(sent, 1), grad, pieces)
     feature_grad, grad = plan.scatter(parts, size)
     mate = along(grad, 1)
-    weight_grad = jnp.where(
-        core == 0, jnp.concatenate([grad, mate]), jnp.concatenate([mate, grad])
-    ).astype(jnp.float32) * (1.0 / math.sqrt(size * groups * panels))
+    scale = 1.0 / math.sqrt(size * groups * panels)
+    weight_grad = whole_grad(grad, mate, scale)
     return activations, weight_grad, feature_grad.astype(jnp.bfloat16)
 
 

time: 51.5 us -> 51.2 us (level)
  Pallas kernels: 4.05 us -> 4.92 us
  other arithmetic: 1.54 us -> 0.8 us
    pallas_call x3 -> x4, Pallas kernels: 0.1 us -> 0.83 us  [local_call(): pl.pallas_call(kernel, out_shape=outs, compiler_params=pltpu.CompilerPara...]
    mul x1 -> x0, other arithmetic: 0.73 us -> none  [on_device(): jnp.where(core == 0, jnp.concatenate([grad, mate]), jnp.concatenate([mate...]
where the time goes in v7:
time: 51.2 us; the launch traced here: 51.4 us
  starting transfers between devices  25.4 us (50%)
  waiting for transfers between devices  18.2 us (36%)
  Pallas kernels  4.92 us (10%)
  local copies, waits for them, and re-layouts  1.24 us (2%)
  between operations  0.82 us (2%)
  other arithmetic  0.8 us (2%)
    ppermute x8, starting transfers between devices, move(): return lax.ppermute(array, BOTH, pairs)  13.4 us
    ppermute x6, waiting for transfers between devices, across(): return lax.ppermute(array, 'rep', xor_pairs(lax.axis_size('rep'), bit))  6.9 us
    ppermute x8, waiting for transfers between devices, move(): return lax.ppermute(array, BOTH, pairs)  6.34 us
    ppermute x6, starting transfers between devices, across(): return lax.ppermute(array, 'rep', xor_pairs(lax.axis_size('rep'), bit))  6.26 us
    ppermute x9, starting transfers between devices, along(): return lax.ppermute(array, 'blk', xor_pairs(lax.axis_size('blk'), bit))  5.7 us
    ppermute x9, waiting for transfers between devices, along(): return lax.ppermute(array, 'blk', xor_pairs(lax.axis_size('blk'), bit))  4.96 us
    pallas_call x1, Pallas kernels, place_tiles(): pl.pallas_call(functools.partial(place_kernel, plan, lax.axis_size('rep')...  1.36 us
    unnamed x8, local copies, waits for them, and re-layouts  1.24 us
  transfers between devices with their start and end apart: 23, of which 9 were waited for; matrix products, arithmetic and copies ran while one was open for 1% of the time, Pallas kernels for 5%

profile of v7, /device:TPU:0, one launch (start us, length us, event | category | flops | bytes accessed | tf_op | source)
XLA Modules:
  0.0 51.4 jit_solution(11566567302616906883)
XLA Ops:
  0.6 0.0 copy-start.1
  0.6 0.5 %collective-permute-start.1 = (bf16[8,4,128,128]{3,2,1,0:T(8,128)(2,1)}, bf16[8,4,128,128]{3,2,1,0:T(8,128)(2,1)S(1)}, u32[]{:S(2)}, u32[]{:S(2)}) collective-permute-start(bf16[8,4,128,128]{3,2,1,0:T(8,128)(2,1)} %bitcast.8), channel_id=1, source_target_pairs={{0,1},{1,0},{2,3},{3,2},{4,5},{5,4},{6,7},{7,6},{8,9},{9,8},{10,11... | collective-permute-start | bytes 3145736 | tf_op jit(solution)/shard_map/ppermute | solution.py:64
  1.2 3.7 %collective-permute-start.5 = (bf16[128,256]{1,0:T(8,128)(2,1)}, bf16[128,256]{1,0:T(8,128)(2,1)S(1)}, u32[]{:S(2)}, u32[]{:S(2)}) collective-permute-start(bf16[128,256]{1,0:T(8,128)(2,1)} %first.1), channel_id=1, source_target_pairs={{0,8},{1,9},{2,10},{3,11},{4,12},{5,13},{6,14},{7,15},{8,0},{9,1},... | collective-permute-start | bytes 196616 | tf_op jit(solution)/shard_map/ppermute | solution.py:56
  4.8 1.5 %collective-permute-start.2 = (bf16[128,256]{1,0:T(8,128)(2,1)}, bf16[128,256]{1,0:T(8,128)(2,1)S(1)}, u32[]{:S(2)}, u32[]{:S(2)}) collective-permute-start(bf16[128,256]{1,0:T(8,128)(2,1)} %first.1), channel_id=1, source_target_pairs={{0,16},{16,0},{1,17},{17,1},{2,18},{18,2},{3,19},{19,3},{4,20},{20... | collective-permute-start | bytes 196616 | tf_op jit(solution)/shard_map/ppermute | solution.py:60
  6.3 0.5 %collective-permute-start.6 = (bf16[128,256]{1,0:T(8,128)(2,1)}, bf16[128,256]{1,0:T(8,128)(2,1)S(1)}, u32[]{:S(2)}, u32[]{:S(2)}) collective-permute-start(bf16[128,256]{1,0:T(8,128)(2,1)} %refs_0_.1), channel_id=1, source_target_pairs={{0,16},{16,0},{1,17},{17,1},{2,18},{18,2},{3,19},{19,3},{4,20},{20... | collective-permute-start | bytes 196616 | tf_op jit(solution)/shard_map/ppermute | solution.py:60
  6.9 0.7 %pad_add_fusion.refs_0_ = s32[9,8]{1,0:T(8,128)S(1)} fusion(s32[1,8]{1,0:T(1,128)} %bitcast.12, s32[4,8]{1,0:T(4,128)} %bitcast.10, s32[4,8]{1,0:T(4,128)} %bitcast.11), kind=kLoop, calls=%fused_computation.5 | loop fusion | flops 144 | bytes 576 | tf_op jit(solution)/shard_map/concatenate | solution.py:467
  7.6 0.0 collective-permute-start
  7.6 2.1 %collective-permute-done.2.second = bf16[128,256]{1,0:T(8,128)(2,1)S(1)} collective-permute-done((bf16[128,256]{1,0:T(8,128)(2,1)}, bf16[128,256]{1,0:T(8,128)(2,1)S(1)}, u32[]{:S(2)}, u32[]{:S(2)}) %collective-permute-start.2) | collective-permute-done | bytes 65568 | tf_op jit(solution)/shard_map/ppermute | solution.py:60
  9.7 0.0 copy-done.1
  9.7 1.6 %collective-permute-start.3 = (bf16[256,256]{1,0:T(8,128)(2,1)S(1)}, bf16[256,256]{1,0:T(8,128)(2,1)S(1)}, u32[]{:S(2)}, u32[]{:S(2)}) collective-permute-start(bf16[256,256]{1,0:T(8,128)(2,1)S(1)} %stack.1.refs_0_), channel_id=1, source_target_pairs={{0,4},{1,5},{2,6},{3,7},{4,8},{5,9},{6,10},{7,11},{8,12},{9,13},{1... | collective-permute-start | bytes 393224 | tf_op jit(solution)/shard_map/ppermute | solution.py:56
  11.3 0.0 collective-permute-done.refs_2_
  11.3 1.0 %collective-permute-start.4 = (bf16[256,256]{1,0:T(8,128)(2,1)S(1)}, bf16[256,256]{1,0:T(8,128)(2,1)S(1)}, u32[]{:S(2)}, u32[]{:S(2)}) collective-permute-start(bf16[256,256]{1,0:T(8,128)(2,1)S(1)} %stack.1.refs_0_), channel_id=1, source_target_pairs={{0,6},{1,7},{2,4},{3,5},{4,10},{5,11},{6,8},{7,9},{8,14},{9,15},{1... | collective-permute-start | bytes 393224 | tf_op jit(solution)/shard_map/ppermute | solution.py:56
  12.4 0.0 collective-permute-done.6.refs_1_
  12.4 0.0 collective-permute-done.5.refs_2_
  12.4 0.0 collective-permute-done.1.refs_3_
  12.4 0.6 %collective-permute-start.8 = (bf16[128,256]{1,0:T(8,128)(2,1)S(1)}, bf16[128,256]{1,0:T(8,128)(2,1)S(1)}, u32[]{:S(2)}, u32[]{:S(2)}) collective-permute-start(bf16[128,256]{1,0:T(8,128)(2,1)S(1)} %get-tuple-element.44), channel_id=1, source_target_pairs={{0,2},{1,3},{2,0},{3,1},{4,6},{5,7},{6,4},{7,5},{8,10},{9,11},{10,... | collective-permute-start | bytes 196616 | tf_op jit(solution)/shard_map/ppermute | solution.py:64
  13.0 2.8 %collective-permute-start.9 = (bf16[128,256]{1,0:T(8,128)(2,1)S(1)}, bf16[128,256]{1,0:T(8,128)(2,1)S(1)}, u32[]{:S(2)}, u32[]{:S(2)}) collective-permute-start(bf16[128,256]{1,0:T(8,128)(2,1)S(1)} %get-tuple-element.43), channel_id=1, source_target_pairs={{0,18},{1,19},{2,16},{3,17},{4,22},{5,23},{6,20},{7,21},{8,26},{9,... | collective-permute-start | bytes 196616 | tf_op jit(solution)/shard_map/ppermute | solution.py:56
  15.8 0.2 collective-permute-start.7
  16.0 0.0 copy-start
  16.0 1.2 %copy-done = bf16[1,1,8,4,128,128]{5,4,3,2,1,0:T(8,128)(2,1)S(1)} copy-done((bf16[1,1,8,4,128,128]{5,4,3,2,1,0:T(8,128)(2,1)S(1)}, bf16[1,1,8,4,128,128]{5,4,3,2,1,0:T(8,128)(2,1)}, u32[]{:S(2)}) %copy-start) | copy-done | bytes 1048600
  17.2 1.4 %place_tiles.1 = (bf16[5,256,256]{2,1,0:T(8,128)(2,1)S(1)}, bf16[5,256,256]{2,1,0:T(8,128)(2,1)S(1)}) custom-call(s32[9,8]{1,0:T(8,128)S(1)} %pad_add_fusion.refs_0_, bf16[8,4,128,128]{3,2,1,0:T(8,128)(2,1)S(1)} %bitcast.9, s32[9,8]{1,0:T(8,128)S(1)} %collective-permute-done.refs_2_, bf16[8,4,128,128]{3,2,1,0:T(8,128)(2,1)S(1)} %collective-permute-done.1.refs_3_), custom_call_target="tpu_custom_call" | custom-call | bytes 2621440 | tf_op jit(solution)/shard_map/place_tiles/pallas_call | solution.py:295
  18.6 0.0 collective-permute-done.3.refs_1_
  18.6 1.1 %collective-permute-done.4.refs_2_ = bf16[256,256]{1,0:T(8,128)(2,1)S(1)} collective-permute-done((bf16[256,256]{1,0:T(8,128)(2,1)S(1)}, bf16[256,256]{1,0:T(8,128)(2,1)S(1)}, u32[]{:S(2)}, u32[]{:S(2)}) %collective-permute-start.4) | collective-permute-done | bytes 131104 | tf_op jit(solution)/shard_map/ppermute | solution.py:56
  19.7 0.4 forward_product.2
  20.1 0.0 collective-permute-done.8.refs_4_
  20.1 0.0 collective-permute-done.9.refs_5_
  20.1 0.0 collective-permute-done.7.refs_3_
  20.1 0.3 forward_product.3
  20.4 0.1 collective-permute-start.10
  20.5 1.3 %collective-permute-done.10 = bf16[256,256]{1,0:T(8,128)(2,1)S(1)} collective-permute-done((bf16[256,256]{1,0:T(8,128)(2,1)S(1)}, bf16[256,256]{1,0:T(8,128)(2,1)S(1)}, u32[]{:S(2)}, u32[]{:S(2)}) %collective-permute-start.10) | collective-permute-done | bytes 131104 | tf_op jit(solution)/shard_map/ppermute | solution.py:64
  21.8 0.0 copy-start.2
  21.8 0.0 copy-start.3
  21.9 0.8 %collective-permute-start.11 = (bf16[256,256]{1,0:T(8,128)(2,1)S(1)}, bf16[256,256]{1,0:T(8,128)(2,1)S(1)}, u32[]{:S(2)}, u32[]{:S(2)}) collective-permute-start(bf16[256,256]{1,0:T(8,128)(2,1)S(1)} %add_convert_fusion.first), channel_id=1, source_target_pairs={{0,16},{16,0},{1,17},{17,1},{2,18},{18,2},{3,19},{19,3},{4,20},{20... | collective-permute-start | bytes 393224 | tf_op jit(solution)/shard_map/ppermute | solution.py:60
  22.7 4.8 %collective-permute-done.11.second = bf16[256,256]{1,0:T(8,128)(2,1)S(1)} collective-permute-done((bf16[256,256]{1,0:T(8,128)(2,1)S(1)}, bf16[256,256]{1,0:T(8,128)(2,1)S(1)}, u32[]{:S(2)}, u32[]{:S(2)}) %collective-permute-start.11) | collective-permute-done | bytes 131104 | tf_op jit(solution)/shard_map/ppermute | solution.py:60
  27.5 0.0 copy-done.2
  27.5 0.0 copy-done.3
  27.5 0.8 %layer.1 = (bf16[128,256]{1,0:T(8,128)(2,1)}, f32[128,256]{1,0:T(8,128)S(1)}, bf16[384,256]{1,0:T(8,128)(2,1)S(1)}) custom-call(bf16[256,256]{1,0:T(8,128)(2,1)S(1)} %add_convert_fusion.first, bf16[256,256]{1,0:T(8,128)(2,1)S(1)} %collective-permute-done.11.second, bf16[256,256]{1,0:T(8,128)(2,1)S(1)} %copy-done.2, bf16[128,256]{1,0:T(8,128)(2,1)S(1)} %copy-done.3, ...), custom_call_target="tpu_custom_call" | custom-call | flops 100663296 | bytes 524288 | tf_op jit(solution)/shard_map/layer/pallas_call | solution.py:386
  28.3 0.0 collective-permute-start.12
  28.3 1.4 %collective-permute-done.12.sib_sent = bf16[384,256]{1,0:T(8,128)(2,1)S(1)} collective-permute-done((bf16[384,256]{1,0:T(8,128)(2,1)S(1)}, bf16[384,256]{1,0:T(8,128)(2,1)S(1)}, u32[]{:S(2)}, u32[]{:S(2)}) %collective-permute-start.12) | collective-permute-done | bytes 196640 | tf_op jit(solution)/shard_map/ppermute | solution.py:64
  29.8 0.5 %backward_product.1 = (f32[256,256]{1,0:T(8,128)S(1)}, f32[128,256]{1,0:T(8,128)S(1)}, bf16[128,256]{1,0:T(8,128)(2,1)S(1)}, bf16[256,256]{1,0:T(8,128)(2,1)S(1)...) custom-call(bf16[5,256,256]{2,1,0:T(8,128)(2,1)S(1)} %get-tuple-element.23.own_a, ...), custom_call_target="tpu_custom_call" | custom-call | flops 335544320 | bytes 1310720 | tf_op jit(solution)/shard_map/backward_product/pallas_call | solution.py:425
  30.3 1.6 %collective-permute-start.13 = (bf16[256,256]{1,0:T(8,128)(2,1)S(1)}, bf16[256,256]{1,0:T(8,128)(2,1)S(1)}, u32[]{:S(2)}, u32[]{:S(2)}) collective-permute-start(bf16[256,256]{1,0:T(8,128)(2,1)S(1)} %get-tuple-element.33.first), channel_id=1, source_target_pairs={{0,2},{1,3},{2,0},{3,1},{4,6},{5,7},{6,4},{7,5},{8,10},{9,11},{10,... | collective-permute-start | bytes 393224 | tf_op jit(solution)/shard_map/ppermute | solution.py:64
  31.9 1.8 %collective-permute-start.17 = (bf16[256,256]{1,0:T(8,128)(2,1)S(1)}, bf16[256,256]{1,0:T(8,128)(2,1)S(1)}, u32[]{:S(2)}, u32[]{:S(2)}) collective-permute-start(bf16[256,256]{1,0:T(8,128)(2,1)S(1)} %get-tuple-element.36), channel_id=1, source_target_pairs={{4,0},{5,1},{6,2},{7,3},{8,4},{9,5},{10,6},{11,7},{12,8},{13,9},{1... | collective-permute-start | bytes 393224 | tf_op jit(solution)/shard_map/ppermute | solution.py:56
  33.7 1.3 %collective-permute-start.18 = (bf16[256,256]{1,0:T(8,128)(2,1)S(1)}, bf16[256,256]{1,0:T(8,128)(2,1)S(1)}, u32[]{:S(2)}, u32[]{:S(2)}) collective-permute-start(bf16[256,256]{1,0:T(8,128)(2,1)S(1)} %get-tuple-element.37), channel_id=1, source_target_pairs={{6,0},{7,1},{4,2},{5,3},{10,4},{11,5},{8,6},{9,7},{14,8},{15,9},{1... | collective-permute-start | bytes 393224 | tf_op jit(solution)/shard_map/ppermute | solution.py:56
  35.0 0.3 collective-permute-start.16
  35.2 1.9 %collective-permute-start.20 = (bf16[128,256]{1,0:T(8,128)(2,1)S(1)}, bf16[128,256]{1,0:T(8,128)(2,1)S(1)}, u32[]{:S(2)}, u32[]{:S(2)}) collective-permute-start(bf16[128,256]{1,0:T(8,128)(2,1)S(1)} %get-tuple-element.41), channel_id=1, source_target_pairs={{0,16},{16,0},{1,17},{17,1},{2,18},{18,2},{3,19},{19,3},{4,20},{20... | collective-permute-start | bytes 196616 | tf_op jit(solution)/shard_map/ppermute | solution.py:60
  37.1 0.0 collective-permute-done.13.second.came
  37.1 1.6 %collective-permute-start.14 = (bf16[128,256]{1,0:T(8,128)(2,1)S(1)}, bf16[128,256]{1,0:T(8,128)(2,1)S(1)}, u32[]{:S(2)}, u32[]{:S(2)}) collective-permute-start(bf16[128,256]{1,0:T(8,128)(2,1)S(1)} %add_tails.1), channel_id=1, source_target_pairs={{0,4},{1,5},{2,6},{3,7},{4,0},{5,1},{6,2},{7,3},{8,12},{9,13},{10,... | collective-permute-start | bytes 196616 | tf_op jit(solution)/shard_map/ppermute | solution.py:64
  38.7 2.1 %collective-permute-done.16.corner = bf16[128,256]{1,0:T(8,128)(2,1)S(1)} collective-permute-done((bf16[128,256]{1,0:T(8,128)(2,1)S(1)}, bf16[128,256]{1,0:T(8,128)(2,1)S(1)}, u32[]{:S(2)}, u32[]{:S(2)}) %collective-permute-start.16) | collective-permute-done | bytes 65568 | tf_op jit(solution)/shard_map/ppermute | solution.py:56
  40.8 0.0 collective-permute-done.20.far_mate
  40.9 1.0 %collective-permute-start.21 = (bf16[128,256]{1,0:T(8,128)(2,1)S(1)}, bf16[128,256]{1,0:T(8,128)(2,1)S(1)}, u32[]{:S(2)}, u32[]{:S(2)}) collective-permute-start(bf16[128,256]{1,0:T(8,128)(2,1)S(1)} %sort_far.1), channel_id=1, source_target_pairs={{8,0},{9,1},{10,2},{11,3},{12,4},{13,5},{14,6},{15,7},{0,8},{1,9},... | collective-permute-start | bytes 196616 | tf_op jit(solution)/shard_map/ppermute | solution.py:56
  41.8 0.0 collective-permute-done.17.ahead
  41.8 0.0 collective-permute-done.18.cross
  41.9 0.1 add_column.1
  41.9 1.4 %collective-permute-start.19 = (bf16[128,256]{1,0:T(8,128)(2,1)S(1)}, bf16[128,256]{1,0:T(8,128)(2,1)S(1)}, u32[]{:S(2)}, u32[]{:S(2)}) collective-permute-start(bf16[128,256]{1,0:T(8,128)(2,1)S(1)} %get-tuple-element.39), channel_id=1, source_target_pairs={{0,16},{16,0},{1,17},{17,1},{2,18},{18,2},{3,19},{19,3},{4,20},{20... | collective-permute-start | bytes 196616 | tf_op jit(solution)/shard_map/ppermute | solution.py:60
  43.3 0.0 collective-permute-done.14
  43.3 1.2 %collective-permute-start.15 = (bf16[128,256]{1,0:T(8,128)(2,1)S(1)}, bf16[128,256]{1,0:T(8,128)(2,1)S(1)}, u32[]{:S(2)}, u32[]{:S(2)}) collective-permute-start(bf16[128,256]{1,0:T(8,128)(2,1)S(1)} %add_convert_fusion.2), channel_id=1, source_target_pairs={{0,8},{1,9},{2,10},{3,11},{4,12},{5,13},{6,14},{7,15},{8,0},{9,1},... | collective-permute-start | bytes 196616 | tf_op jit(solution)/shard_map/ppermute | solution.py:64
  44.6 3.1 %collective-permute-done.21.third = bf16[128,256]{1,0:T(8,128)(2,1)S(1)} collective-permute-done((bf16[128,256]{1,0:T(8,128)(2,1)S(1)}, bf16[128,256]{1,0:T(8,128)(2,1)S(1)}, u32[]{:S(2)}, u32[]{:S(2)}) %collective-permute-start.21) | collective-permute-done | bytes 65568 | tf_op jit(solution)/shard_map/ppermute | solution.py:56
  47.7 0.0 collective-permute-done.19.second
  47.7 0.7 %finish.1 = bf16[128,256]{1,0:T(8,128)(2,1)} custom-call(f32[128,256]{1,0:T(8,128)S(1)} %get-tuple-element.38.first, bf16[128,256]{1,0:T(8,128)(2,1)S(1)} %collective-permute-done.19.second, bf16[128,256]{1,0:T(8,128)(2,1)S(1)} %collective-permute-done.21.third), custom_call_target="tpu_custom_call" | custom-call | flops 65536 | bytes 262144 | tf_op jit(solution)/shard_map/finish/pallas_call | solution.py:172
  48.3 0.9 %collective-permute-done.15 = bf16[128,256]{1,0:T(8,128)(2,1)S(1)} collective-permute-done((bf16[128,256]{1,0:T(8,128)(2,1)S(1)}, bf16[128,256]{1,0:T(8,128)(2,1)S(1)}, u32[]{:S(2)}, u32[]{:S(2)}) %collective-permute-start.15) | collective-permute-done | bytes 65568 | tf_op jit(solution)/shard_map/ppermute | solution.py:64
  49.3 0.1 collective-permute-start.22
  49.4 1.2 %collective-permute-done.22.theirs = bf16[128,256]{1,0:T(8,128)(2,1)S(1)} collective-permute-done((bf16[128,256]{1,0:T(8,128)(2,1)S(1)}, bf16[128,256]{1,0:T(8,128)(2,1)S(1)}, u32[]{:S(2)}, u32[]{:S(2)}) %collective-permute-start.22) | collective-permute-done | bytes 65568 | tf_op jit(solution)/shard_map/ppermute | solution.py:64
  50.6 0.7 %whole_grad.1 = f32[256,256]{1,0:T(8,128)} custom-call(bf16[128,256]{1,0:T(8,128)(2,1)S(1)} %add_convert_fusion.1.mine, bf16[128,256]{1,0:T(8,128)(2,1)S(1)} %collective-permute-done.22.theirs), custom_call_target="tpu_custom_call" | custom-call | flops 131072 | bytes 131072 | tf_op jit(solution)/shard_map/whole_grad/pallas_call | solution.py:134
  (7 shorter events, 0.1 us)
Async XLA Ops:
  0.6 9.1 %copy-start.1 = (bf16[128,256]{1,0:T(8,128)(2,1)S(1)}, bf16[128,256]{1,0:T(8,128)(2,1)}, u32[]{:S(2)}) copy-start(bf16[128,256]{1,0:T(8,128)(2,1)} %first.1) | copy-start | bytes 196612
  0.6 11.7 %collective-permute-start.1 = (bf16[8,4,128,128]{3,2,1,0:T(8,128)(2,1)}, bf16[8,4,128,128]{3,2,1,0:T(8,128)(2,1)S(1)}, u32[]{:S(2)}, u32[]{:S(2)}) collective-permute-start(bf16[8,4,128,128]{3,2,1,0:T(8,128)(2,1)} %bitcast.8), channel_id=1, source_target_pairs={{0,1},{1,0},{2,3},{3,2},{4,5},{5,4},{6,7},{7,6},{8,9},{9,8},{10,11... | collective-permute-start | bytes 3145736 | tf_op jit(solution)/shard_map/ppermute | solution.py:64
  1.2 11.2 %collective-permute-start.5 = (bf16[128,256]{1,0:T(8,128)(2,1)}, bf16[128,256]{1,0:T(8,128)(2,1)S(1)}, u32[]{:S(2)}, u32[]{:S(2)}) collective-permute-start(bf16[128,256]{1,0:T(8,128)(2,1)} %first.1), channel_id=1, source_target_pairs={{0,8},{1,9},{2,10},{3,11},{4,12},{5,13},{6,14},{7,15},{8,0},{9,1},... | collective-permute-start | bytes 196616 | tf_op jit(solution)/shard_map/ppermute | solution.py:56
  4.8 4.9 %collective-permute-start.2 = (bf16[128,256]{1,0:T(8,128)(2,1)}, bf16[128,256]{1,0:T(8,128)(2,1)S(1)}, u32[]{:S(2)}, u32[]{:S(2)}) collective-permute-start(bf16[128,256]{1,0:T(8,128)(2,1)} %first.1), channel_id=1, source_target_pairs={{0,16},{16,0},{1,17},{17,1},{2,18},{18,2},{3,19},{19,3},{4,20},{20... | collective-permute-start | bytes 196616 | tf_op jit(solution)/shard_map/ppermute | solution.py:60
  6.3 6.0 %collective-permute-start.6 = (bf16[128,256]{1,0:T(8,128)(2,1)}, bf16[128,256]{1,0:T(8,128)(2,1)S(1)}, u32[]{:S(2)}, u32[]{:S(2)}) collective-permute-start(bf16[128,256]{1,0:T(8,128)(2,1)} %refs_0_.1), channel_id=1, source_target_pairs={{0,16},{16,0},{1,17},{17,1},{2,18},{18,2},{3,19},{19,3},{4,20},{20... | collective-permute-start | bytes 196616 | tf_op jit(solution)/shard_map/ppermute | solution.py:60
  7.6 3.8 %collective-permute-start = (s32[9,8]{1,0:T(8,128)S(1)}, s32[9,8]{1,0:T(8,128)S(1)}, u32[]{:S(2)}, u32[]{:S(2)}) collective-permute-start(s32[9,8]{1,0:T(8,128)S(1)} %pad_add_fusion.refs_0_), channel_id=1, source_target_pairs={{0,1},{1,0},{2,3},{3,2},{4,5},{5,4},{6,7},{7,6},{8,9},{9,8},{10,11... | collective-permute-start | bytes 872 | tf_op jit(solution)/shard_map/ppermute | solution.py:64
  9.7 8.9 %collective-permute-start.3 = (bf16[256,256]{1,0:T(8,128)(2,1)S(1)}, bf16[256,256]{1,0:T(8,128)(2,1)S(1)}, u32[]{:S(2)}, u32[]{:S(2)}) collective-permute-start(bf16[256,256]{1,0:T(8,128)(2,1)S(1)} %stack.1.refs_0_), channel_id=1, source_target_pairs={{0,4},{1,5},{2,6},{3,7},{4,8},{5,9},{6,10},{7,11},{8,12},{9,13},{1... | collective-permute-start | bytes 393224 | tf_op jit(solution)/shard_map/ppermute | solution.py:56
  11.3 8.4 %collective-permute-start.4 = (bf16[256,256]{1,0:T(8,128)(2,1)S(1)}, bf16[256,256]{1,0:T(8,128)(2,1)S(1)}, u32[]{:S(2)}, u32[]{:S(2)}) collective-permute-start(bf16[256,256]{1,0:T(8,128)(2,1)S(1)} %stack.1.refs_0_), channel_id=1, source_target_pairs={{0,6},{1,7},{2,4},{3,5},{4,10},{5,11},{6,8},{7,9},{8,14},{9,15},{1... | collective-permute-start | bytes 393224 | tf_op jit(solution)/shard_map/ppermute | solution.py:56
  12.4 7.7 %collective-permute-start.8 = (bf16[128,256]{1,0:T(8,128)(2,1)S(1)}, bf16[128,256]{1,0:T(8,128)(2,1)S(1)}, u32[]{:S(2)}, u32[]{:S(2)}) collective-permute-start(bf16[128,256]{1,0:T(8,128)(2,1)S(1)} %get-tuple-element.44), channel_id=1, source_target_pairs={{0,2},{1,3},{2,0},{3,1},{4,6},{5,7},{6,4},{7,5},{8,10},{9,11},{10,... | collective-permute-start | bytes 196616 | tf_op jit(solution)/shard_map/ppermute | solution.py:64
  13.0 7.1 %collective-permute-start.9 = (bf16[128,256]{1,0:T(8,128)(2,1)S(1)}, bf16[128,256]{1,0:T(8,128)(2,1)S(1)}, u32[]{:S(2)}, u32[]{:S(2)}) collective-permute-start(bf16[128,256]{1,0:T(8,128)(2,1)S(1)} %get-tuple-element.43), channel_id=1, source_target_pairs={{0,18},{1,19},{2,16},{3,17},{4,22},{5,23},{6,20},{7,21},{8,26},{9,... | collective-permute-start | bytes 196616 | tf_op jit(solution)/shard_map/ppermute | solution.py:56
  15.8 4.3 %collective-permute-start.7 = (bf16[128,256]{1,0:T(8,128)(2,1)S(1)}, bf16[128,256]{1,0:T(8,128)(2,1)S(1)}, u32[]{:S(2)}, u32[]{:S(2)}) collective-permute-start(bf16[128,256]{1,0:T(8,128)(2,1)S(1)} %collective-permute-done.5.refs_2_), channel_id=1, source_target_pairs={{0,16},{16,0},{1,17},{17,1},{2,18},{18,2},{3,19},{19,3},{4,20},{20... | collective-permute-start | bytes 196616 | tf_op jit(solution)/shard_map/ppermute | solution.py:60
  16.0 1.2 %copy-start = (bf16[1,1,8,4,128,128]{5,4,3,2,1,0:T(8,128)(2,1)S(1)}, bf16[1,1,8,4,128,128]{5,4,3,2,1,0:T(8,128)(2,1)}, u32[]{:S(2)}) copy-start(bf16[1,1,8,4,128,128]{5,4,3,2,1,0:T(8,128)(2,1)} %param.13) | copy-start | bytes 3145732
  20.4 1.4 %collective-permute-start.10 = (bf16[256,256]{1,0:T(8,128)(2,1)S(1)}, bf16[256,256]{1,0:T(8,128)(2,1)S(1)}, u32[]{:S(2)}, u32[]{:S(2)}) collective-permute-start(bf16[256,256]{1,0:T(8,128)(2,1)S(1)} %get-tuple-element.29), channel_id=1, source_target_pairs={{0,1},{1,0},{2,3},{3,2},{4,5},{5,4},{6,7},{7,6},{8,9},{9,8},{10,11... | collective-permute-start | bytes 393224 | tf_op jit(solution)/shard_map/ppermute | solution.py:64
  21.8 5.7 %copy-start.2 = (bf16[256,256]{1,0:T(8,128)(2,1)S(1)}, bf16[256,256]{1,0:T(8,128)(2,1)}, u32[]{:S(2)}) copy-start(bf16[256,256]{1,0:T(8,128)(2,1)} %weight.1) | copy-start | bytes 393220
  21.8 5.7 %copy-start.3 = (bf16[128,256]{1,0:T(8,128)(2,1)S(1)}, bf16[128,256]{1,0:T(8,128)(2,1)}, u32[]{:S(2)}) copy-start(bf16[128,256]{1,0:T(8,128)(2,1)} %refs_0_.1) | copy-start | bytes 196612
  21.9 5.6 %collective-permute-start.11 = (bf16[256,256]{1,0:T(8,128)(2,1)S(1)}, bf16[256,256]{1,0:T(8,128)(2,1)S(1)}, u32[]{:S(2)}, u32[]{:S(2)}) collective-permute-start(bf16[256,256]{1,0:T(8,128)(2,1)S(1)} %add_convert_fusion.first), channel_id=1, source_target_pairs={{0,16},{16,0},{1,17},{17,1},{2,18},{18,2},{3,19},{19,3},{4,20},{20... | collective-permute-start | bytes 393224 | tf_op jit(solution)/shard_map/ppermute | solution.py:60
  28.3 1.4 %collective-permute-start.12 = (bf16[384,256]{1,0:T(8,128)(2,1)S(1)}, bf16[384,256]{1,0:T(8,128)(2,1)S(1)}, u32[]{:S(2)}, u32[]{:S(2)}) collective-permute-start(bf16[384,256]{1,0:T(8,128)(2,1)S(1)} %get-tuple-element.31.own_sent), channel_id=1, source_target_pairs={{0,1},{1,0},{2,3},{3,2},{4,5},{5,4},{6,7},{7,6},{8,9},{9,8},{10,11... | collective-permute-start | bytes 589832 | tf_op jit(solution)/shard_map/ppermute | solution.py:64
  30.3 6.8 %collective-permute-start.13 = (bf16[256,256]{1,0:T(8,128)(2,1)S(1)}, bf16[256,256]{1,0:T(8,128)(2,1)S(1)}, u32[]{:S(2)}, u32[]{:S(2)}) collective-permute-start(bf16[256,256]{1,0:T(8,128)(2,1)S(1)} %get-tuple-element.33.first), channel_id=1, source_target_pairs={{0,2},{1,3},{2,0},{3,1},{4,6},{5,7},{6,4},{7,5},{8,10},{9,11},{10,... | collective-permute-start | bytes 393224 | tf_op jit(solution)/shard_map/ppermute | solution.py:64
  31.9 9.9 %collective-permute-start.17 = (bf16[256,256]{1,0:T(8,128)(2,1)S(1)}, bf16[256,256]{1,0:T(8,128)(2,1)S(1)}, u32[]{:S(2)}, u32[]{:S(2)}) collective-permute-start(bf16[256,256]{1,0:T(8,128)(2,1)S(1)} %get-tuple-element.36), channel_id=1, source_target_pairs={{4,0},{5,1},{6,2},{7,3},{8,4},{9,5},{10,6},{11,7},{12,8},{13,9},{1... | collective-permute-start | bytes 393224 | tf_op jit(solution)/shard_map/ppermute | solution.py:56
  33.7 8.1 %collective-permute-start.18 = (bf16[256,256]{1,0:T(8,128)(2,1)S(1)}, bf16[256,256]{1,0:T(8,128)(2,1)S(1)}, u32[]{:S(2)}, u32[]{:S(2)}) collective-permute-start(bf16[256,256]{1,0:T(8,128)(2,1)S(1)} %get-tuple-element.37), channel_id=1, source_target_pairs={{6,0},{7,1},{4,2},{5,3},{10,4},{11,5},{8,6},{9,7},{14,8},{15,9},{1... | collective-permute-start | bytes 393224 | tf_op jit(solution)/shard_map/ppermute | solution.py:56
  35.0 5.9 %collective-permute-start.16 = (bf16[128,256]{1,0:T(8,128)(2,1)S(1)}, bf16[128,256]{1,0:T(8,128)(2,1)S(1)}, u32[]{:S(2)}, u32[]{:S(2)}) collective-permute-start(bf16[128,256]{1,0:T(8,128)(2,1)S(1)} %get-tuple-element.35), channel_id=1, source_target_pairs={{18,0},{19,1},{16,2},{17,3},{22,4},{23,5},{20,6},{21,7},{26,8},{27... | collective-permute-start | bytes 196616 | tf_op jit(solution)/shard_map/ppermute | solution.py:56
  35.2 5.6 %collective-permute-start.20 = (bf16[128,256]{1,0:T(8,128)(2,1)S(1)}, bf16[128,256]{1,0:T(8,128)(2,1)S(1)}, u32[]{:S(2)}, u32[]{:S(2)}) collective-permute-start(bf16[128,256]{1,0:T(8,128)(2,1)S(1)} %get-tuple-element.41), channel_id=1, source_target_pairs={{0,16},{16,0},{1,17},{17,1},{2,18},{18,2},{3,19},{19,3},{4,20},{20... | collective-permute-start | bytes 196616 | tf_op jit(solution)/shard_map/ppermute | solution.py:60
  37.1 6.2 %collective-permute-start.14 = (bf16[128,256]{1,0:T(8,128)(2,1)S(1)}, bf16[128,256]{1,0:T(8,128)(2,1)S(1)}, u32[]{:S(2)}, u32[]{:S(2)}) collective-permute-start(bf16[128,256]{1,0:T(8,128)(2,1)S(1)} %add_tails.1), channel_id=1, source_target_pairs={{0,4},{1,5},{2,6},{3,7},{4,0},{5,1},{6,2},{7,3},{8,12},{9,13},{10,... | collective-permute-start | bytes 196616 | tf_op jit(solution)/shard_map/ppermute | solution.py:64
  40.9 6.8 %collective-permute-start.21 = (bf16[128,256]{1,0:T(8,128)(2,1)S(1)}, bf16[128,256]{1,0:T(8,128)(2,1)S(1)}, u32[]{:S(2)}, u32[]{:S(2)}) collective-permute-start(bf16[128,256]{1,0:T(8,128)(2,1)S(1)} %sort_far.1), channel_id=1, source_target_pairs={{8,0},{9,1},{10,2},{11,3},{12,4},{13,5},{14,6},{15,7},{0,8},{1,9},... | collective-permute-start | bytes 196616 | tf_op jit(solution)/shard_map/ppermute | solution.py:56
  41.9 5.8 %collective-permute-start.19 = (bf16[128,256]{1,0:T(8,128)(2,1)S(1)}, bf16[128,256]{1,0:T(8,128)(2,1)S(1)}, u32[]{:S(2)}, u32[]{:S(2)}) collective-permute-start(bf16[128,256]{1,0:T(8,128)(2,1)S(1)} %get-tuple-element.39), channel_id=1, source_target_pairs={{0,16},{16,0},{1,17},{17,1},{2,18},{18,2},{3,19},{19,3},{4,20},{20... | collective-permute-start | bytes 196616 | tf_op jit(solution)/shard_map/ppermute | solution.py:60
  43.3 5.9 %collective-permute-start.15 = (bf16[128,256]{1,0:T(8,128)(2,1)S(1)}, bf16[128,256]{1,0:T(8,128)(2,1)S(1)}, u32[]{:S(2)}, u32[]{:S(2)}) collective-permute-start(bf16[128,256]{1,0:T(8,128)(2,1)S(1)} %add_convert_fusion.2), channel_id=1, source_target_pairs={{0,8},{1,9},{2,10},{3,11},{4,12},{5,13},{6,14},{7,15},{8,0},{9,1},... | collective-permute-start | bytes 196616 | tf_op jit(solution)/shard_map/ppermute | solution.py:64
  49.3 1.3 %collective-permute-start.22 = (bf16[128,256]{1,0:T(8,128)(2,1)S(1)}, bf16[128,256]{1,0:T(8,128)(2,1)S(1)}, u32[]{:S(2)}, u32[]{:S(2)}) collective-permute-start(bf16[128,256]{1,0:T(8,128)(2,1)S(1)} %add_convert_fusion.1.mine), channel_id=1, source_target_pairs={{0,1},{1,0},{2,3},{3,2},{4,5},{5,4},{6,7},{7,6},{8,9},{9,8},{10,11... | collective-permute-start | bytes 196616 | tf_op jit(solution)/shard_map/ppermute | solution.py:64
